TPU v7x, 32 devices: a whole 2x2x4 slice. The times are simulated.
32 devices in a mesh: img: 4 (over z), ori: 8 (over y, x, core).
Axes of the slice: x: 2, y: 2, z: 4, core: 2. Of those that a mesh axis runs over, the one named last changes fastest.
Arguments:
- images: bfloat16 [64, 16384], P(('img', 'ori')), may hold values from -8 to 8
- references: bfloat16 [128, 16384], P('ori'), may hold values from -6 to 6
- shifts: float32 [12, 2], replicated, may hold values from -3 to 3
- owners: int32 [16384, 1], P(('ori', 'img')), may hold values from 0 to 7; in each aligned block of 512 rows (0 to 511, 512 to 1023, ...) at most 256 rows name the same one
- slot_rows: int32 [16384], P(('ori', 'img')), may hold values from 0 to 255
- interpolation: float32 [4096, 128], P(('ori', 'img')), may hold values from -0.5 to 0.5
- regularizer: float32 [8192], P(('ori', 'img')), may hold values from 1 to 16
Outputs:
- volume: float32 [8192, 128], P(('ori', 'img'))
- resampled: float32 [128, 16384], P(('ori', 'img'))
Inputs may be any that keep to these rules, and one draw needn't show every extreme that they name: `owners`: among the 512 segments of one device (aligned blocks of rows), no owner is named more than 256 times, a bound that some block reaches.
All inputs are finite; a program needn't handle non-finite values.
Results may differ from a plain program's by a relative error of at most 0.014.
Values may be sent and summed in bfloat16 or wider, within the bound.
No kernel may reach another device: no remote copies, remote signals or barrier semaphores. Data moves between devices by JAX's collectives and lax.ppermute only.
A program may use at most 64 MiB of HBM per device.

v0:
```python
import math

import jax
import jax.numpy as jnp
from jax import lax
from jax.sharding import PartitionSpec as P

COEF = 16384
SEGLEN = 128
SHIFTS = 12
SEGS = 128


grid_width = 64
image_side = 128.0


def merged(shard, axis, combine):
    everything = jax.tree.map(lambda part: lax.all_gather(part, axis), shard)
    first = jax.tree.map(lambda part: part[0], everything)

    def step(k, so_far):
        return combine(so_far, jax.tree.map(lambda part: part[k], everything))

    return lax.fori_loop(1, lax.axis_size(axis), step, first)


def phase_tables(shifts):
    half_len = COEF // 2
    positions = jnp.arange(half_len, dtype=jnp.int32)
    freq_x = (positions % grid_width).astype(jnp.float32)
    freq_y = (positions // grid_width - half_len // grid_width // 2).astype(jnp.float32)
    angles = (
        2.0
        * math.pi
        / image_side
        * (shifts[:, 0:1] * freq_x[None, :] + shifts[:, 1:2] * freq_y[None, :])
    )
    return (jnp.cos(angles), jnp.sin(angles))


def one_rotation(real_part, imag_part, cosine_row, sine_row):
    rotated_re = real_part * cosine_row[None, :] - imag_part * sine_row[None, :]
    rotated_im = real_part * sine_row[None, :] + imag_part * cosine_row[None, :]
    return jnp.concatenate([rotated_re, rotated_im], axis=1).astype(jnp.bfloat16)


def backproject(weights_b, group_images, cosine_table, sine_table):
    half_len = COEF // 2
    orient_count = weights_b.shape[1]
    total_re = jnp.zeros((orient_count, half_len), jnp.float32)
    total_im = jnp.zeros((orient_count, half_len), jnp.float32)
    for shift_number in range(SHIFTS):
        summed = lax.dot_general(
            weights_b[:, :, shift_number],
            group_images,
            (((0,), (0,)), ((), ())),
            preferred_element_type=jnp.float32,
        )
        sum_re = summed[:, :half_len]
        sum_im = summed[:, half_len:]
        total_re = (
            total_re + sum_re * cosine_table[shift_number] + sum_im * sine_table[shift_number]
        )
        total_im = (
            total_im - sum_re * sine_table[shift_number] + sum_im * cosine_table[shift_number]
        )
    return jnp.concatenate([total_re, total_im], axis=1)


def combine_pair(first_pair, second_pair):
    peak_first, total_first = first_pair
    peak_second, total_second = second_pair
    joined = jnp.maximum(peak_first, peak_second)
    return (
        joined,
        total_first * jnp.exp(peak_first - joined) + total_second * jnp.exp(peak_second - joined),
    )


def shards(images, references, shifts, owners, slot_rows, interpolation, regularizer):
    cosine_table, sine_table = phase_tables(shifts)
    score_scale = 2.0 / math.sqrt(COEF)
    half_len = COEF // 2
    real_part = references[:, :half_len].astype(jnp.float32)
    imag_part = references[:, half_len:].astype(jnp.float32)
    group_images = lax.all_gather(images, "ori", axis=0, tiled=True)
    group_rows = group_images.shape[0]
    score_list = []
    for shift_number in range(SHIFTS):
        rotated = one_rotation(
            real_part, imag_part, cosine_table[shift_number], sine_table[shift_number]
        )
        score_list.append(
            lax.dot_general(
                group_images, rotated, (((1,), (1,)), ((), ())), preferred_element_type=jnp.float32
            )
        )
    scores = jnp.stack(score_list, axis=2).reshape(group_rows, -1) * score_scale
    local_peak = jnp.max(scores, axis=1)
    local_total = jnp.sum(jnp.exp(scores - local_peak[:, None]), axis=1)
    row_peak, row_total = merged((local_peak, local_total), "ori", combine_pair)
    exponent = jnp.exp(scores - row_peak[:, None])
    weights = exponent / row_total[:, None]
    orient_count = references.shape[0]
    weights3 = weights.reshape(group_rows, orient_count, SHIFTS)
    orient_mass = jnp.sum(weights3, axis=(0, 2))
    summed = backproject(weights3.astype(jnp.bfloat16), group_images, cosine_table, sine_table)
    sub_rows = orient_count // lax.axis_size("img")
    full_slices, full_mass = lax.psum((summed, orient_mass), "img")
    first_row = lax.axis_index("img") * sub_rows
    own_slices = lax.dynamic_slice_in_dim(full_slices, first_row, sub_rows, 0)
    own_mass = lax.dynamic_slice_in_dim(full_mass, first_row, sub_rows, 0)
    ori_count = lax.axis_size("ori")
    segments = own_slices.reshape(-1, SEGLEN)
    seg_count = segments.shape[0]
    seg_mass = jnp.repeat(own_mass, SEGS)
    capacity = max(2, 4 * seg_count // ori_count)
    dest_owner = owners[:, 0]
    onehot = (dest_owner[:, None] == jnp.arange(ori_count, dtype=jnp.int32)[None, :]).astype(
        jnp.int32
    )
    slot_rank = jnp.sum(jnp.cumsum(onehot, axis=0) * onehot, axis=1) - 1
    slot_index = dest_owner * capacity + slot_rank
    send_values = (
        jnp.zeros((ori_count * capacity, SEGLEN), jnp.float32).at[slot_index].set(segments)
    )
    send_mass = jnp.zeros((ori_count * capacity,), jnp.float32).at[slot_index].set(seg_mass)
    send_rows = (
        jnp.zeros((ori_count * capacity,), jnp.float32)
        .at[slot_index]
        .set(slot_rows.astype(jnp.float32))
    )
    got_values, got_mass, got_rows = (
        lax.all_to_all(
            send_values.reshape(ori_count, capacity, SEGLEN),
            "ori",
            split_axis=0,
            concat_axis=0,
            tiled=True,
        ),
        lax.all_to_all(
            send_mass.reshape(ori_count, capacity), "ori", split_axis=0, concat_axis=0, tiled=True
        ),
        lax.all_to_all(
            send_rows.reshape(ori_count, capacity), "ori", split_axis=0, concat_axis=0, tiled=True
        ),
    )
    flat_values = got_values.reshape(-1, SEGLEN)
    flat_rows = got_rows.reshape(-1).astype(jnp.int32)
    row_count = regularizer.shape[0]
    inserted = jnp.zeros((row_count, SEGLEN), jnp.float32).at[flat_rows].add(flat_values)
    weight_sum = jnp.zeros((row_count,), jnp.float32).at[flat_rows].add(got_mass.reshape(-1))
    mapped = jnp.dot(
        inserted, interpolation, precision=lax.Precision.HIGHEST, preferred_element_type=jnp.float32
    )
    volume = mapped / (weight_sum + regularizer)[:, None]
    back_values = lax.dot_general(
        volume,
        interpolation,
        (((1,), (1,)), ((), ())),
        precision=lax.Precision.HIGHEST,
        preferred_element_type=jnp.float32,
    )
    reply_values = back_values[flat_rows].reshape(ori_count, capacity, SEGLEN)
    returned = lax.all_to_all(reply_values, "ori", split_axis=0, concat_axis=0, tiled=True)
    resampled = returned.reshape(-1, SEGLEN)[slot_index].reshape(own_slices.shape)
    return (volume, resampled)


def solution(mesh):
    in_specs = (
        P(("img", "ori"), None),
        P("ori", None),
        P(),
        P(("ori", "img"), None),
        P(("ori", "img")),
        P(("ori", "img"), None),
        P(("ori", "img")),
    )
    out_specs = (P(("ori", "img"), None), P(("ori", "img"), None))
    return jax.shard_map(shards, mesh=mesh, in_specs=in_specs, out_specs=out_specs, check_vma=False)
```

profile of v0, /device:TPU:0, one launch (start us, length us, event | category | flops | bytes accessed | tf_op | source)
XLA Modules:
  0.0 178.8 jit_solution(16074664980183056933)
XLA Ops:
  7.3 0.7 copy-done.7
  7.9 1.9 %fusion.99 = (f32[12,8192]{1,0:T(8,128)S(1)}, f32[12,8192]{1,0:T(8,128)S(1)}) fusion(f32[8192]{0:T(1024)S(1)} %get-tuple-element.222, f32[12]{0:T(128)S(1)} %get-tuple-element.220, f32[8192]{0:T(1024)S(1)} %get-tuple-element.221, f32[12]{0:T(128)S(1)} %get-tuple-element.219), kind=kLoop, calls=%fused_computation.175 | loop fusion | flops 393216 | bytes 852064 | tf_op jit(solution)/shard_map/cos | solution.py:39
  10.5 0.5 copy-done.4
  11.0 11.3 %all-gather.2 = bf16[8,2,16384]{2,1,0:T(2,128)(2,1)S(1)} all-gather(bf16[1,2,16384]{2,1,0:T(2,128)(2,1)S(1)} %bitcast.280), channel_id=1, replica_groups=mesh['img'=4,'ori'=8] {'ori'}, dimensions={0}, use_global_device_ids=true | all-gather | bytes 589824 | tf_op jit(solution)/shard_map/all_gather | solution.py:87
  22.5 0.8 copy-done.2
  23.4 0.4 fusion.23
  23.8 0.3 fusion.13
  24.1 0.3 fusion.12
  24.4 0.3 fusion.11
  24.7 0.4 fusion.35
  25.2 0.3 fusion.10
  25.5 0.3 fusion.9
  25.8 0.3 fusion.8
  26.2 0.4 fusion.47
  26.6 0.3 fusion.7
  26.9 0.3 fusion.6
  27.3 0.3 fusion.5
  27.6 0.4 fusion.59
  28.0 0.3 fusion.4
  28.4 0.3 fusion.3
  28.7 0.3 fusion.2
  29.2 0.6 copy-done.8
  29.8 0.6 dynamic-slice
  31.5 13.4 %all-reduce.2 = (f32[128]{0:T(128)S(1)}, f32[128]{0:T(128)S(1)}) all-reduce(f32[128]{0:T(128)S(1)} %dynamic-update-slice, f32[128]{0:T(128)S(1)} %dynamic-update-slice.1), channel_id=2, replica_groups=mesh['img'=4,'ori'=8] {'ori'}, use_global_device_ids=true, to_apply=%add | all-reduce | flops 256 | bytes 2048
  48.8 1.4 multiply_add_fusion.1
  50.2 1.4 multiply_add_fusion
  51.6 1.1 pad_maximum_fusion
  52.8 0.7 copy-done.5
  53.4 1.1 reduce-window.6
  54.8 0.7 copy-done.6
  55.6 3.0 %scatter_custom_fusion = f32[2048]{0:T(1024)} fusion(s32[512]{0:T(512)S(1)} %bitcast.287, f32[512]{0:T(512)S(1)} %convert_element_type.57, f32[]{:T(128)} %constant.90.clone.1), kind=kCustom, calls=%fused_computation.234 | custom fusion | bytes 8196 | tf_op jit(solution)/shard_map/scatter | solution.py:132
  58.6 3.3 %all-to-all-start = ((f32[8,1,256]{2,1,0:T(1,128)}), f32[8,1,256]{2,1,0:T(1,128)S(1)}, u32[]{:S(2)}, u32[]{:S(2)}) async-start(f32[8,1,256]{2,1,0:T(1,128)} %bitcast.8), calls=%async_computation | async-start | bytes 16384 | tf_op jit(solution)/shard_map/all_to_all | solution.py:145
  62.0 12.8 %psum.15 = f32[16]{0:T(128)S(1)} all-reduce(f32[16]{0:T(128)S(1)} %get-tuple-element.215), channel_id=1, replica_groups=mesh['img'=4,'ori'=8] {'img'}, use_global_device_ids=true, to_apply=%region_12.13 | all-reduce | flops 16 | bytes 128 | tf_op jit(solution)/shard_map/psum | solution.py:110
  74.9 3.0 %scatter_custom_fusion.3 = f32[2048]{0:T(1024)} fusion(s32[512]{0:T(512)S(1)} %bitcast.288, f32[512]{0:T(512)S(1)} %broadcast_bitcast_fusion, f32[]{:T(128)} %constant.90.clone.1), kind=kCustom, calls=%fused_computation.232 | custom fusion | bytes 8196 | tf_op jit(solution)/shard_map/scatter | solution.py:128
  77.9 3.9 %all-to-all-start.2 = ((f32[8,1,256]{2,1,0:T(1,128)}), f32[8,1,256]{2,1,0:T(1,128)S(1)}, u32[]{:S(2)}, u32[]{:S(2)}) async-start(f32[8,1,256]{2,1,0:T(1,128)} %bitcast.78), calls=%async_computation.2 | async-start | bytes 16384 | tf_op jit(solution)/shard_map/all_to_all | solution.py:142
  81.8 23.5 %all-reduce.5.cloned.1.call-done = f32[16,16384]{1,0:T(8,128)} async-done(((f32[16,16384]{1,0:T(8,128)}), f32[16,16384]{1,0:T(8,128)}) %all-reduce.5.cloned.1.call-update) | async-done | bytes 1048592 | tf_op jit(solution)/shard_map/psum | solution.py:110
  105.3 1.1 constant_dynamic-slice_fusion.1
  106.6 2.7 %scatter_custom_fusion.1 = f32[2048,128]{1,0:T(8,128)} fusion(s32[512]{0:T(512)S(1)} %bitcast.289, f32[512,128]{1,0:T(8,128)S(1)} %reshape.167, f32[]{:T(128)} %constant.90.clone.1), kind=kCustom, calls=%fused_computation.176 | custom fusion | bytes 1048580 | tf_op jit(solution)/shard_map/scatter | solution.py:126
  109.3 3.7 %all-to-all-start.1 = ((f32[8,256,128]{2,1,0:T(8,128)}), f32[8,256,128]{2,1,0:T(8,128)S(1)}, u32[]{:S(2)}, u32[]{:S(2)}) async-start(f32[8,256,128]{2,1,0:T(8,128)} %bitcast.75), calls=%async_computation.1 | async-start | bytes 2097152 | tf_op jit(solution)/shard_map/all_to_all | solution.py:135
  113.0 0.7 copy-done.1
  113.7 14.7 %scatter_fusion = f32[256]{0:T(256)S(1)} fusion(f32[256]{0:T(256)S(1)} %copy-done.1, s32[2048]{0:T(1024)S(1)} %bitcast.277, f32[2048]{0:T(1024)S(1)} %bitcast.281), kind=kCustom, calls=%fused_computation.6 | custom fusion | flops 2048 | bytes 32768 | tf_op jit(solution)/shard_map/scatter-add | solution.py:153
  128.4 14.2 %scatter_custom_fusion.2 = f32[256,128]{1,0:T(8,128)S(1)} fusion(s32[2048]{0:T(1024)S(1)} %bitcast.279, f32[2048,128]{1,0:T(8,128)S(1)} %bitcast.204, f32[]{:T(128)} %constant.90.clone.1), kind=kCustom, calls=%fused_computation.181 | custom fusion | flops 262144 | bytes 131076 | tf_op jit(solution)/shard_map/scatter-add | solution.py:152
  143.2 0.4 copy-done.3
  143.5 7.6 %gather_fusion = f32[2048,128]{1,0:T(8,128)} fusion(f32[256,128]{1,0:T(8,128)S(1)} %fusion.146, s32[2048]{0:T(1024)S(1)} %broadcast_clamp_fusion), kind=kCustom, calls=%fused_computation | custom fusion | bytes 2105344 | tf_op jit(solution)/shard_map/gather | solution.py:165
  151.1 3.6 %all-to-all-start.3 = ((f32[8,256,128]{2,1,0:T(8,128)}), f32[8,256,128]{2,1,0:T(8,128)S(1)}, u32[]{:S(2)}, u32[]{:S(2)}) async-start(f32[8,256,128]{2,1,0:T(8,128)} %bitcast.80), calls=%async_computation.3 | async-start | bytes 2097152 | tf_op jit(solution)/shard_map/all_to_all | solution.py:166
  154.7 15.4 %all-to-all-done.3 = f32[8,256,128]{2,1,0:T(8,128)S(1)} async-done(((f32[8,256,128]{2,1,0:T(8,128)}), f32[8,256,128]{2,1,0:T(8,128)S(1)}, u32[]{:S(2)}, u32[]{:S(2)}) %all-to-all-start.3) | async-done | bytes 1048608 | tf_op jit(solution)/shard_map/all_to_all | solution.py:166
  170.1 1.0 gather_fusion.1
  171.1 0.8 reshape.138
  (66 shorter events, 6.7 us)
Async XLA Ops:
  7.2 135.4 %copy-start = (f32[128,128]{1,0:T(8,128)S(1)}, f32[128,128]{1,0:T(8,128)}, u32[]{:S(2)}) copy-start(f32[128,128]{1,0:T(8,128)} %param.14) | copy-start | bytes 196612
  7.2 98.1 %all-reduce.5.cloned.1.call-start = ((), (), s32[]{:S(2)}) async-start(), calls=%async_computation.4 | async-start | bytes 2097152 | tf_op jit(solution)/shard_map/psum | solution.py:110
  7.2 0.7 copy-start.7
  10.2 0.8 copy-start.4
  22.3 1.0 copy-start.2
  29.2 0.7 copy-start.8
  52.7 0.7 copy-start.5
  54.8 0.7 copy-start.6
  58.6 19.3 %all-to-all-start = ((f32[8,1,256]{2,1,0:T(1,128)}), f32[8,1,256]{2,1,0:T(1,128)S(1)}, u32[]{:S(2)}, u32[]{:S(2)}) async-start(f32[8,1,256]{2,1,0:T(1,128)} %bitcast.8), calls=%async_computation | async-start | bytes 16384 | tf_op jit(solution)/shard_map/all_to_all | solution.py:145
  77.9 31.4 %all-to-all-start.2 = ((f32[8,1,256]{2,1,0:T(1,128)}), f32[8,1,256]{2,1,0:T(1,128)S(1)}, u32[]{:S(2)}, u32[]{:S(2)}) async-start(f32[8,1,256]{2,1,0:T(1,128)} %bitcast.78), calls=%async_computation.2 | async-start | bytes 16384 | tf_op jit(solution)/shard_map/all_to_all | solution.py:142
  109.3 19.1 %all-to-all-start.1 = ((f32[8,256,128]{2,1,0:T(8,128)}), f32[8,256,128]{2,1,0:T(8,128)S(1)}, u32[]{:S(2)}, u32[]{:S(2)}) async-start(f32[8,256,128]{2,1,0:T(8,128)} %bitcast.75), calls=%async_computation.1 | async-start | bytes 2097152 | tf_op jit(solution)/shard_map/all_to_all | solution.py:135
  113.0 0.7 copy-start.1
  142.9 0.7 copy-start.3
  151.1 19.0 %all-to-all-start.3 = ((f32[8,256,128]{2,1,0:T(8,128)}), f32[8,256,128]{2,1,0:T(8,128)S(1)}, u32[]{:S(2)}, u32[]{:S(2)}) async-start(f32[8,256,128]{2,1,0:T(8,128)} %bitcast.80), calls=%async_computation.3 | async-start | bytes 2097152 | tf_op jit(solution)/shard_map/all_to_all | solution.py:166
Sparse Core Ops, SparseCore 0:
  52.9 52.3 all-reduce.4
where the time goes:
time: 180 us; the launch traced here: 179 us
  waiting for transfers between devices  38.9 us (22%)
  other arithmetic  38.1 us (21%)
  blocking collectives  37.4 us (21%)
  local copies, waits for them, and re-layouts  26.9 us (15%)
  between operations  15 us (8%)
  starting transfers between devices  14.5 us (8%)
  matrix products  7.79 us (4%)
    psum x1, waiting for transfers between devices, shards(): full_slices, full_mass = lax.psum((summed, orient_mass), 'img')  23.5 us
    all_to_all x1, waiting for transfers between devices, shards(): lax.all_to_all(reply_values, 'ori', split_axis=0, concat_axis=0, tiled=True)  15.4 us
    scatter-add x1, other arithmetic, shards(): jnp.zeros((row_count,), jnp.float32).at[flat_rows].add(got_mass.reshape(-1))  14.7 us
    scatter-add x1, other arithmetic, shards(): jnp.zeros((row_count, SEGLEN), jnp.float32).at[flat_rows].add(flat_values)  14.2 us
    unnamed x1, blocking collectives  13.4 us
    psum x1, blocking collectives, shards(): full_slices, full_mass = lax.psum((summed, orient_mass), 'img')  12.8 us
    all_gather x1, blocking collectives, shards(): group_images = lax.all_gather(images, 'ori', axis=0, tiled=True)  11.3 us
    gather x1, local copies, waits for them, and re-layouts, shards(): reply_values = back_values[flat_rows].reshape(ori_count, capacity, SEGLEN)  7.57 us
  transfers between devices with their start and end apart: 5, of which 2 were waited for; matrix products, arithmetic and copies ran while one was open for 15% of the time, Pallas kernels for 0%

commit v1 on v0

v1 whole, which is shorter than its diff:
```python
import math

import jax
import jax.numpy as jnp
from jax import lax
from jax.sharding import PartitionSpec as P

SEGLEN = 128
grid_width = 64
image_side = 128.0
bf16 = jnp.bfloat16
f32 = jnp.float32


def hop(value, axis, distance):
    pairs = [(place, place ^ distance) for place in range(lax.axis_size(axis))]
    return lax.ppermute(value, axis, pairs)


def even_distances():
    return range(2, lax.axis_size("ori"), 2)


def gather_plane(value):
    near = jnp.concatenate([value] + [hop(value, "ori", k) for k in even_distances()], axis=0)
    return jnp.concatenate([near, hop(near, "ori", 1)], axis=0)


def phase_tables(shifts, coef):
    half_len = coef // 2
    positions = jnp.arange(half_len, dtype=jnp.int32)
    freq_x = (positions % grid_width).astype(f32)
    freq_y = (positions // grid_width - half_len // grid_width // 2).astype(f32)
    angles = (
        2.0
        * math.pi
        / image_side
        * (shifts[:, 0:1] * freq_x[None, :] + shifts[:, 1:2] * freq_y[None, :])
    )
    return (jnp.cos(angles), jnp.sin(angles))


def rotate(real_part, imag_part, cosine_row, sine_row):
    rotated_re = real_part * cosine_row[None, :] - imag_part * sine_row[None, :]
    rotated_im = real_part * sine_row[None, :] + imag_part * cosine_row[None, :]
    return jnp.concatenate([rotated_re, rotated_im], axis=1).astype(bf16)


def backproject(weights_b, group_images, cosine_table, sine_table):
    half_len = group_images.shape[1] // 2
    orient_count = weights_b.shape[1]
    total_re = jnp.zeros((orient_count, half_len), f32)
    total_im = jnp.zeros((orient_count, half_len), f32)
    for s in range(cosine_table.shape[0]):
        summed = lax.dot_general(
            weights_b[:, :, s],
            group_images,
            (((0,), (0,)), ((), ())),
            preferred_element_type=f32,
        )
        sum_re = summed[:, :half_len]
        sum_im = summed[:, half_len:]
        total_re = total_re + sum_re * cosine_table[s] + sum_im * sine_table[s]
        total_im = total_im - sum_re * sine_table[s] + sum_im * cosine_table[s]
    return jnp.concatenate([total_re, total_im], axis=1)


def merge_stats(stats, distance):
    far = hop(stats, "ori", distance)
    if distance == 1:
        return far[:, ::-1]
    half = distance // 2
    return jnp.stack([far[:, :, e ^ half] for e in range(far.shape[2])], axis=2)


def join(pairs):
    peak = pairs[0][0]
    for pair in pairs[1:]:
        peak = jnp.maximum(peak, pair[0])
    total = sum(pair[1] * jnp.exp(pair[0] - peak) for pair in pairs)
    return jnp.stack([peak, total])


def shards(images, references, shifts, owners, slot_rows, interpolation, regularizer):
    ori_count, img_count = lax.axis_size("ori"), lax.axis_size("img")
    ori, img = lax.axis_index("ori"), lax.axis_index("img")
    shift_count = shifts.shape[0]
    coef = images.shape[1]
    own_images = images.shape[0]
    segs = coef // SEGLEN
    row_count = regularizer.shape[0]
    orient_count = references.shape[0]
    sub_rows = orient_count // img_count
    half_len = coef // 2

    group_images = gather_plane(images)
    group_rows = group_images.shape[0]
    cosine_table, sine_table = phase_tables(shifts, coef)
    references = jnp.concatenate(
        [
            lax.dynamic_slice_in_dim(references, (img ^ m) * sub_rows, sub_rows, 0)
            for m in range(img_count)
        ],
        axis=0,
    )
    real_part = references[:, :half_len].astype(f32)
    imag_part = references[:, half_len:].astype(f32)
    distance = owners[:, 0] ^ ori
    place = (distance >> 1) + (distance & 1) * (ori_count // 2)
    target = place * row_count + slot_rows
    all_rows = ori_count * row_count
    chosen = (jnp.arange(all_rows, dtype=jnp.int32)[:, None] == target[None, :]).astype(bf16)

    score_list = []
    for s in range(shift_count):
        rotated = rotate(real_part, imag_part, cosine_table[s], sine_table[s])
        score_list.append(
            lax.dot_general(
                group_images, rotated, (((1,), (1,)), ((), ())), preferred_element_type=f32
            )
        )
    scores = jnp.stack(score_list, axis=2).reshape(group_rows, -1) * (2.0 / math.sqrt(coef))
    local_peak = jnp.max(scores, axis=1)
    local_total = jnp.sum(jnp.exp(scores - local_peak[:, None]), axis=1)
    stats = jnp.stack([local_peak, local_total]).reshape(2, 2, ori_count // 2, own_images)
    stats = join([stats, merge_stats(stats, 1)])
    stats = join([stats] + [merge_stats(stats, k) for k in even_distances()])
    stats = stats.reshape(2, group_rows)
    weights = jnp.exp(scores - stats[0][:, None]) / stats[1][:, None]
    weights3 = weights.reshape(group_rows, orient_count, shift_count)
    orient_mass = jnp.sum(weights3, axis=(0, 2))
    summed = backproject(weights3.astype(bf16), group_images, cosine_table, sine_table)

    blocks = summed.reshape(img_count, sub_rows, coef)
    masses = orient_mass.reshape(img_count, sub_rows, 1)
    outgoing = jnp.concatenate(
        [blocks, jnp.broadcast_to(masses, (img_count, sub_rows, SEGLEN))], axis=2
    ).astype(bf16)
    incoming = [hop(outgoing[m], "img", m).astype(f32) for m in range(1, img_count)]
    own = blocks[0] + sum(value[:, :coef] for value in incoming)
    own_mass = masses[0] + sum(value[:, coef : coef + 1] for value in incoming)
    segments = own.astype(bf16).reshape(-1, SEGLEN)
    seg_mass = jnp.repeat(own_mass[:, 0], segs)[None, :]

    part = jnp.dot(chosen, segments, preferred_element_type=f32)
    part_mass = lax.dot_general(
        seg_mass.astype(bf16), chosen, (((1,), (1,)), ((), ())), preferred_element_type=f32
    )
    mass_rows = max(16, row_count // SEGLEN)
    part_mass = part_mass.reshape(ori_count, row_count)
    part_mass = jnp.pad(part_mass, ((0, 0), (0, mass_rows * SEGLEN - row_count)))
    parcel = jnp.concatenate(
        [part.reshape(ori_count, row_count, SEGLEN), part_mass.reshape(ori_count, -1, SEGLEN)], axis=1
    ).astype(bf16)
    half = ori_count // 2
    parcel = parcel[:half].astype(f32) + hop(parcel[half:], "ori", 1).astype(f32)
    small = parcel.astype(bf16)
    brick = parcel[0] + sum(hop(small[k // 2], "ori", k).astype(f32) for k in even_distances())
    inserted = brick[:row_count]
    weight_sum = brick[row_count:].reshape(-1)[:row_count]
    mapped = jnp.dot(
        inserted, interpolation, precision=lax.Precision.HIGHEST, preferred_element_type=f32
    )
    volume = mapped / (weight_sum + regularizer)[:, None]
    back_values = lax.dot_general(
        volume,
        interpolation,
        (((1,), (1,)), ((), ())),
        precision=lax.Precision.HIGHEST,
        preferred_element_type=f32,
    )
    bricks = gather_plane(back_values.astype(bf16))
    resampled = lax.dot_general(
        chosen, bricks, (((0,), (0,)), ((), ())), preferred_element_type=f32
    )
    return (volume, resampled.reshape(sub_rows, coef))


def solution(mesh):
    in_specs = (
        P(("img", "ori"), None),
        P("ori", None),
        P(),
        P(("ori", "img"), None),
        P(("ori", "img")),
        P(("ori", "img"), None),
        P(("ori", "img")),
    )
    out_specs = (P(("ori", "img"), None), P(("ori", "img"), None))
    return jax.shard_map(shards, mesh=mesh, in_specs=in_specs, out_specs=out_specs, check_vma=False)
```

time: 180 us -> 77.5 us (0.43)
  blocking collectives: 37.4 us -> 0 us
  other arithmetic: 38.1 us -> 11.1 us
  local copies, waits for them, and re-layouts: 26.9 us -> 6.56 us
  between operations: 15 us -> 1.18 us
  waiting for transfers between devices: 38.9 us -> 25.3 us
  starting transfers between devices: 14.5 us -> 20.1 us
  matrix products: 7.79 us -> 13.1 us
    scatter-add x2 -> x0, other arithmetic: 28.9 us -> none  [the longest x1 14.7 us: shards(): jnp.zeros((row_count,), jnp.float32).at[flat_rows].add(got_mass.reshape(-1))]
    ppermute x0 -> x19, waiting for transfers between devices: none -> 25.3 us  [hop(): return lax.ppermute(value, axis, pairs)]
    psum x1 -> x0, waiting for transfers between devices: 23.5 us -> none  [shards(): full_slices, full_mass = lax.psum((summed, orient_mass), 'img')]
    ppermute x0 -> x19, starting transfers between devices: none -> 20.1 us  [hop(): return lax.ppermute(value, axis, pairs)]
    all_to_all x4 -> x0, waiting for transfers between devices: 15.4 us -> none  [the longest x1 15.4 us: shards(): lax.all_to_all(reply_values, 'ori', split_axis=0, concat_axis=0, tiled=True)]
    all_to_all x4 -> x0, starting transfers between devices: 14.5 us -> none  [the longest x1 3.91 us: shards(): lax.all_to_all(send_mass.reshape(ori_count, capacity), 'ori', split_axis=...]
    unnamed x1 -> x0, blocking collectives: 13.4 us -> none
    psum x1 -> x0, blocking collectives: 12.8 us -> none  [shards(): full_slices, full_mass = lax.psum((summed, orient_mass), 'img')]
  transfers between devices with their start and end apart: 5 -> 19, of which waited for: 2 -> 15; matrix products, arithmetic and copies ran while one was open for 15% -> 11% of each run, Pallas kernels for 0% -> 0%
where the time goes in v1:
time: 77.5 us; the launch traced here: 77.2 us
  waiting for transfers between devices  25.3 us (33%)
  starting transfers between devices  20.1 us (26%)
  matrix products  13.1 us (17%)
  other arithmetic  11.1 us (14%)
  local copies, waits for them, and re-layouts  6.56 us (8%)
  between operations  1.18 us (2%)
    ppermute x19, waiting for transfers between devices, hop(): return lax.ppermute(value, axis, pairs)  25.3 us
    ppermute x19, starting transfers between devices, hop(): return lax.ppermute(value, axis, pairs)  20.1 us
    dot_general x12, matrix products, shards(): lax.dot_general(group_images, rotated, (((1,), (1,)), ((), ())), preferre...  6.21 us
    another operation x6, other arithmetic  4.63 us
    dot_general x12, matrix products, backproject(): lax.dot_general(weights_b[:, :, s], group_images, (((0,), (0,)), ((), ())...  3.23 us
    cos x1, other arithmetic, phase_tables(): return (jnp.cos(angles), jnp.sin(angles))  1.94 us
    unnamed x45, local copies, waits for them, and re-layouts  1.57 us
  transfers between devices with their start and end apart: 19, of which 15 were waited for; matrix products, arithmetic and copies ran while one was open for 11% of the time, Pallas kernels for 0%

profile of v1, /device:TPU:0, one launch (start us, length us, event | category | flops | bytes accessed | tf_op | source)
XLA Modules:
  0.0 77.2 jit_solution(853957776070609690)
XLA Ops:
  0.6 3.0 %collective-permute-start = (bf16[2,16384]{1,0:T(2,128)(2,1)}, bf16[2,16384]{1,0:T(2,128)(2,1)S(1)}, u32[]{:S(2)}, u32[]{:S(2)}) collective-permute-start(bf16[2,16384]{1,0:T(2,128)(2,1)} %param.7), channel_id=1, source_target_pairs={{0,2},{1,3},{2,0},{3,1},{4,6},{5,7},{6,4},{7,5},{8,10},{9,11},{10,... | collective-permute-start | bytes 196616 | tf_op jit(solution)/shard_map/ppermute | solution.py:17
  3.6 1.5 %collective-permute-start.1 = (bf16[2,16384]{1,0:T(2,128)(2,1)}, bf16[2,16384]{1,0:T(2,128)(2,1)S(1)}, u32[]{:S(2)}, u32[]{:S(2)}) collective-permute-start(bf16[2,16384]{1,0:T(2,128)(2,1)} %param.7), channel_id=1, source_target_pairs={{0,4},{1,5},{2,6},{3,7},{4,0},{5,1},{6,2},{7,3},{8,12},{9,13},{10,... | collective-permute-start | bytes 196616 | tf_op jit(solution)/shard_map/ppermute | solution.py:17
  5.2 0.8 slice_bitcast_fusion.31
  6.0 1.9 %fusion.111 = (f32[12,8192]{1,0:T(8,128)S(1)}, f32[12,8192]{1,0:T(8,128)S(1)}) fusion(f32[8192]{0:T(1024)S(1)} %get-tuple-element.103, f32[12]{0:T(128)S(1)} %get-tuple-element.99, f32[8192]{0:T(1024)S(1)} %get-tuple-element.102, f32[12]{0:T(128)S(1)} %get-tuple-element.98), kind=kLoop, calls=%fused_computation.182 | loop fusion | flops 393216 | bytes 852064 | tf_op jit(solution)/shard_map/cos | solution.py:40
  8.5 0.4 copy-done.1
  9.5 0.4 fusion.71
  10.0 1.3 %fusion.59 = (bf16[16,8192]{1,0:T(8,128)(2,1)S(1)}, bf16[16,8192]{1,0:T(8,128)(2,1)}, bf16[16,8192]{1,0:T(8,128)(2,1)}, bf16[16,8192]{1,0:T(8,128)(2,1)}, bf16[16,8192]{1,0:T(8,128)(2,1)}, /*index=5*/bf16[16,8192]{1,0:T(8,128)(2,1)}) fusion(f32[8192]{0:T(1024)S(1)} %bitcast.220, f32[8192]{0:T(1024)S(1)} %bitcast.184, ...), kind=kLoop, calls=%fused_computation.126 | loop fusion | flops 3407872 | bytes 2293760 | tf_op jit(solution)/shard_map/convert.14
  11.3 1.4 %fusion.47 = (bf16[16,8192]{1,0:T(8,128)(2,1)}, bf16[16,8192]{1,0:T(8,128)(2,1)}, bf16[16,8192]{1,0:T(8,128)(2,1)}, bf16[16,8192]{1,0:T(8,128)(2,1)}, bf16[16,8192]{1,0:T(8,128)(2,1)}, /*index=5*/bf16[16,8192]{1,0:T(8,128)(2,1)}) fusion(f32[8192]{0:T(1024)S(1)} %bitcast.229, f32[8192]{0:T(1024)S(1)} %bitcast.193, ...), kind=kLoop, calls=%fused_computation.114 | loop fusion | flops 3407872 | bytes 2293760 | tf_op jit(solution)/shard_map/convert.20
  12.7 1.4 %fusion.35 = (bf16[16,8192]{1,0:T(8,128)(2,1)}, bf16[16,8192]{1,0:T(8,128)(2,1)}, bf16[16,8192]{1,0:T(8,128)(2,1)}, bf16[16,8192]{1,0:T(8,128)(2,1)}, bf16[16,8192]{1,0:T(8,128)(2,1)}, /*index=5*/bf16[16,8192]{1,0:T(8,128)(2,1)}) fusion(f32[8192]{0:T(1024)S(1)} %bitcast.238, f32[8192]{0:T(1024)S(1)} %bitcast.202, ...), kind=kLoop, calls=%fused_computation.102 | loop fusion | flops 3407872 | bytes 2293760 | tf_op jit(solution)/shard_map/convert.26
  14.6 1.6 %collective-permute-done.3 = bf16[8,16384]{1,0:T(8,128)(2,1)} collective-permute-done((bf16[8,16384]{1,0:T(8,128)(2,1)S(1)}, bf16[8,16384]{1,0:T(8,128)(2,1)}, u32[]{:S(2)}, u32[]{:S(2)}) %collective-permute-start.3) | collective-permute-done | bytes 262176 | tf_op jit(solution)/shard_map/ppermute | solution.py:17
  16.2 1.4 %concatenate.78 = bf16[16,16384]{1,0:T(8,128)(2,1)S(1)} concatenate(bf16[2,16384]{1,0:T(2,128)(2,1)S(1)} %copy-done.15, bf16[2,16384]{1,0:T(2,128)(2,1)S(1)} %collective-permute-done, bf16[2,16384]{1,0:T(2,128)(2,1)S(1)} %collective-permute-done.1, bf16[2,16384]{1,0:T(2,128)(2,1)S(1)} %collective-permute-done.2, bf16[8,16384]{1,0:T(8,128)(2,1)} %collective-permute-done.3), dimensions={0} | concatenate | bytes 1048576 | tf_op jit(solution)/shard_map/concatenate | solution.py:26
  17.7 1.4 %fusion.24 = f32[16,16,12]{0,1,2:T(8,128)S(1)} fusion(bf16[16,16384]{1,0:T(8,128)(2,1)S(1)} %concatenate.78, bf16[16,8192]{1,0:T(8,128)(2,1)} %get-tuple-element.73, bf16[16,8192]{1,0:T(8,128)(2,1)} %get-tuple-element.74), kind=kOutput, calls=%fused_computation.88 | convolution fusion | flops 9437183 | bytes 1056768 | tf_op jit(solution)/shard_map/dot_general | solution.py:118
  19.1 1.4 %fusion.23 = f32[16,16,12]{0,1,2:T(8,128)S(1)} fusion(f32[16,16,12]{0,1,2:T(8,128)S(1)} %fusion.24, bf16[16,16384]{1,0:T(8,128)(2,1)S(1)} %concatenate.78, bf16[16,8192]{1,0:T(8,128)(2,1)} %get-tuple-element.71, bf16[16,8192]{1,0:T(8,128)(2,1)} %get-tuple-element.72), kind=kOutput, calls=%fused_computation.86 | convolution fusion | flops 9437184 | bytes 1056768 | tf_op jit(solution)/shard_map/dot_general | solution.py:118
  20.6 0.3 fusion.22
  20.9 0.3 fusion.21
  22.0 0.3 fusion.19
  24.0 0.3 fusion.15
  24.3 0.3 fusion.14
  24.6 0.3 fusion.13
  25.5 1.0 %collective-permute-done.4 = f32[2,2,4,2]{3,2,1,0:T(4,128)S(1)} collective-permute-done((f32[2,2,4,2]{3,2,1,0:T(4,128)S(1)}, f32[2,2,4,2]{3,2,1,0:T(4,128)S(1)}, u32[]{:S(2)}, u32[]{:S(2)}) %collective-permute-start.4) | collective-permute-done | bytes 160 | tf_op jit(solution)/shard_map/ppermute | solution.py:17
  26.6 2.0 %collective-permute-start.5 = (f32[2,2,4,2]{3,2,1,0:T(4,128)S(1)}, f32[2,2,4,2]{3,2,1,0:T(4,128)S(1)}, u32[]{:S(2)}, u32[]{:S(2)}) collective-permute-start(f32[2,2,4,2]{3,2,1,0:T(4,128)S(1)} %pad_maximum_fusion.7), channel_id=1, source_target_pairs={{0,2},{1,3},{2,0},{3,1},{4,6},{5,7},{6,4},{7,5},{8,10},{9,11},{10,... | collective-permute-start | bytes 392 | tf_op jit(solution)/shard_map/ppermute | solution.py:17
  28.6 1.5 %collective-permute-start.7 = (f32[2,2,4,2]{3,2,1,0:T(4,128)S(1)}, f32[2,2,4,2]{3,2,1,0:T(4,128)S(1)}, u32[]{:S(2)}, u32[]{:S(2)}) collective-permute-start(f32[2,2,4,2]{3,2,1,0:T(4,128)S(1)} %pad_maximum_fusion.7), channel_id=1, source_target_pairs={{0,6},{1,7},{2,4},{3,5},{4,2},{5,3},{6,0},{7,1},{8,14},{9,15},{10,... | collective-permute-start | bytes 392 | tf_op jit(solution)/shard_map/ppermute | solution.py:17
  30.3 2.8 %collective-permute-done.7 = f32[2,2,4,2]{3,2,1,0:T(4,128)S(1)} collective-permute-done((f32[2,2,4,2]{3,2,1,0:T(4,128)S(1)}, f32[2,2,4,2]{3,2,1,0:T(4,128)S(1)}, u32[]{:S(2)}, u32[]{:S(2)}) %collective-permute-start.7) | collective-permute-done | bytes 160 | tf_op jit(solution)/shard_map/ppermute | solution.py:17
  33.1 0.6 collective-permute-done.6
  37.4 1.4 %multiply_add_fusion.1 = f32[16,8192]{1,0:T(8,128)S(1)} fusion(f32[16,16384]{1,0:T(8,128)S(1)} %fusion.130, f32[16,16384]{1,0:T(8,128)S(1)} %fusion.131, f32[16,16384]{1,0:T(8,128)S(1)} %fusion.132, f32[16,16384]{1,0:T(8,128)S(1)} %fusion.133, f32[16,16384]{1,0:T(8,128)S(1)} %fusion.134, f32[16,16384]{1,0:T(8,128)S(1)} %fusion.135, ...), kind=kLoop, calls=%fused_computation.179 | loop fusion | flops 6160384 | bytes 13893632 | tf_op jit(solution)/shard_map/add | solution.py:63
  38.8 1.4 %multiply_add_fusion = f32[16,8192]{1,0:T(8,128)S(1)} fusion(f32[16,16384]{1,0:T(8,128)S(1)} %fusion.130, f32[16,16384]{1,0:T(8,128)S(1)} %fusion.131, f32[16,16384]{1,0:T(8,128)S(1)} %fusion.132, f32[16,16384]{1,0:T(8,128)S(1)} %fusion.133, f32[16,16384]{1,0:T(8,128)S(1)} %fusion.134, f32[16,16384]{1,0:T(8,128)S(1)} %fusion.135, ...), kind=kLoop, calls=%fused_computation.178 | loop fusion | flops 6291456 | bytes 13893632 | tf_op jit(solution)/shard_map/add | solution.py:64
  40.8 1.6 %collective-permute-start.8 = (bf16[4,16512]{1,0:T(4,128)(2,1)S(1)}, bf16[4,16512]{1,0:T(4,128)(2,1)S(1)}, u32[]{:S(2)}, u32[]{:S(2)}) collective-permute-start(bf16[4,16512]{1,0:T(4,128)(2,1)S(1)} %get-tuple-element.32), channel_id=1, source_target_pairs={{0,8},{8,0},{16,24},{24,16},{1,9},{9,1},{17,25},{25,17},{2,10},{10... | collective-permute-start | bytes 396296 | tf_op jit(solution)/shard_map/ppermute | solution.py:17
  42.5 2.6 %collective-permute-start.9 = (bf16[4,16512]{1,0:T(4,128)(2,1)S(1)}, bf16[4,16512]{1,0:T(4,128)(2,1)S(1)}, u32[]{:S(2)}, u32[]{:S(2)}) collective-permute-start(bf16[4,16512]{1,0:T(4,128)(2,1)S(1)} %get-tuple-element.33), channel_id=1, source_target_pairs={{0,16},{8,24},{16,0},{24,8},{1,17},{9,25},{17,1},{25,9},{2,18},{10... | collective-permute-start | bytes 396296 | tf_op jit(solution)/shard_map/ppermute | solution.py:17
  45.4 1.6 %collective-permute-done.8 = bf16[4,16512]{1,0:T(4,128)(2,1)S(1)} collective-permute-done((bf16[4,16512]{1,0:T(4,128)(2,1)S(1)}, bf16[4,16512]{1,0:T(4,128)(2,1)S(1)}, u32[]{:S(2)}, u32[]{:S(2)}) %collective-permute-start.8) | collective-permute-done | bytes 132128 | tf_op jit(solution)/shard_map/ppermute | solution.py:17
  47.0 7.0 %collective-permute-done.9 = bf16[4,16512]{1,0:T(4,128)(2,1)S(1)} collective-permute-done((bf16[4,16512]{1,0:T(4,128)(2,1)S(1)}, bf16[4,16512]{1,0:T(4,128)(2,1)S(1)}, u32[]{:S(2)}, u32[]{:S(2)}) %collective-permute-start.9) | collective-permute-done | bytes 132128 | tf_op jit(solution)/shard_map/ppermute | solution.py:17
  54.6 1.0 %fusion.10 = bf16[8,256,128]{2,1,0:T(8,128)(2,1)S(1)} fusion(bf16[512,128,1]{1,0,2:T(8,128)(2,1)S(1)} %reshape.151, s32[512]{0:T(512)S(1)} %add.244, s32[8,256]{1,0:T(8,128)S(1)} %multiply_add_fusion.2), kind=kOutput, calls=%fused_computation.59 | convolution fusion | flops 269746176 | bytes 665600 | tf_op jit(solution)/shard_map/dot_general | solution.py:145
  55.7 0.8 %fusion = bf16[1,8,256]{2,0,1:T(2,128)(2,1)S(1)} fusion(bf16[512,1,1]{0,1,2:T(2,128)(2,1)S(1)} %reshape.152, s32[512]{0:T(512)S(1)} %add.244, s32[8,256]{1,0:T(8,128)S(1)} %multiply_add_fusion.2), kind=kOutput, calls=%fused_computation | convolution fusion | flops 3145728 | bytes 15360 | tf_op jit(solution)/shard_map/dot_general | solution.py:146
  56.6 1.5 %collective-permute-done.11 = bf16[4,272,128]{2,1,0:T(8,128)(2,1)S(1)} collective-permute-done((bf16[4,272,128]{2,1,0:T(8,128)(2,1)S(1)}, bf16[4,272,128]{2,1,0:T(8,128)(2,1)S(1)}, u32[]{:S(2)}, u32[]{:S(2)}) %collective-permute-start.11) | collective-permute-done | bytes 278560 | tf_op jit(solution)/shard_map/ppermute | solution.py:17
  58.3 1.7 %collective-permute-start.12 = (bf16[272,128]{1,0:T(8,128)(2,1)S(1)}, bf16[272,128]{1,0:T(8,128)(2,1)S(1)}, u32[]{:S(2)}, u32[]{:S(2)}) collective-permute-start(bf16[272,128]{1,0:T(8,128)(2,1)S(1)} %get-tuple-element.79), channel_id=1, source_target_pairs={{0,2},{1,3},{2,0},{3,1},{4,6},{5,7},{6,4},{7,5},{8,10},{9,11},{10,... | collective-permute-start | bytes 208904 | tf_op jit(solution)/shard_map/ppermute | solution.py:17
  59.9 0.4 collective-permute-start.13
  60.3 1.5 %collective-permute-start.14 = (bf16[272,128]{1,0:T(8,128)(2,1)S(1)}, bf16[272,128]{1,0:T(8,128)(2,1)S(1)}, u32[]{:S(2)}, u32[]{:S(2)}) collective-permute-start(bf16[272,128]{1,0:T(8,128)(2,1)S(1)} %get-tuple-element.80), channel_id=1, source_target_pairs={{0,6},{1,7},{2,4},{3,5},{4,2},{5,3},{6,0},{7,1},{8,14},{9,15},{10,... | collective-permute-start | bytes 208904 | tf_op jit(solution)/shard_map/ppermute | solution.py:17
  61.8 0.8 %collective-permute-done.12 = bf16[272,128]{1,0:T(8,128)(2,1)S(1)} collective-permute-done((bf16[272,128]{1,0:T(8,128)(2,1)S(1)}, bf16[272,128]{1,0:T(8,128)(2,1)S(1)}, u32[]{:S(2)}, u32[]{:S(2)}) %collective-permute-start.12) | collective-permute-done | bytes 69664 | tf_op jit(solution)/shard_map/ppermute | solution.py:17
  62.6 2.3 %collective-permute-done.13 = bf16[272,128]{1,0:T(8,128)(2,1)S(1)} collective-permute-done((bf16[272,128]{1,0:T(8,128)(2,1)S(1)}, bf16[272,128]{1,0:T(8,128)(2,1)S(1)}, u32[]{:S(2)}, u32[]{:S(2)}) %collective-permute-start.13) | collective-permute-done | bytes 69664 | tf_op jit(solution)/shard_map/ppermute | solution.py:17
  64.9 0.7 collective-permute-done.14
  66.3 1.3 %collective-permute-start.15 = (bf16[256,128]{1,0:T(8,128)(2,1)S(1)}, bf16[256,128]{1,0:T(8,128)(2,1)S(1)}, u32[]{:S(2)}, u32[]{:S(2)}) collective-permute-start(bf16[256,128]{1,0:T(8,128)(2,1)S(1)} %get-tuple-element.101), channel_id=1, source_target_pairs={{0,2},{1,3},{2,0},{3,1},{4,6},{5,7},{6,4},{7,5},{8,10},{9,11},{10,... | collective-permute-start | bytes 196616 | tf_op jit(solution)/shard_map/ppermute | solution.py:17
  67.5 0.8 %collective-permute-start.16 = (bf16[256,128]{1,0:T(8,128)(2,1)S(1)}, bf16[256,128]{1,0:T(8,128)(2,1)S(1)}, u32[]{:S(2)}, u32[]{:S(2)}) collective-permute-start(bf16[256,128]{1,0:T(8,128)(2,1)S(1)} %get-tuple-element.101), channel_id=1, source_target_pairs={{0,4},{1,5},{2,6},{3,7},{4,0},{5,1},{6,2},{7,3},{8,12},{9,13},{10,... | collective-permute-start | bytes 196616 | tf_op jit(solution)/shard_map/ppermute | solution.py:17
  68.3 1.5 %collective-permute-start.17 = (bf16[256,128]{1,0:T(8,128)(2,1)S(1)}, bf16[256,128]{1,0:T(8,128)(2,1)S(1)}, u32[]{:S(2)}, u32[]{:S(2)}) collective-permute-start(bf16[256,128]{1,0:T(8,128)(2,1)S(1)} %get-tuple-element.101), channel_id=1, source_target_pairs={{0,6},{1,7},{2,4},{3,5},{4,2},{5,3},{6,0},{7,1},{8,14},{9,15},{10,... | collective-permute-start | bytes 196616 | tf_op jit(solution)/shard_map/ppermute | solution.py:17
  69.8 1.0 %collective-permute-done.15 = bf16[256,128]{1,0:T(8,128)(2,1)S(1)} collective-permute-done((bf16[256,128]{1,0:T(8,128)(2,1)S(1)}, bf16[256,128]{1,0:T(8,128)(2,1)S(1)}, u32[]{:S(2)}, u32[]{:S(2)}) %collective-permute-start.15) | collective-permute-done | bytes 65568 | tf_op jit(solution)/shard_map/ppermute | solution.py:17
  70.8 0.9 %collective-permute-done.16 = bf16[256,128]{1,0:T(8,128)(2,1)S(1)} collective-permute-done((bf16[256,128]{1,0:T(8,128)(2,1)S(1)}, bf16[256,128]{1,0:T(8,128)(2,1)S(1)}, u32[]{:S(2)}, u32[]{:S(2)}) %collective-permute-start.16) | collective-permute-done | bytes 65568 | tf_op jit(solution)/shard_map/ppermute | solution.py:17
  71.8 1.7 %collective-permute-done.17 = bf16[256,128]{1,0:T(8,128)(2,1)S(1)} collective-permute-done((bf16[256,128]{1,0:T(8,128)(2,1)S(1)}, bf16[256,128]{1,0:T(8,128)(2,1)S(1)}, u32[]{:S(2)}, u32[]{:S(2)}) %collective-permute-start.17) | collective-permute-done | bytes 65568 | tf_op jit(solution)/shard_map/ppermute | solution.py:17
  73.6 1.5 %collective-permute-done.18 = bf16[1024,128]{1,0:T(8,128)(2,1)S(1)} collective-permute-done((bf16[1024,128]{1,0:T(8,128)(2,1)S(1)}, bf16[1024,128]{1,0:T(8,128)(2,1)S(1)}, u32[]{:S(2)}, u32[]{:S(2)}) %collective-permute-start.18) | collective-permute-done | bytes 262176 | tf_op jit(solution)/shard_map/ppermute | solution.py:17
  75.1 1.3 %fusion.4 = f32[512,128]{1,0:T(8,128)S(1)} fusion(bf16[2048,128]{1,0:T(8,128)(2,1)S(1)} %constant_dynamic-update-slice_fusion, s32[512]{0:T(512)S(1)} %add.244), kind=kOutput, calls=%fused_computation.5 | convolution fusion | flops 269484032 | bytes 788480 | tf_op jit(solution)/shard_map/dot_general | solution.py:173
  76.4 0.8 %reshape.147 = f32[4,16384]{1,0:T(4,128)} reshape(f32[512,128]{1,0:T(8,128)S(1)} %fusion.4) | data formatting | bytes 524288 | tf_op jit(solution)/shard_map/reshape | solution.py:176
  (124 shorter events, 10.9 us)
Async XLA Ops:
  0.6 65.1 %copy-start = (f32[128,128]{1,0:T(8,128)S(1)}, f32[128,128]{1,0:T(8,128)}, u32[]{:S(2)}) copy-start(f32[128,128]{1,0:T(8,128)} %param.12) | copy-start | bytes 196612
  0.6 13.5 %collective-permute-start = (bf16[2,16384]{1,0:T(2,128)(2,1)}, bf16[2,16384]{1,0:T(2,128)(2,1)S(1)}, u32[]{:S(2)}, u32[]{:S(2)}) collective-permute-start(bf16[2,16384]{1,0:T(2,128)(2,1)} %param.7), channel_id=1, source_target_pairs={{0,2},{1,3},{2,0},{3,1},{4,6},{5,7},{6,4},{7,5},{8,10},{9,11},{10,... | collective-permute-start | bytes 196616 | tf_op jit(solution)/shard_map/ppermute | solution.py:17
  3.6 10.5 %collective-permute-start.1 = (bf16[2,16384]{1,0:T(2,128)(2,1)}, bf16[2,16384]{1,0:T(2,128)(2,1)S(1)}, u32[]{:S(2)}, u32[]{:S(2)}) collective-permute-start(bf16[2,16384]{1,0:T(2,128)(2,1)} %param.7), channel_id=1, source_target_pairs={{0,4},{1,5},{2,6},{3,7},{4,0},{5,1},{6,2},{7,3},{8,12},{9,13},{10,... | collective-permute-start | bytes 196616 | tf_op jit(solution)/shard_map/ppermute | solution.py:17
  5.2 9.0 %collective-permute-start.2 = (bf16[2,16384]{1,0:T(2,128)(2,1)}, bf16[2,16384]{1,0:T(2,128)(2,1)S(1)}, u32[]{:S(2)}, u32[]{:S(2)}) collective-permute-start(bf16[2,16384]{1,0:T(2,128)(2,1)} %param.7), channel_id=1, source_target_pairs={{0,6},{1,7},{2,4},{3,5},{4,2},{5,3},{6,0},{7,1},{8,14},{9,15},{10,... | collective-permute-start | bytes 196616 | tf_op jit(solution)/shard_map/ppermute | solution.py:17
  7.9 1.0 %copy-start.1 = (bf16[16,16384]{1,0:T(8,128)(2,1)S(1)}, bf16[16,16384]{1,0:T(8,128)(2,1)}, u32[]{:S(2)}) copy-start(bf16[16,16384]{1,0:T(8,128)(2,1)} %param.8) | copy-start | bytes 1572868
  12.7 1.4 %copy-start.15 = (bf16[2,16384]{1,0:T(2,128)(2,1)S(1)}, bf16[2,16384]{1,0:T(2,128)(2,1)}, u32[]{:S(2)}) copy-start(bf16[2,16384]{1,0:T(2,128)(2,1)} %param.7) | copy-start | bytes 196612
  12.7 1.8 %copy-start.18 = (s32[512,1]{0,1:T(1,128)S(1)}, s32[512,1]{0,1:T(1,128)}, u32[]{:S(2)}) copy-start(s32[512,1]{0,1:T(1,128)} %param.10) | copy-start | bytes 6148
  14.5 1.7 %collective-permute-start.3 = (bf16[8,16384]{1,0:T(8,128)(2,1)S(1)}, bf16[8,16384]{1,0:T(8,128)(2,1)}, u32[]{:S(2)}, u32[]{:S(2)}) collective-permute-start(bf16[8,16384]{1,0:T(8,128)(2,1)S(1)} %pad_maximum_fusion.3), channel_id=1, source_target_pairs={{0,1},{1,0},{2,3},{3,2},{4,5},{5,4},{6,7},{7,6},{8,9},{9,8},{10,11... | collective-permute-start | bytes 786440 | tf_op jit(solution)/shard_map/ppermute | solution.py:17
  17.6 2.9 %copy-start.13 = (bf16[16,8192]{1,0:T(8,128)(2,1)S(1)}, bf16[16,8192]{1,0:T(8,128)(2,1)}, u32[]{:S(2)}) copy-start(bf16[16,8192]{1,0:T(8,128)(2,1)} %get-tuple-element.26) | copy-start | bytes 786436
  17.7 2.9 %copy-start.14 = (bf16[16,8192]{1,0:T(8,128)(2,1)S(1)}, bf16[16,8192]{1,0:T(8,128)(2,1)}, u32[]{:S(2)}) copy-start(bf16[16,8192]{1,0:T(8,128)(2,1)} %get-tuple-element.27) | copy-start | bytes 786436
  19.1 1.8 %copy-start.11 = (bf16[16,8192]{1,0:T(8,128)(2,1)S(1)}, bf16[16,8192]{1,0:T(8,128)(2,1)}, u32[]{:S(2)}) copy-start(bf16[16,8192]{1,0:T(8,128)(2,1)} %get-tuple-element.69) | copy-start | bytes 786436
  19.1 1.8 %copy-start.12 = (bf16[16,8192]{1,0:T(8,128)(2,1)S(1)}, bf16[16,8192]{1,0:T(8,128)(2,1)}, u32[]{:S(2)}) copy-start(bf16[16,8192]{1,0:T(8,128)(2,1)} %get-tuple-element.70) | copy-start | bytes 786436
  20.5 1.0 %copy-start.9 = (bf16[16,8192]{1,0:T(8,128)(2,1)S(1)}, bf16[16,8192]{1,0:T(8,128)(2,1)}, u32[]{:S(2)}) copy-start(bf16[16,8192]{1,0:T(8,128)(2,1)} %get-tuple-element.67) | copy-start | bytes 786436
  20.5 1.0 %copy-start.10 = (bf16[16,8192]{1,0:T(8,128)(2,1)S(1)}, bf16[16,8192]{1,0:T(8,128)(2,1)}, u32[]{:S(2)}) copy-start(bf16[16,8192]{1,0:T(8,128)(2,1)} %get-tuple-element.68) | copy-start | bytes 786436
  20.9 1.0 %copy-start.7 = (bf16[16,8192]{1,0:T(8,128)(2,1)S(1)}, bf16[16,8192]{1,0:T(8,128)(2,1)}, u32[]{:S(2)}) copy-start(bf16[16,8192]{1,0:T(8,128)(2,1)} %get-tuple-element.20) | copy-start | bytes 786436
  20.9 1.1 %copy-start.8 = (bf16[16,8192]{1,0:T(8,128)(2,1)S(1)}, bf16[16,8192]{1,0:T(8,128)(2,1)}, u32[]{:S(2)}) copy-start(bf16[16,8192]{1,0:T(8,128)(2,1)} %get-tuple-element.21) | copy-start | bytes 786436
  21.6 1.0 %copy-start.5 = (bf16[16,8192]{1,0:T(8,128)(2,1)S(1)}, bf16[16,8192]{1,0:T(8,128)(2,1)}, u32[]{:S(2)}) copy-start(bf16[16,8192]{1,0:T(8,128)(2,1)} %get-tuple-element.65) | copy-start | bytes 786436
  21.6 1.1 %copy-start.6 = (bf16[16,8192]{1,0:T(8,128)(2,1)S(1)}, bf16[16,8192]{1,0:T(8,128)(2,1)}, u32[]{:S(2)}) copy-start(bf16[16,8192]{1,0:T(8,128)(2,1)} %get-tuple-element.66) | copy-start | bytes 786436
  22.0 1.0 %copy-start.3 = (bf16[16,8192]{1,0:T(8,128)(2,1)S(1)}, bf16[16,8192]{1,0:T(8,128)(2,1)}, u32[]{:S(2)}) copy-start(bf16[16,8192]{1,0:T(8,128)(2,1)} %get-tuple-element.63) | copy-start | bytes 786436
  22.0 1.1 %copy-start.4 = (bf16[16,8192]{1,0:T(8,128)(2,1)S(1)}, bf16[16,8192]{1,0:T(8,128)(2,1)}, u32[]{:S(2)}) copy-start(bf16[16,8192]{1,0:T(8,128)(2,1)} %get-tuple-element.64) | copy-start | bytes 786436
  22.6 1.0 %copy-start.2 = (bf16[16,8192]{1,0:T(8,128)(2,1)S(1)}, bf16[16,8192]{1,0:T(8,128)(2,1)}, u32[]{:S(2)}) copy-start(bf16[16,8192]{1,0:T(8,128)(2,1)} %get-tuple-element.15) | copy-start | bytes 786436
  24.6 0.8 %copy-start.17 = (s32[512]{0:T(512)S(1)}, s32[512]{0:T(512)}, u32[]{:S(2)}) copy-start(s32[512]{0:T(512)} %param.11) | copy-start | bytes 6148
  25.3 1.2 %collective-permute-start.4 = (f32[2,2,4,2]{3,2,1,0:T(4,128)S(1)}, f32[2,2,4,2]{3,2,1,0:T(4,128)S(1)}, u32[]{:S(2)}, u32[]{:S(2)}) collective-permute-start(f32[2,2,4,2]{3,2,1,0:T(4,128)S(1)} %pad_maximum_fusion.6), channel_id=1, source_target_pairs={{0,1},{1,0},{2,3},{3,2},{4,5},{5,4},{6,7},{7,6},{8,9},{9,8},{10,11... | collective-permute-start | bytes 392 | tf_op jit(solution)/shard_map/ppermute | solution.py:17
  26.6 3.7 %collective-permute-start.5 = (f32[2,2,4,2]{3,2,1,0:T(4,128)S(1)}, f32[2,2,4,2]{3,2,1,0:T(4,128)S(1)}, u32[]{:S(2)}, u32[]{:S(2)}) collective-permute-start(f32[2,2,4,2]{3,2,1,0:T(4,128)S(1)} %pad_maximum_fusion.7), channel_id=1, source_target_pairs={{0,2},{1,3},{2,0},{3,1},{4,6},{5,7},{6,4},{7,5},{8,10},{9,11},{10,... | collective-permute-start | bytes 392 | tf_op jit(solution)/shard_map/ppermute | solution.py:17
  28.6 4.5 %collective-permute-start.7 = (f32[2,2,4,2]{3,2,1,0:T(4,128)S(1)}, f32[2,2,4,2]{3,2,1,0:T(4,128)S(1)}, u32[]{:S(2)}, u32[]{:S(2)}) collective-permute-start(f32[2,2,4,2]{3,2,1,0:T(4,128)S(1)} %pad_maximum_fusion.7), channel_id=1, source_target_pairs={{0,6},{1,7},{2,4},{3,5},{4,2},{5,3},{6,0},{7,1},{8,14},{9,15},{10,... | collective-permute-start | bytes 392 | tf_op jit(solution)/shard_map/ppermute | solution.py:17
  30.1 3.7 %collective-permute-start.6 = (f32[2,2,4,2]{3,2,1,0:T(4,128)S(1)}, f32[2,2,4,2]{3,2,1,0:T(4,128)S(1)}, u32[]{:S(2)}, u32[]{:S(2)}) collective-permute-start(f32[2,2,4,2]{3,2,1,0:T(4,128)S(1)} %pad_maximum_fusion.7), channel_id=1, source_target_pairs={{0,4},{1,5},{2,6},{3,7},{4,0},{5,1},{6,2},{7,3},{8,12},{9,13},{10,... | collective-permute-start | bytes 392 | tf_op jit(solution)/shard_map/ppermute | solution.py:17
  40.8 6.1 %collective-permute-start.8 = (bf16[4,16512]{1,0:T(4,128)(2,1)S(1)}, bf16[4,16512]{1,0:T(4,128)(2,1)S(1)}, u32[]{:S(2)}, u32[]{:S(2)}) collective-permute-start(bf16[4,16512]{1,0:T(4,128)(2,1)S(1)} %get-tuple-element.32), channel_id=1, source_target_pairs={{0,8},{8,0},{16,24},{24,16},{1,9},{9,1},{17,25},{25,17},{2,10},{10... | collective-permute-start | bytes 396296 | tf_op jit(solution)/shard_map/ppermute | solution.py:17
  42.5 11.6 %collective-permute-start.9 = (bf16[4,16512]{1,0:T(4,128)(2,1)S(1)}, bf16[4,16512]{1,0:T(4,128)(2,1)S(1)}, u32[]{:S(2)}, u32[]{:S(2)}) collective-permute-start(bf16[4,16512]{1,0:T(4,128)(2,1)S(1)} %get-tuple-element.33), channel_id=1, source_target_pairs={{0,16},{8,24},{16,0},{24,8},{1,17},{9,25},{17,1},{25,9},{2,18},{10... | collective-permute-start | bytes 396296 | tf_op jit(solution)/shard_map/ppermute | solution.py:17
  45.0 9.0 %collective-permute-start.10 = (bf16[4,16512]{1,0:T(4,128)(2,1)S(1)}, bf16[4,16512]{1,0:T(4,128)(2,1)S(1)}, u32[]{:S(2)}, u32[]{:S(2)}) collective-permute-start(bf16[4,16512]{1,0:T(4,128)(2,1)S(1)} %get-tuple-element.34), channel_id=1, source_target_pairs={{0,24},{8,16},{16,8},{24,0},{1,25},{9,17},{17,9},{25,1},{2,26},{10... | collective-permute-start | bytes 396296 | tf_op jit(solution)/shard_map/ppermute | solution.py:17
  56.5 9.1 %copy-start.19 = (f32[256]{0:T(256)S(1)}, f32[256]{0:T(256)}, u32[]{:S(2)}) copy-start(f32[256]{0:T(256)} %param.13) | copy-start | bytes 3076
  56.5 1.6 %collective-permute-start.11 = (bf16[4,272,128]{2,1,0:T(8,128)(2,1)S(1)}, bf16[4,272,128]{2,1,0:T(8,128)(2,1)S(1)}, u32[]{:S(2)}, u32[]{:S(2)}) collective-permute-start(bf16[4,272,128]{2,1,0:T(8,128)(2,1)S(1)} %pad_maximum_fusion.2), channel_id=1, source_target_pairs={{0,1},{1,0},{2,3},{3,2},{4,5},{5,4},{6,7},{7,6},{8,9},{9,8},{10,11... | collective-permute-start | bytes 835592 | tf_op jit(solution)/shard_map/ppermute | solution.py:17
  58.3 4.4 %collective-permute-start.12 = (bf16[272,128]{1,0:T(8,128)(2,1)S(1)}, bf16[272,128]{1,0:T(8,128)(2,1)S(1)}, u32[]{:S(2)}, u32[]{:S(2)}) collective-permute-start(bf16[272,128]{1,0:T(8,128)(2,1)S(1)} %get-tuple-element.79), channel_id=1, source_target_pairs={{0,2},{1,3},{2,0},{3,1},{4,6},{5,7},{6,4},{7,5},{8,10},{9,11},{10,... | collective-permute-start | bytes 208904 | tf_op jit(solution)/shard_map/ppermute | solution.py:17
  59.9 4.9 %collective-permute-start.13 = (bf16[272,128]{1,0:T(8,128)(2,1)S(1)}, bf16[272,128]{1,0:T(8,128)(2,1)S(1)}, u32[]{:S(2)}, u32[]{:S(2)}) collective-permute-start(bf16[272,128]{1,0:T(8,128)(2,1)S(1)} %get-tuple-element.81), channel_id=1, source_target_pairs={{0,4},{1,5},{2,6},{3,7},{4,0},{5,1},{6,2},{7,3},{8,12},{9,13},{10,... | collective-permute-start | bytes 208904 | tf_op jit(solution)/shard_map/ppermute | solution.py:17
  60.3 5.3 %collective-permute-start.14 = (bf16[272,128]{1,0:T(8,128)(2,1)S(1)}, bf16[272,128]{1,0:T(8,128)(2,1)S(1)}, u32[]{:S(2)}, u32[]{:S(2)}) collective-permute-start(bf16[272,128]{1,0:T(8,128)(2,1)S(1)} %get-tuple-element.80), channel_id=1, source_target_pairs={{0,6},{1,7},{2,4},{3,5},{4,2},{5,3},{6,0},{7,1},{8,14},{9,15},{10,... | collective-permute-start | bytes 208904 | tf_op jit(solution)/shard_map/ppermute | solution.py:17
  66.0 10.4 %copy-start.16 = (f32[256,128]{1,0:T(8,128)}, f32[256,128]{1,0:T(8,128)S(1)}, u32[]{:S(2)}) copy-start(f32[256,128]{1,0:T(8,128)S(1)} %convolution_divide_fusion) | copy-start | bytes 393220
  66.3 4.6 %collective-permute-start.15 = (bf16[256,128]{1,0:T(8,128)(2,1)S(1)}, bf16[256,128]{1,0:T(8,128)(2,1)S(1)}, u32[]{:S(2)}, u32[]{:S(2)}) collective-permute-start(bf16[256,128]{1,0:T(8,128)(2,1)S(1)} %get-tuple-element.101), channel_id=1, source_target_pairs={{0,2},{1,3},{2,0},{3,1},{4,6},{5,7},{6,4},{7,5},{8,10},{9,11},{10,... | collective-permute-start | bytes 196616 | tf_op jit(solution)/shard_map/ppermute | solution.py:17
  67.5 4.3 %collective-permute-start.16 = (bf16[256,128]{1,0:T(8,128)(2,1)S(1)}, bf16[256,128]{1,0:T(8,128)(2,1)S(1)}, u32[]{:S(2)}, u32[]{:S(2)}) collective-permute-start(bf16[256,128]{1,0:T(8,128)(2,1)S(1)} %get-tuple-element.101), channel_id=1, source_target_pairs={{0,4},{1,5},{2,6},{3,7},{4,0},{5,1},{6,2},{7,3},{8,12},{9,13},{10,... | collective-permute-start | bytes 196616 | tf_op jit(solution)/shard_map/ppermute | solution.py:17
  68.3 5.2 %collective-permute-start.17 = (bf16[256,128]{1,0:T(8,128)(2,1)S(1)}, bf16[256,128]{1,0:T(8,128)(2,1)S(1)}, u32[]{:S(2)}, u32[]{:S(2)}) collective-permute-start(bf16[256,128]{1,0:T(8,128)(2,1)S(1)} %get-tuple-element.101), channel_id=1, source_target_pairs={{0,6},{1,7},{2,4},{3,5},{4,2},{5,3},{6,0},{7,1},{8,14},{9,15},{10,... | collective-permute-start | bytes 196616 | tf_op jit(solution)/shard_map/ppermute | solution.py:17
  73.5 1.6 %collective-permute-start.18 = (bf16[1024,128]{1,0:T(8,128)(2,1)S(1)}, bf16[1024,128]{1,0:T(8,128)(2,1)S(1)}, u32[]{:S(2)}, u32[]{:S(2)}) collective-permute-start(bf16[1024,128]{1,0:T(8,128)(2,1)S(1)} %pad_maximum_fusion.4), channel_id=1, source_target_pairs={{0,1},{1,0},{2,3},{3,2},{4,5},{5,4},{6,7},{7,6},{8,9},{9,8},{10,11... | collective-permute-start | bytes 786440 | tf_op jit(solution)/shard_map/ppermute | solution.py:17

commit v2 on v1

--- a/solution.py
+++ b/solution.py
@@ -1,13 +1,22 @@
+import functools
 import math
 
 import jax
 import jax.numpy as jnp
 from jax import lax
+from jax.experimental import pallas as pl
+from jax.experimental.pallas import tpu as pltpu
 from jax.sharding import PartitionSpec as P
 
 SEGLEN = 128
 grid_width = 64
 image_side = 128.0
+CHUNK = 256
+LANES = (((1,), (1,)), ((), ()))
+COST_SCORE = 10.0
+COST_WEIGHT = 5.0
+COST_PLACE = 1.0
+COST_VOLUME = 10.0
 bf16 = jnp.bfloat16
 f32 = jnp.float32
 
@@ -81,7 +90,7 @@
     return jnp.stack([peak, total])
 
 
-def shards(images, references, shifts, owners, slot_rows, interpolation, regularizer):
+def reduced(images, references, shifts, owners, slot_rows, interpolation, regularizer):
     ori_count, img_count = lax.axis_size("ori"), lax.axis_size("img")
     ori, img = lax.axis_index("ori"), lax.axis_index("img")
     shift_count = shifts.shape[0]
@@ -176,6 +185,383 @@
     return (volume, resampled.reshape(sub_rows, coef))
 
 
+def iota(shape, axis):
+    return lax.broadcasted_iota(jnp.int32, shape, axis)
+
+
+def distance_of(place, ori_count):
+    half = ori_count // 2
+    return jnp.where(place < half, 2 * place, 2 * (place - half) + 1)
+
+
+def gather_pair(value):
+    near = jnp.stack([value] + [hop(value, "ori", k) for k in even_distances()], axis=0)
+    return near, hop(near, "ori", 1)
+
+
+def first_phases(shifts):
+    rows = jnp.pad(shifts, ((0, -shifts.shape[0] % 8), (0, 0)))
+    lane = jnp.arange(CHUNK, dtype=jnp.int32)
+    freq_x = (lane % grid_width).astype(f32)
+    freq_y = (lane // grid_width).astype(f32) - image_side / 2
+    unit = 2.0 * math.pi / image_side
+    angles = unit * (rows[:, 0:1] * freq_x[None, :] + rows[:, 1:2] * freq_y[None, :])
+    steps = unit * rows[:, 1:2] * jnp.full((1, CHUNK), float(CHUNK // grid_width), f32)
+    angles = jnp.stack([angles, steps])
+    return jnp.stack([jnp.cos(angles), jnp.sin(angles)])
+
+
+def turn(phases, now):
+    cosine, sine = now[0], now[1]
+    cos_step, sin_step = phases[0, 1], phases[1, 1]
+    now[0] = cosine * cos_step - sine * sin_step
+    now[1] = sine * cos_step + cosine * sin_step
+
+
+def place_images(near, far, first, order, out, row, group_rows):
+    shares = 2 * near.shape[0]
+    step = 16 * shares // group_rows
+    for q in range(out.shape[1] // SEGLEN // step):
+        rows = pl.ds(first + 16 * q, 16)
+        block = jnp.concatenate([near[:, rows, :], far[:, rows, :]], axis=0)
+        block = block.reshape(shares * 16, SEGLEN)
+        placed = jnp.dot(order, block, preferred_element_type=f32).astype(bf16)
+        for jj in range(step):
+            lanes = pl.ds((q * step + jj) * SEGLEN, SEGLEN)
+            out[row : row + group_rows, lanes] = placed[jj * group_rows : (jj + 1) * group_rows]
+
+
+def score_kernel(shift_count, near, far, order, references, phases, scores, own, now):
+    group_rows, coef = own.shape
+    half_len = coef // 2
+    place_images(near, far, 0, order[...], own, 0, group_rows)
+    now[0] = phases[0, 0]
+    now[1] = phases[1, 0]
+
+    def step(t, total):
+        re_lanes = pl.ds(pl.multiple_of(t * CHUNK, CHUNK), CHUNK)
+        im_lanes = pl.ds(pl.multiple_of(half_len + t * CHUNK, CHUNK), CHUNK)
+        real_part = references[:, re_lanes].astype(f32)
+        imag_part = references[:, im_lanes].astype(f32)
+        rotated_re, rotated_im = [], []
+        for s in range(shift_count):
+            c, d = now[0, s : s + 1, :], now[1, s : s + 1, :]
+            rotated_re.append((real_part * c - imag_part * d).astype(bf16))
+            rotated_im.append((real_part * d + imag_part * c).astype(bf16))
+        total += lax.dot_general(
+            jnp.concatenate(rotated_re, axis=0), own[:, re_lanes], LANES, preferred_element_type=f32
+        )
+        total += lax.dot_general(
+            jnp.concatenate(rotated_im, axis=0), own[:, im_lanes], LANES, preferred_element_type=f32
+        )
+        turn(phases, now)
+        return total
+
+    columns = shift_count * references.shape[0]
+    total = lax.fori_loop(
+        0, half_len // CHUNK, step, jnp.zeros((columns, group_rows), f32), unroll=2
+    )
+    scores[...] = jnp.swapaxes(total, 0, 1) * (2.0 / math.sqrt(coef))
+
+
+def weight_kernel(near, far, pick, messages):
+    half = near.shape[0]
+    parts = [near[p] for p in range(half)] + [far[p] for p in range(half)]
+    peak = jnp.max(parts[0], axis=1, keepdims=True)
+    for part in parts[1:]:
+        peak = jnp.maximum(peak, jnp.max(part, axis=1, keepdims=True))
+    exponents = [jnp.exp(part - peak) for part in parts]
+    total = sum(jnp.sum(part, axis=1, keepdims=True) for part in exponents)
+    weights = [(part / total).astype(bf16) for part in exponents]
+    picked = jnp.dot(
+        jnp.concatenate(weights[:half], axis=0), pick[0], preferred_element_type=f32
+    ) + jnp.dot(jnp.concatenate(weights[half:], axis=0), pick[1], preferred_element_type=f32)
+    for k in range(messages.shape[0]):
+        messages[k] = picked[:, k * SEGLEN : (k + 1) * SEGLEN].astype(bf16)
+
+
+def place_kernel(near, far, order, own, everything):
+    group_rows, coef = own.shape
+    everything[:group_rows, :] = own[...]
+    rows = group_rows * coef // SEGLEN // (2 * near.shape[0])
+    for k in range(1, everything.shape[0] // group_rows):
+        place_images(
+            near, far, (k - 1) * rows, order[...], everything, k * group_rows, group_rows
+        )
+
+
+def volume_kernel(shift_count, first, *refs):
+    (
+        *messages,
+        images,
+        phases,
+        arrange,
+        near,
+        far,
+        owner_ids,
+        volume,
+        resampled,
+        now,
+        raw,
+        segments,
+        chosen,
+        result,
+    ) = refs
+    img_count = len(messages)
+    half = near.shape[0]
+    shares = 2 * half
+    coef = images.shape[1]
+    tiles = coef // SEGLEN
+    half_len = coef // 2
+    group_rows = images.shape[0] // img_count
+    sub_rows = resampled.shape[0]
+    orients = shares * sub_rows
+    row_count = volume.shape[0]
+    reg_rows = row_count // SEGLEN
+    kernel_rows = pl.ds(first, SEGLEN)
+    fact_rows = pl.ds(first + SEGLEN, near.shape[1] - first - SEGLEN)
+    fact_count = near.shape[1] - first - SEGLEN
+
+    facts = jnp.concatenate([near[:, fact_rows, :], far[:, fact_rows, :]], axis=0).astype(f32)
+    facts = facts.reshape(shares * fact_count, SEGLEN)
+    upright = jnp.swapaxes(facts, 0, 1)
+
+    def column(share, fact):
+        place = share * fact_count + fact
+        return upright[:, place : place + 1]
+
+    stacked = jnp.concatenate(
+        [
+            jnp.concatenate(
+                [message[a * group_rows : (a + 1) * group_rows, :] for message in messages], axis=0
+            )
+            for a in range(half)
+        ],
+        axis=1,
+    )
+    weights = lax.dot_general(arrange[...], stacked, LANES, preferred_element_type=f32)
+    mass = jnp.sum(weights, axis=1, keepdims=True)
+    mass = sum(mass[s * orients : (s + 1) * orients] for s in range(shift_count))
+    weights = weights.astype(bf16)
+
+    slot_number = iota((row_count, SEGLEN), 0).astype(f32)
+    for o in range(orients):
+        place = o // sub_rows * fact_count + o % sub_rows
+        chosen[:, o * tiles : (o + 1) * tiles] = jnp.where(
+            slot_number == facts[place : place + 1, :], 1.0, 0.0
+        ).astype(bf16)
+
+    now[0] = phases[0, 0]
+    now[1] = phases[1, 0]
+
+    def step(t, carry):
+        re_lanes = pl.ds(pl.multiple_of(t * CHUNK, CHUNK), CHUNK)
+        im_lanes = pl.ds(pl.multiple_of(half_len + t * CHUNK, CHUNK), CHUNK)
+        summed_re = jnp.dot(weights, images[:, re_lanes], preferred_element_type=f32)
+        summed_im = jnp.dot(weights, images[:, im_lanes], preferred_element_type=f32)
+        total_re = jnp.zeros((orients, CHUNK), f32)
+        total_im = jnp.zeros((orients, CHUNK), f32)
+        for s in range(shift_count):
+            c, d = now[0, s : s + 1, :], now[1, s : s + 1, :]
+            part_re = summed_re[s * orients : (s + 1) * orients]
+            part_im = summed_im[s * orients : (s + 1) * orients]
+            total_re += part_re * c + part_im * d
+            total_im += part_im * c - part_re * d
+        turn(phases, now)
+        for h in range(CHUNK // SEGLEN):
+            j = t * (CHUNK // SEGLEN) + h
+            lanes = slice(h * SEGLEN, (h + 1) * SEGLEN)
+            raw[pl.ds(j, orients, stride=tiles), :] = total_re[:, lanes]
+            raw[pl.ds(half_len // SEGLEN + j, orients, stride=tiles), :] = total_im[:, lanes]
+        return carry
+
+    lax.fori_loop(0, half_len // CHUNK, step, 0, unroll=2)
+
+    lane = iota((tiles, SEGLEN), 1)
+    ids = [owner_ids[w].astype(bf16) for w in range(shares)]
+    lane_owner = sum(
+        jnp.where(lane % shares == w, owner_ids[w], 0) for w in range(shares)
+    ).astype(bf16)
+    zero = jnp.zeros((tiles, SEGLEN), bf16)
+    for o in range(orients):
+        share = o // sub_rows
+        rows = slice(o * tiles, (o + 1) * tiles)
+        part = raw[rows, :].astype(bf16)
+        owner = jnp.broadcast_to(column(share, sub_rows + o % sub_rows), (tiles, SEGLEN))
+        owner = owner.astype(bf16)
+        for w in range(shares):
+            segments[rows, w * SEGLEN : (w + 1) * SEGLEN] = jnp.where(owner == ids[w], part, zero)
+        own_mass = jnp.broadcast_to(mass[o : o + 1, :], (tiles, SEGLEN))
+        mass_hi = own_mass.astype(bf16)
+        mass_lo = (own_mass - mass_hi.astype(f32)).astype(bf16)
+        mass_part = jnp.where(lane < shares, mass_hi.astype(f32), mass_lo.astype(f32))
+        mass_part = jnp.where(lane < 2 * shares, mass_part, 0.0).astype(bf16)
+        segments[rows, shares * SEGLEN :] = jnp.where(owner == lane_owner, mass_part, zero)
+
+    inserted = jnp.dot(chosen[...], segments[...], preferred_element_type=f32)
+    tail = shares * SEGLEN
+    weight_sum = inserted[:, tail : tail + shares] + inserted[:, tail + shares : tail + 2 * shares]
+    back = []
+    for w in range(shares):
+        regularizer = jnp.concatenate(
+            [
+                column(w, 2 * sub_rows + h) + column(w, 2 * sub_rows + reg_rows + h)
+                for h in range(reg_rows)
+            ],
+            axis=0,
+        )
+        kernel = near[w, kernel_rows, :] if w < half else far[w - half, kernel_rows, :]
+        part = inserted[:, w * SEGLEN : (w + 1) * SEGLEN].astype(bf16)
+        mapped = jnp.dot(part, kernel, preferred_element_type=f32)
+        mapped = mapped / (weight_sum[:, w : w + 1] + regularizer)
+        if w == 0:
+            volume[...] = mapped
+        back.append(
+            lax.dot_general(
+                mapped.astype(bf16), kernel, LANES, preferred_element_type=f32
+            ).astype(bf16)
+        )
+    back = jnp.concatenate(back, axis=1)
+    slot_lane = iota((tiles, row_count), 1).astype(f32)
+    for o in range(sub_rows):
+        own_slots = jnp.where(slot_lane == column(0, o), 1.0, 0.0).astype(bf16)
+        taken = jnp.dot(own_slots, back, preferred_element_type=f32)
+        owner = jnp.broadcast_to(column(0, sub_rows + o), (tiles, SEGLEN))
+        total = jnp.zeros((tiles, SEGLEN), f32)
+        for w in range(shares):
+            total += jnp.where(
+                owner == owner_ids[w].astype(f32), taken[:, w * SEGLEN : (w + 1) * SEGLEN], 0.0
+            )
+        result[o * tiles : (o + 1) * tiles, :] = total
+    for j in range(tiles):
+        resampled[:, j * SEGLEN : (j + 1) * SEGLEN] = result[pl.ds(j, sub_rows, stride=tiles), :]
+
+
+def call(kernel, inputs, outputs, scratch=(), cost=1.0, small=()):
+    inside = pl.BlockSpec(memory_space=pltpu.VMEM)
+    scalars = pl.BlockSpec(memory_space=pltpu.SMEM)
+    return pl.pallas_call(
+        kernel,
+        out_shape=[jax.ShapeDtypeStruct(shape, dtype) for shape, dtype in outputs],
+        in_specs=[inside] * len(inputs) + [scalars] * len(small),
+        out_specs=[inside] * len(outputs),
+        scratch_shapes=list(scratch),
+        compiler_params=pltpu.CompilerParams(vmem_limit_bytes=40 * 2**20),
+        cost_estimate=pl.CostEstimate(
+            flops=int(cost * 1e9), bytes_accessed=0, transcendentals=0
+        ),
+    )(*inputs, *small)
+
+
+def whole_plane(images, references, shifts, owners, slot_rows, interpolation, regularizer):
+    ori_count, img_count = lax.axis_size("ori"), lax.axis_size("img")
+    ori, img = lax.axis_index("ori"), lax.axis_index("img")
+    shift_count = shifts.shape[0]
+    own_images, coef = images.shape
+    tiles = coef // SEGLEN
+    half = ori_count // 2
+    row_count = regularizer.shape[0]
+    orient_count = references.shape[0]
+    sub_rows = orient_count // img_count
+    group_rows = own_images * ori_count
+    columns = shift_count * orient_count
+    orients = ori_count * sub_rows
+
+    piece = images.reshape(own_images, tiles, SEGLEN).transpose(1, 0, 2).reshape(-1, SEGLEN)
+    near, far = gather_pair(piece)
+
+    others = [hop(piece, "img", k) for k in range(1, img_count)]
+    reg_rows = regularizer.reshape(-1, SEGLEN)
+    reg_hi = reg_rows.astype(bf16)
+    facts = jnp.concatenate(
+        [
+            slot_rows.reshape(-1, SEGLEN).astype(bf16),
+            owners.reshape(-1, SEGLEN).astype(bf16),
+            reg_hi,
+            (reg_rows - reg_hi.astype(f32)).astype(bf16),
+        ],
+        axis=0,
+    )
+    facts = jnp.pad(facts, ((0, -facts.shape[0] % 16), (0, 0)))
+    parcel = jnp.concatenate(others + [interpolation.astype(bf16), facts], axis=0)
+
+    place = jnp.arange(ori_count * 16, dtype=jnp.int32)
+    step = 16 // own_images
+    image = (ori ^ distance_of(place // 16, ori_count)) * own_images + place % own_images
+    out_row = place % 16 // own_images * group_rows + image
+    order = (jnp.arange(step * group_rows)[:, None] == out_row[None, :]).astype(bf16)
+    phases = first_phases(shifts)
+    turning = pltpu.VMEM(phases.shape[1:], f32)
+
+    scores, own = call(
+        functools.partial(score_kernel, shift_count),
+        (near, far, order, references, phases),
+        (((group_rows, columns), f32), ((group_rows, coef), bf16)),
+        scratch=(turning,),
+        cost=COST_SCORE,
+    )
+    scores_near, scores_far = gather_pair(scores)
+
+    column = jnp.arange(columns, dtype=jnp.int32)
+    orient = column % orient_count
+    lane = (orient // sub_rows ^ img) * SEGLEN + column // orient_count * sub_rows + orient % sub_rows
+    pick = jnp.stack(
+        [
+            (jnp.arange(img_count * SEGLEN)[None, :] == (lane + h * (SEGLEN // 2))[:, None]).astype(bf16)
+            for h in range(2)
+        ]
+    )
+    (messages,) = call(
+        weight_kernel,
+        (scores_near, scores_far, pick),
+        (((img_count, half * group_rows, SEGLEN), bf16),),
+        cost=COST_WEIGHT,
+    )
+    arrived = [messages[0]] + [hop(messages[k], "img", k) for k in range(1, img_count)]
+
+    parcel_near, parcel_far = gather_pair(parcel)
+    (everything,) = call(
+        place_kernel,
+        (parcel_near, parcel_far, order, own),
+        (((img_count * group_rows, coef), bf16),),
+        cost=COST_PLACE,
+    )
+
+    row = jnp.arange(shift_count * orients, dtype=jnp.int32)
+    share = row % orients // sub_rows
+    source = (
+        share % half * SEGLEN
+        + share // half * (SEGLEN // 2)
+        + row // orients * sub_rows
+        + row % sub_rows
+    )
+    arrange = (source[:, None] == jnp.arange(half * SEGLEN)[None, :]).astype(bf16)
+    owner_ids = ori ^ distance_of(jnp.arange(ori_count, dtype=jnp.int32), ori_count)
+    volume, resampled = call(
+        functools.partial(volume_kernel, shift_count, (img_count - 1) * piece.shape[0]),
+        (*arrived, everything, phases, arrange, parcel_near, parcel_far),
+        (((row_count, SEGLEN), f32), ((sub_rows, coef), f32)),
+        scratch=(
+            turning,
+            pltpu.VMEM((orients * tiles, SEGLEN), f32),
+            pltpu.VMEM((orients * tiles, (ori_count + 1) * SEGLEN), bf16),
+            pltpu.VMEM((row_count, orients * tiles), bf16),
+            pltpu.VMEM((sub_rows * tiles, SEGLEN), f32),
+        ),
+        small=(owner_ids,),
+        cost=COST_VOLUME,
+    )
+    return (volume, resampled)
+
+
+def shards(images, references, shifts, owners, slot_rows, interpolation, regularizer):
+    arguments = (images, references, shifts, owners, slot_rows, interpolation, regularizer)
+    whole_bytes = images.size * 2 * lax.axis_size("img") * lax.axis_size("ori")
+    if whole_bytes <= 4 * 2**20:
+        return whole_plane(*arguments)
+    return reduced(*arguments)
+
+
 def solution(mesh):
     in_specs = (
         P(("img", "ori"), None),

time: 77.5 us -> 63 us (0.81)
  Pallas kernels: 0 us -> 19.5 us
  matrix products: 13.1 us -> 0 us
  waiting for transfers between devices: 25.3 us -> 15.9 us
  local copies, waits for them, and re-layouts: 6.56 us -> 0.12 us
  other arithmetic: 11.1 us -> 5.42 us
  starting transfers between devices: 20.1 us -> 21 us
    pallas_call x0 -> x4, Pallas kernels: none -> 19.5 us  [call(): pl.pallas_call(kernel, out_shape=[jax.ShapeDtypeStruct(shape, dtype) for...]
    dot_general x29 -> x0, matrix products: 13.1 us -> none  [the longest x12 6.21 us: shards(): lax.dot_general(group_images, rotated, (((1,), (1,)), ((), ())), preferre...]
    ppermute x19 -> x18, waiting for transfers between devices: 25.3 us -> 15.9 us  [hop(): return lax.ppermute(value, axis, pairs)]
    another operation x10 -> x6, other arithmetic: 4.68 us -> 1.11 us  [the longest x3 1 us: gather_pair(): jnp.stack([value] + [hop(value, 'ori', k) for k in even_distances()], axi...]
    add x7 -> x3, other arithmetic: 2.93 us -> 0.04 us  [the longest x1 0.02 us: whole_plane(): share % half * SEGLEN + share // half * (SEGLEN // 2)]
    cos x1, other arithmetic: 1.94 us -> 0.13 us  [first_phases(): return jnp.stack([jnp.cos(angles), jnp.sin(angles)])]
    convert_element_type x8 -> x6, other arithmetic: 0.57 us -> 2.22 us  [the longest x1 0.7 us: whole_plane(): owners.reshape(-1, SEGLEN).astype(bf16)]
    unnamed x45 -> x5, local copies, waits for them, and re-layouts: 1.57 us -> 0.04 us
  transfers between devices with their start and end apart: 19 -> 18, of which waited for: 15 -> 10; matrix products, arithmetic and copies ran while one was open for 11% -> 9% of each run, Pallas kernels for 0% -> 9%
where the time goes in v2:
time: 63 us; the launch traced here: 62.7 us
  starting transfers between devices  21 us (33%)
  Pallas kernels  19.5 us (31%)
  waiting for transfers between devices  15.9 us (25%)
  other arithmetic  5.42 us (9%)
  between operations  0.81 us (1%)
    ppermute x18, starting transfers between devices, hop(): return lax.ppermute(value, axis, pairs)  21 us
    pallas_call x4, Pallas kernels, call(): pl.pallas_call(kernel, out_shape=[jax.ShapeDtypeStruct(shape, dtype) for...  19.5 us
    ppermute x18, waiting for transfers between devices, hop(): return lax.ppermute(value, axis, pairs)  15.9 us
  transfers between devices with their start and end apart: 18, of which 10 were waited for; matrix products, arithmetic and copies ran while one was open for 9% of the time, Pallas kernels for 9%

profile of v2, /device:TPU:0, one launch (start us, length us, event | category | flops | bytes accessed | tf_op | source)
XLA Modules:
  0.0 62.7 jit_solution(949890738397242974)
XLA Ops:
  0.6 3.1 %collective-permute-start.11 = (bf16[256,128]{1,0:T(8,128)(2,1)}, bf16[256,128]{1,0:T(8,128)(2,1)S(1)}, u32[]{:S(2)}, u32[]{:S(2)}) collective-permute-start(bf16[256,128]{1,0:T(8,128)(2,1)} %bitcast.48), channel_id=1, source_target_pairs={{0,8},{8,0},{16,24},{24,16},{1,9},{9,1},{17,25},{25,17},{2,10},{10... | collective-permute-start | bytes 196616 | tf_op jit(solution)/shard_map/ppermute | solution.py:26
  3.7 2.6 %collective-permute-start.12 = (bf16[256,128]{1,0:T(8,128)(2,1)}, bf16[256,128]{1,0:T(8,128)(2,1)S(1)}, u32[]{:S(2)}, u32[]{:S(2)}) collective-permute-start(bf16[256,128]{1,0:T(8,128)(2,1)} %bitcast.49), channel_id=1, source_target_pairs={{0,16},{8,24},{16,0},{24,8},{1,17},{9,25},{17,1},{25,9},{2,18},{10... | collective-permute-start | bytes 196616 | tf_op jit(solution)/shard_map/ppermute | solution.py:26
  6.3 0.0 collective-permute-start.13
  6.3 1.7 %collective-permute-start = (bf16[256,128]{1,0:T(8,128)(2,1)}, bf16[256,128]{1,0:T(8,128)(2,1)S(1)}, u32[]{:S(2)}, u32[]{:S(2)}) collective-permute-start(bf16[256,128]{1,0:T(8,128)(2,1)} %bitcast.51), channel_id=1, source_target_pairs={{0,2},{1,3},{2,0},{3,1},{4,6},{5,7},{6,4},{7,5},{8,10},{9,11},{10,... | collective-permute-start | bytes 196616 | tf_op jit(solution)/shard_map/ppermute | solution.py:26
  8.0 1.5 %collective-permute-start.1 = (bf16[256,128]{1,0:T(8,128)(2,1)}, bf16[256,128]{1,0:T(8,128)(2,1)S(1)}, u32[]{:S(2)}, u32[]{:S(2)}) collective-permute-start(bf16[256,128]{1,0:T(8,128)(2,1)} %bitcast.52), channel_id=1, source_target_pairs={{0,4},{1,5},{2,6},{3,7},{4,0},{5,1},{6,2},{7,3},{8,12},{9,13},{10,... | collective-permute-start | bytes 196616 | tf_op jit(solution)/shard_map/ppermute | solution.py:26
  9.6 0.7 %fusion.39 = (bf16[2,128]{1,0:T(2,128)(2,1)S(1)}, bf16[2,128]{1,0:T(2,128)(2,1)S(1)}) fusion(f32[256]{0:T(256)} %param.13), kind=kLoop, calls=%fused_computation.101 | loop fusion | flops 1024 | bytes 2048 | tf_op jit(solution)/shard_map/convert_element_type | solution.py:481
  10.3 0.7 %convert_bitcast_fusion = bf16[4,128]{1,0:T(4,128)(2,1)S(1)} fusion(s32[512]{0:T(512)} %param.11), kind=kLoop, calls=%fused_computation.104 | loop fusion | flops 512 | bytes 3072 | tf_op jit(solution)/shard_map/convert_element_type | solution.py:478
  11.0 0.8 %fusion.43 = (f32[16]{0:T(128)S(1)}, f32[16]{0:T(128)S(1)}, f32[16]{0:T(128)S(1)}) fusion(f32[12,2]{0,1:T(2,128)} %param.9), kind=kLoop, calls=%fused_computation.113 | loop fusion | flops 16 | bytes 288 | tf_op jit(solution)/shard_map/mul | solution.py:208
  11.8 0.1 iota_compare_fusion.1
  11.9 0.1 iota_compare_fusion.2
  12.1 0.1 fusion.refs_6_
  12.2 0.1 multiply_bitcast_fusion
  12.3 0.7 %convert_reduce_fusion = bf16[512]{0:T(512)(128)(2,1)S(1)} fusion(s32[512,1]{0,1:T(1,128)} %param.10), kind=kLoop, calls=%fused_computation.64 | loop fusion | flops 512 | bytes 3072 | tf_op jit(solution)/shard_map/convert_element_type | solution.py:479
  13.0 0.0 collective-permute-done.11
  13.0 0.3 collective-permute-start.2
  13.3 0.0 collective-permute-done.12
  13.4 0.9 %convert_dynamic-update-slice_fusion = bf16[912,128]{1,0:T(8,128)(2,1)S(1)} fusion(bf16[912,128]{1,0:T(8,128)(2,1)S(1)} %constant_dynamic-update-slice_fusion.1, f32[128,128]{1,0:T(8,128)} %param.12), kind=kLoop, calls=%fused_computation.14 | loop fusion | flops 16384 | bytes 98304
  14.2 1.8 %collective-permute-start.14 = (bf16[912,128]{1,0:T(8,128)(2,1)S(1)}, bf16[912,128]{1,0:T(8,128)(2,1)S(1)}, u32[]{:S(2)}, u32[]{:S(2)}) collective-permute-start(bf16[912,128]{1,0:T(8,128)(2,1)S(1)} %constant_dynamic-update-slice_fusion), channel_id=1, source_target_pairs={{0,2},{1,3},{2,0},{3,1},{4,6},{5,7},{6,4},{7,5},{8,10},{9,11},{10,... | collective-permute-start | bytes 700424 | tf_op jit(solution)/shard_map/ppermute | solution.py:26
  16.0 1.5 %collective-permute-start.15 = (bf16[912,128]{1,0:T(8,128)(2,1)S(1)}, bf16[912,128]{1,0:T(8,128)(2,1)S(1)}, u32[]{:S(2)}, u32[]{:S(2)}) collective-permute-start(bf16[912,128]{1,0:T(8,128)(2,1)S(1)} %constant_dynamic-update-slice_fusion), channel_id=1, source_target_pairs={{0,4},{1,5},{2,6},{3,7},{4,0},{5,1},{6,2},{7,3},{8,12},{9,13},{10,... | collective-permute-start | bytes 700424 | tf_op jit(solution)/shard_map/ppermute | solution.py:26
  17.5 0.3 collective-permute-start.16
  17.8 1.4 %collective-permute-done.2 = bf16[256,128]{1,0:T(8,128)(2,1)S(1)} collective-permute-done((bf16[256,128]{1,0:T(8,128)(2,1)}, bf16[256,128]{1,0:T(8,128)(2,1)S(1)}, u32[]{:S(2)}, u32[]{:S(2)}) %collective-permute-start.2) | collective-permute-done | bytes 65568 | tf_op jit(solution)/shard_map/ppermute | solution.py:26
  19.2 0.9 %pad_maximum_fusion.1.near = bf16[4,256,128]{2,1,0:T(8,128)(2,1)S(1)} fusion(bf16[1,256,128]{2,1,0:T(8,128)(2,1)S(1)} %bitcast.57, bf16[1,256,128]{2,1,0:T(8,128)(2,1)S(1)} %bitcast.56, bf16[1,256,128]{2,1,0:T(8,128)(2,1)S(1)} %bitcast.55, bf16[1,256,128]{2,1,0:T(8,128)(2,1)} %bitcast.54), kind=kLoop, calls=%fused_computation.6 | loop fusion | flops 393216 | bytes 524288 | tf_op jit(solution)/shard_map/stack | solution.py:198
  20.1 0.1 collective-permute-start.3
  20.1 0.1 stack.68
  20.2 0.1 fusion.3
  20.4 2.9 %collective-permute-done.14 = bf16[912,128]{1,0:T(8,128)(2,1)S(1)} collective-permute-done((bf16[912,128]{1,0:T(8,128)(2,1)S(1)}, bf16[912,128]{1,0:T(8,128)(2,1)S(1)}, u32[]{:S(2)}, u32[]{:S(2)}) %collective-permute-start.14) | collective-permute-done | bytes 233504 | tf_op jit(solution)/shard_map/ppermute | solution.py:26
  23.2 4.0 %collective-permute-done.15 = bf16[912,128]{1,0:T(8,128)(2,1)S(1)} collective-permute-done((bf16[912,128]{1,0:T(8,128)(2,1)S(1)}, bf16[912,128]{1,0:T(8,128)(2,1)S(1)}, u32[]{:S(2)}, u32[]{:S(2)}) %collective-permute-start.15) | collective-permute-done | bytes 233504 | tf_op jit(solution)/shard_map/ppermute | solution.py:26
  27.3 0.1 pad_maximum_fusion.near.refs_7_
  27.4 0.1 collective-permute-start.17
  27.5 4.8 %shard_map.86 = (f32[16,192]{1,0:T(8,128)S(1)}, bf16[16,16384]{1,0:T(8,128)(2,1)S(1)}) custom-call(bf16[4,256,128]{2,1,0:T(8,128)(2,1)S(1)} %pad_maximum_fusion.1.near, bf16[4,256,128]{2,1,0:T(8,128)(2,1)S(1)} %collective-permute-done.3.far, bf16[128,128]{1,0:T(8,128)(2,1)S(1)} %fusion.1.order, bf16[16,16384]{1,0:T(8,128)(2,1)S(1)} %copy-done, ...), custom_call_target="tpu_custom_call" | custom-call | flops 10000000000 | tf_op jit(solution)/shard_map/pallas_call | solution.py:443
  32.3 1.3 %collective-permute-start.4 = (f32[16,192]{1,0:T(8,128)S(1)}, f32[16,192]{1,0:T(8,128)S(1)}, u32[]{:S(2)}, u32[]{:S(2)}) collective-permute-start(f32[16,192]{1,0:T(8,128)S(1)} %get-tuple-element.4), channel_id=1, source_target_pairs={{0,2},{1,3},{2,0},{3,1},{4,6},{5,7},{6,4},{7,5},{8,10},{9,11},{10,... | collective-permute-start | bytes 36872 | tf_op jit(solution)/shard_map/ppermute | solution.py:26
  33.5 0.8 %collective-permute-start.5 = (f32[16,192]{1,0:T(8,128)S(1)}, f32[16,192]{1,0:T(8,128)S(1)}, u32[]{:S(2)}, u32[]{:S(2)}) collective-permute-start(f32[16,192]{1,0:T(8,128)S(1)} %get-tuple-element.4), channel_id=1, source_target_pairs={{0,4},{1,5},{2,6},{3,7},{4,0},{5,1},{6,2},{7,3},{8,12},{9,13},{10,... | collective-permute-start | bytes 36872 | tf_op jit(solution)/shard_map/ppermute | solution.py:26
  34.3 1.5 %collective-permute-start.6 = (f32[16,192]{1,0:T(8,128)S(1)}, f32[16,192]{1,0:T(8,128)S(1)}, u32[]{:S(2)}, u32[]{:S(2)}) collective-permute-start(f32[16,192]{1,0:T(8,128)S(1)} %get-tuple-element.4), channel_id=1, source_target_pairs={{0,6},{1,7},{2,4},{3,5},{4,2},{5,3},{6,0},{7,1},{8,14},{9,15},{10,... | collective-permute-start | bytes 36872 | tf_op jit(solution)/shard_map/ppermute | solution.py:26
  35.8 0.2 collective-permute-done.4
  36.0 1.2 %collective-permute-done.5 = f32[16,192]{1,0:T(8,128)S(1)} collective-permute-done((f32[16,192]{1,0:T(8,128)S(1)}, f32[16,192]{1,0:T(8,128)S(1)}, u32[]{:S(2)}, u32[]{:S(2)}) %collective-permute-start.5) | collective-permute-done | bytes 12320 | tf_op jit(solution)/shard_map/ppermute | solution.py:26
  37.3 1.7 %collective-permute-done.6 = f32[16,192]{1,0:T(8,128)S(1)} collective-permute-done((f32[16,192]{1,0:T(8,128)S(1)}, f32[16,192]{1,0:T(8,128)S(1)}, u32[]{:S(2)}, u32[]{:S(2)}) %collective-permute-start.6) | collective-permute-done | bytes 12320 | tf_op jit(solution)/shard_map/ppermute | solution.py:26
  39.0 0.1 collective-permute-start.7
  39.1 1.2 %collective-permute-done.7.far = f32[4,16,192]{2,1,0:T(8,128)S(1)} collective-permute-done((f32[4,16,192]{2,1,0:T(8,128)S(1)}, f32[4,16,192]{2,1,0:T(8,128)S(1)}, u32[]{:S(2)}, u32[]{:S(2)}) %collective-permute-start.7) | collective-permute-done | bytes 49184 | tf_op jit(solution)/shard_map/ppermute | solution.py:26
  40.3 0.4 shard_map.87
  40.7 3.6 %collective-permute-start.10 = (bf16[64,128]{1,0:T(8,128)(2,1)S(1)}, bf16[64,128]{1,0:T(8,128)(2,1)S(1)}, u32[]{:S(2)}, u32[]{:S(2)}) collective-permute-start(bf16[64,128]{1,0:T(8,128)(2,1)S(1)} %get-tuple-element.8), channel_id=1, source_target_pairs={{0,24},{8,16},{16,8},{24,0},{1,25},{9,17},{17,9},{25,1},{2,26},{10... | collective-permute-start | bytes 49160 | tf_op jit(solution)/shard_map/ppermute | solution.py:26
  44.3 0.0 collective-permute-start.8
  44.3 0.8 %collective-permute-start.9 = (bf16[64,128]{1,0:T(8,128)(2,1)S(1)}, bf16[64,128]{1,0:T(8,128)(2,1)S(1)}, u32[]{:S(2)}, u32[]{:S(2)}) collective-permute-start(bf16[64,128]{1,0:T(8,128)(2,1)S(1)} %get-tuple-element.9), channel_id=1, source_target_pairs={{0,16},{8,24},{16,0},{24,8},{1,17},{9,25},{17,1},{25,9},{2,18},{10... | collective-permute-start | bytes 49160 | tf_op jit(solution)/shard_map/ppermute | solution.py:26
  45.1 0.0 collective-permute-done.17.far.refs_8_
  45.1 0.6 shard_map.88.refs_4_
  45.7 0.5 collective-permute-done.10.refs_3_
  46.3 1.8 %collective-permute-done.8.refs_1_ = bf16[64,128]{1,0:T(8,128)(2,1)S(1)} collective-permute-done((bf16[64,128]{1,0:T(8,128)(2,1)S(1)}, bf16[64,128]{1,0:T(8,128)(2,1)S(1)}, u32[]{:S(2)}, u32[]{:S(2)}) %collective-permute-start.8) | collective-permute-done | bytes 16416 | tf_op jit(solution)/shard_map/ppermute | solution.py:26
  48.0 0.9 %collective-permute-done.9.refs_2_ = bf16[64,128]{1,0:T(8,128)(2,1)S(1)} collective-permute-done((bf16[64,128]{1,0:T(8,128)(2,1)S(1)}, bf16[64,128]{1,0:T(8,128)(2,1)S(1)}, u32[]{:S(2)}, u32[]{:S(2)}) %collective-permute-start.9) | collective-permute-done | bytes 16416 | tf_op jit(solution)/shard_map/ppermute | solution.py:26
  49.0 13.7 %shard_map.89 = (f32[256,128]{1,0:T(8,128)}, f32[4,16384]{1,0:T(4,128)}) custom-call(bf16[64,128]{1,0:T(8,128)(2,1)S(1)} %get-tuple-element.11.refs_0_, bf16[64,128]{1,0:T(8,128)(2,1)S(1)} %collective-permute-done.8.refs_1_, bf16[64,128]{1,0:T(8,128)(2,1)S(1)} %collective-permute-done.9.refs_2_, bf16[64,128]{1,0:T(8,128)(2,1)S(1)} %collective-permute-done.10.refs_3_, ...), custom_call_target="tpu_custom_call" | custom-call | flops 10000000000 | tf_op jit(solution)/shard_map/pallas_call | solution.py:443
  (22 shorter events, 0.2 us)
Async XLA Ops:
  0.6 26.8 %copy-start = (bf16[16,16384]{1,0:T(8,128)(2,1)S(1)}, bf16[16,16384]{1,0:T(8,128)(2,1)}, u32[]{:S(2)}) copy-start(bf16[16,16384]{1,0:T(8,128)(2,1)} %references.1) | copy-start | bytes 1572868
  0.6 12.3 %collective-permute-start.11 = (bf16[256,128]{1,0:T(8,128)(2,1)}, bf16[256,128]{1,0:T(8,128)(2,1)S(1)}, u32[]{:S(2)}, u32[]{:S(2)}) collective-permute-start(bf16[256,128]{1,0:T(8,128)(2,1)} %bitcast.48), channel_id=1, source_target_pairs={{0,8},{8,0},{16,24},{24,16},{1,9},{9,1},{17,25},{25,17},{2,10},{10... | collective-permute-start | bytes 196616 | tf_op jit(solution)/shard_map/ppermute | solution.py:26
  3.7 9.6 %collective-permute-start.12 = (bf16[256,128]{1,0:T(8,128)(2,1)}, bf16[256,128]{1,0:T(8,128)(2,1)S(1)}, u32[]{:S(2)}, u32[]{:S(2)}) collective-permute-start(bf16[256,128]{1,0:T(8,128)(2,1)} %bitcast.49), channel_id=1, source_target_pairs={{0,16},{8,24},{16,0},{24,8},{1,17},{9,25},{17,1},{25,9},{2,18},{10... | collective-permute-start | bytes 196616 | tf_op jit(solution)/shard_map/ppermute | solution.py:26
  6.3 7.0 %collective-permute-start.13 = (bf16[256,128]{1,0:T(8,128)(2,1)}, bf16[256,128]{1,0:T(8,128)(2,1)S(1)}, u32[]{:S(2)}, u32[]{:S(2)}) collective-permute-start(bf16[256,128]{1,0:T(8,128)(2,1)} %bitcast.50), channel_id=1, source_target_pairs={{0,24},{8,16},{16,8},{24,0},{1,25},{9,17},{17,9},{25,1},{2,26},{10... | collective-permute-start | bytes 196616 | tf_op jit(solution)/shard_map/ppermute | solution.py:26
  6.3 11.2 %collective-permute-start = (bf16[256,128]{1,0:T(8,128)(2,1)}, bf16[256,128]{1,0:T(8,128)(2,1)S(1)}, u32[]{:S(2)}, u32[]{:S(2)}) collective-permute-start(bf16[256,128]{1,0:T(8,128)(2,1)} %bitcast.51), channel_id=1, source_target_pairs={{0,2},{1,3},{2,0},{3,1},{4,6},{5,7},{6,4},{7,5},{8,10},{9,11},{10,... | collective-permute-start | bytes 196616 | tf_op jit(solution)/shard_map/ppermute | solution.py:26
  8.0 9.8 %collective-permute-start.1 = (bf16[256,128]{1,0:T(8,128)(2,1)}, bf16[256,128]{1,0:T(8,128)(2,1)S(1)}, u32[]{:S(2)}, u32[]{:S(2)}) collective-permute-start(bf16[256,128]{1,0:T(8,128)(2,1)} %bitcast.52), channel_id=1, source_target_pairs={{0,4},{1,5},{2,6},{3,7},{4,0},{5,1},{6,2},{7,3},{8,12},{9,13},{10,... | collective-permute-start | bytes 196616 | tf_op jit(solution)/shard_map/ppermute | solution.py:26
  13.0 6.2 %collective-permute-start.2 = (bf16[256,128]{1,0:T(8,128)(2,1)}, bf16[256,128]{1,0:T(8,128)(2,1)S(1)}, u32[]{:S(2)}, u32[]{:S(2)}) collective-permute-start(bf16[256,128]{1,0:T(8,128)(2,1)} %bitcast.53), channel_id=1, source_target_pairs={{0,6},{1,7},{2,4},{3,5},{4,2},{5,3},{6,0},{7,1},{8,14},{9,15},{10,... | collective-permute-start | bytes 196616 | tf_op jit(solution)/shard_map/ppermute | solution.py:26
  14.2 9.0 %collective-permute-start.14 = (bf16[912,128]{1,0:T(8,128)(2,1)S(1)}, bf16[912,128]{1,0:T(8,128)(2,1)S(1)}, u32[]{:S(2)}, u32[]{:S(2)}) collective-permute-start(bf16[912,128]{1,0:T(8,128)(2,1)S(1)} %constant_dynamic-update-slice_fusion), channel_id=1, source_target_pairs={{0,2},{1,3},{2,0},{3,1},{4,6},{5,7},{6,4},{7,5},{8,10},{9,11},{10,... | collective-permute-start | bytes 700424 | tf_op jit(solution)/shard_map/ppermute | solution.py:26
  16.0 11.2 %collective-permute-start.15 = (bf16[912,128]{1,0:T(8,128)(2,1)S(1)}, bf16[912,128]{1,0:T(8,128)(2,1)S(1)}, u32[]{:S(2)}, u32[]{:S(2)}) collective-permute-start(bf16[912,128]{1,0:T(8,128)(2,1)S(1)} %constant_dynamic-update-slice_fusion), channel_id=1, source_target_pairs={{0,4},{1,5},{2,6},{3,7},{4,0},{5,1},{6,2},{7,3},{8,12},{9,13},{10,... | collective-permute-start | bytes 700424 | tf_op jit(solution)/shard_map/ppermute | solution.py:26
  17.5 9.7 %collective-permute-start.16 = (bf16[912,128]{1,0:T(8,128)(2,1)S(1)}, bf16[912,128]{1,0:T(8,128)(2,1)S(1)}, u32[]{:S(2)}, u32[]{:S(2)}) collective-permute-start(bf16[912,128]{1,0:T(8,128)(2,1)S(1)} %constant_dynamic-update-slice_fusion), channel_id=1, source_target_pairs={{0,6},{1,7},{2,4},{3,5},{4,2},{5,3},{6,0},{7,1},{8,14},{9,15},{10,... | collective-permute-start | bytes 700424 | tf_op jit(solution)/shard_map/ppermute | solution.py:26
  20.1 7.4 %collective-permute-start.3 = (bf16[4,256,128]{2,1,0:T(8,128)(2,1)S(1)}, bf16[4,256,128]{2,1,0:T(8,128)(2,1)S(1)}, u32[]{:S(2)}, u32[]{:S(2)}) collective-permute-start(bf16[4,256,128]{2,1,0:T(8,128)(2,1)S(1)} %pad_maximum_fusion.1.near), channel_id=1, source_target_pairs={{0,1},{1,0},{2,3},{3,2},{4,5},{5,4},{6,7},{7,6},{8,9},{9,8},{10,11... | collective-permute-start | bytes 786440 | tf_op jit(solution)/shard_map/ppermute | solution.py:26
  27.4 17.8 %collective-permute-start.17 = (bf16[4,912,128]{2,1,0:T(8,128)(2,1)S(1)}, bf16[4,912,128]{2,1,0:T(8,128)(2,1)S(1)}, u32[]{:S(2)}, u32[]{:S(2)}) collective-permute-start(bf16[4,912,128]{2,1,0:T(8,128)(2,1)S(1)} %pad_maximum_fusion.near.refs_7_), channel_id=1, source_target_pairs={{0,1},{1,0},{2,3},{3,2},{4,5},{5,4},{6,7},{7,6},{8,9},{9,8},{10,11... | collective-permute-start | bytes 2801672 | tf_op jit(solution)/shard_map/ppermute | solution.py:26
  32.3 3.8 %collective-permute-start.4 = (f32[16,192]{1,0:T(8,128)S(1)}, f32[16,192]{1,0:T(8,128)S(1)}, u32[]{:S(2)}, u32[]{:S(2)}) collective-permute-start(f32[16,192]{1,0:T(8,128)S(1)} %get-tuple-element.4), channel_id=1, source_target_pairs={{0,2},{1,3},{2,0},{3,1},{4,6},{5,7},{6,4},{7,5},{8,10},{9,11},{10,... | collective-permute-start | bytes 36872 | tf_op jit(solution)/shard_map/ppermute | solution.py:26
  33.5 3.7 %collective-permute-start.5 = (f32[16,192]{1,0:T(8,128)S(1)}, f32[16,192]{1,0:T(8,128)S(1)}, u32[]{:S(2)}, u32[]{:S(2)}) collective-permute-start(f32[16,192]{1,0:T(8,128)S(1)} %get-tuple-element.4), channel_id=1, source_target_pairs={{0,4},{1,5},{2,6},{3,7},{4,0},{5,1},{6,2},{7,3},{8,12},{9,13},{10,... | collective-permute-start | bytes 36872 | tf_op jit(solution)/shard_map/ppermute | solution.py:26
  34.3 4.6 %collective-permute-start.6 = (f32[16,192]{1,0:T(8,128)S(1)}, f32[16,192]{1,0:T(8,128)S(1)}, u32[]{:S(2)}, u32[]{:S(2)}) collective-permute-start(f32[16,192]{1,0:T(8,128)S(1)} %get-tuple-element.4), channel_id=1, source_target_pairs={{0,6},{1,7},{2,4},{3,5},{4,2},{5,3},{6,0},{7,1},{8,14},{9,15},{10,... | collective-permute-start | bytes 36872 | tf_op jit(solution)/shard_map/ppermute | solution.py:26
  39.0 1.3 %collective-permute-start.7 = (f32[4,16,192]{2,1,0:T(8,128)S(1)}, f32[4,16,192]{2,1,0:T(8,128)S(1)}, u32[]{:S(2)}, u32[]{:S(2)}) collective-permute-start(f32[4,16,192]{2,1,0:T(8,128)S(1)} %pad_maximum_fusion.3.near), channel_id=1, source_target_pairs={{0,1},{1,0},{2,3},{3,2},{4,5},{5,4},{6,7},{7,6},{8,9},{9,8},{10,11... | collective-permute-start | bytes 147464 | tf_op jit(solution)/shard_map/ppermute | solution.py:26
  40.7 5.6 %collective-permute-start.10 = (bf16[64,128]{1,0:T(8,128)(2,1)S(1)}, bf16[64,128]{1,0:T(8,128)(2,1)S(1)}, u32[]{:S(2)}, u32[]{:S(2)}) collective-permute-start(bf16[64,128]{1,0:T(8,128)(2,1)S(1)} %get-tuple-element.8), channel_id=1, source_target_pairs={{0,24},{8,16},{16,8},{24,0},{1,25},{9,17},{17,9},{25,1},{2,26},{10... | collective-permute-start | bytes 49160 | tf_op jit(solution)/shard_map/ppermute | solution.py:26
  44.3 3.7 %collective-permute-start.8 = (bf16[64,128]{1,0:T(8,128)(2,1)S(1)}, bf16[64,128]{1,0:T(8,128)(2,1)S(1)}, u32[]{:S(2)}, u32[]{:S(2)}) collective-permute-start(bf16[64,128]{1,0:T(8,128)(2,1)S(1)} %get-tuple-element.10), channel_id=1, source_target_pairs={{0,8},{8,0},{16,24},{24,16},{1,9},{9,1},{17,25},{25,17},{2,10},{10... | collective-permute-start | bytes 49160 | tf_op jit(solution)/shard_map/ppermute | solution.py:26
  44.3 4.6 %collective-permute-start.9 = (bf16[64,128]{1,0:T(8,128)(2,1)S(1)}, bf16[64,128]{1,0:T(8,128)(2,1)S(1)}, u32[]{:S(2)}, u32[]{:S(2)}) collective-permute-start(bf16[64,128]{1,0:T(8,128)(2,1)S(1)} %get-tuple-element.9), channel_id=1, source_target_pairs={{0,16},{8,24},{16,0},{24,8},{1,17},{9,25},{17,1},{25,9},{2,18},{10... | collective-permute-start | bytes 49160 | tf_op jit(solution)/shard_map/ppermute | solution.py:26

commit v3 on v1

--- a/solution.py
+++ b/solution.py
@@ -1,13 +1,29 @@
+import functools
 import math
 
 import jax
 import jax.numpy as jnp
+import numpy as np
 from jax import lax
+from jax.experimental import pallas as pl
+from jax.experimental.pallas import tpu as pltpu
 from jax.sharding import PartitionSpec as P
 
 SEGLEN = 128
 grid_width = 64
 image_side = 128.0
+CHUNK = 256
+LANES = (((1,), (1,)), ((), ()))
+COST_PHASE = 12.0
+COST_SCORE = 0.001
+COST_WEIGHT = 0.001
+COST_STACK = 0.001
+COST_FETCH = 0.001
+COST_CHOICE = 0.001
+COST_COUNT = 0.001
+COST_SLICE = 0.001
+COST_NEAR = 0.001
+COST_VOLUME = 0.001
 bf16 = jnp.bfloat16
 f32 = jnp.float32
 
@@ -81,7 +97,7 @@
     return jnp.stack([peak, total])
 
 
-def shards(images, references, shifts, owners, slot_rows, interpolation, regularizer):
+def reduced(images, references, shifts, owners, slot_rows, interpolation, regularizer):
     ori_count, img_count = lax.axis_size("ori"), lax.axis_size("img")
     ori, img = lax.axis_index("ori"), lax.axis_index("img")
     shift_count = shifts.shape[0]
@@ -176,6 +192,579 @@
     return (volume, resampled.reshape(sub_rows, coef))
 
 
+def iota(shape, axis):
+    return lax.broadcasted_iota(jnp.int32, shape, axis)
+
+
+def distance_of(place, shares):
+    half = shares // 2
+    if isinstance(place, int):
+        return 2 * place if place < half else 2 * (place - half) + 1
+    return jnp.where(place < half, 2 * place, 2 * (place - half) + 1)
+
+
+def gather_pair(value, *after, own=None):
+    parts = [value if own is None else own]
+    parts += [hop(value, "ori", k) for k in even_distances()]
+    (near,) = call(
+        functools.partial(stack_kernel, len(parts)),
+        (*parts, *after),
+        (((len(parts), *value.shape), value.dtype),),
+        cost=COST_STACK,
+    )
+    return near, hop(near, "ori", 1)
+
+
+def stack_kernel(count, *refs):
+    for place in range(count):
+        refs[-1][place] = refs[place][...]
+
+
+def phase_kernel(shifts, place, phases, tables):
+    count = shifts.shape[0]
+    unit = 2.0 * math.pi / image_side
+    moves = unit * shifts[...]
+
+    def angles(start, positions):
+        lane = iota((count, positions), 1)
+        freq_x = (lane % grid_width).astype(f32)
+        freq_y = (lane // grid_width + start).astype(f32) - image_side / 2
+        return moves[:, 0:1] * freq_x + moves[:, 1:2] * freq_y
+
+    first = angles(0, CHUNK)
+    step = jnp.broadcast_to(moves[:, 1:2] * float(CHUNK // grid_width), (count, CHUNK))
+    phases[...] = jnp.zeros(phases.shape, f32)
+    for h, angle in enumerate((first, step)):
+        phases[0, h, :count, :] = jnp.cos(angle)
+        phases[1, h, :count, :] = jnp.sin(angle)
+    length = tables.shape[2]
+    angle = angles(place[0] * (length // grid_width), length)
+    tables[...] = jnp.zeros(tables.shape, f32)
+    tables[0, :count, :] = jnp.cos(angle)
+    tables[1, :count, :] = jnp.sin(angle)
+
+
+def turn(phases, now):
+    cosine, sine = now[0], now[1]
+    cos_step, sin_step = phases[0, 1], phases[1, 1]
+    now[0] = cosine * cos_step - sine * sin_step
+    now[1] = sine * cos_step + cosine * sin_step
+
+
+def place_order(ori, shares, group_rows):
+    own_images = group_rows // shares
+    rows = 16 // own_images * group_rows
+    out_row, in_row = iota((rows, 16 * shares), 0), iota((rows, 16 * shares), 1)
+    share, part = in_row // 16, in_row % 16
+    image = (distance_of(share, shares) ^ ori) * own_images + part % own_images
+    return jnp.where(out_row == part // own_images * group_rows + image, 1.0, 0.0).astype(bf16)
+
+
+def place_images(near, far, ori, out):
+    shares, group_rows = 2 * near.shape[0], out.shape[0]
+    step = 16 * shares // group_rows
+    order = place_order(ori, shares, group_rows)
+    for q in range(out.shape[1] // SEGLEN // step):
+        rows = slice(16 * q, 16 * q + 16)
+        block = jnp.concatenate([near[:, rows, :], far[:, rows, :]], axis=0)
+        block = block.reshape(shares * 16, SEGLEN)
+        placed = jnp.dot(order, block, preferred_element_type=f32).astype(bf16)
+        for jj in range(step):
+            lanes = pl.ds((q * step + jj) * SEGLEN, SEGLEN)
+            out[:, lanes] = placed[jj * group_rows : (jj + 1) * group_rows]
+
+
+def score_kernel(
+    shift_count,
+    near,
+    far,
+    references,
+    phases,
+    slots,
+    owners,
+    regularizer,
+    place,
+    message,
+    piece,
+    own,
+    now,
+):
+    group_rows, coef = own.shape
+    half_len = coef // 2
+    place_images(near, far, place[0], own)
+    tiles = piece.shape[0] // group_rows // 2
+    for h in range(2):
+        for t in range(tiles):
+            first = h * half_len + (place[0] * tiles + t) * SEGLEN
+            row = (h * tiles + t) * group_rows
+            piece[row : row + group_rows, :] = own[:, pl.ds(pl.multiple_of(first, SEGLEN), SEGLEN)]
+    now[0] = phases[0, 0]
+    now[1] = phases[1, 0]
+
+    def step(t, total):
+        re_lanes = pl.ds(pl.multiple_of(t * CHUNK, CHUNK), CHUNK)
+        im_lanes = pl.ds(pl.multiple_of(half_len + t * CHUNK, CHUNK), CHUNK)
+        real_part = references[:, re_lanes].astype(f32)
+        imag_part = references[:, im_lanes].astype(f32)
+        rotated_re, rotated_im = [], []
+        for s in range(shift_count):
+            c, d = now[0, s : s + 1, :], now[1, s : s + 1, :]
+            rotated_re.append((real_part * c - imag_part * d).astype(bf16))
+            rotated_im.append((real_part * d + imag_part * c).astype(bf16))
+        total += lax.dot_general(
+            jnp.concatenate(rotated_re, axis=0), own[:, re_lanes], LANES, preferred_element_type=f32
+        )
+        total += lax.dot_general(
+            jnp.concatenate(rotated_im, axis=0), own[:, im_lanes], LANES, preferred_element_type=f32
+        )
+        turn(phases, now)
+        return total
+
+    columns = shift_count * references.shape[0]
+    total = lax.fori_loop(
+        0, half_len // CHUNK, step, jnp.zeros((columns, group_rows), f32), unroll=True
+    )
+    message[...] = jnp.zeros(message.shape, f32)
+    message[:group_rows, :columns] = jnp.swapaxes(total, 0, 1) * (2.0 / math.sqrt(coef))
+    row = group_rows
+    for fact in (slots, owners, regularizer):
+        message[row : row + fact.shape[0], :SEGLEN] = fact[...].astype(f32)
+        row += fact.shape[0]
+
+
+def in_order(near, far, place, rows, out):
+    half = near.shape[0]
+    for p in range(2 * half):
+        part = near[p, rows, :] if p < half else far[p - half, rows, :]
+        out[place[0] ^ distance_of(p, 2 * half)] = part
+
+
+def weight_kernel(group_rows, columns, near, far, pick, piece, place, *refs):
+    *messages, scores, picked = refs
+    shares = scores.shape[0]
+    half = shares // 2
+    in_order(near, far, place, slice(0, group_rows), scores)
+    parts = [scores[p, :, :columns] for p in range(shares)]
+    peak = jnp.max(parts[0], axis=1, keepdims=True)
+    for part in parts[1:]:
+        peak = jnp.maximum(peak, jnp.max(part, axis=1, keepdims=True))
+    exponents = [jnp.exp(part - peak) for part in parts]
+    total = sum(jnp.sum(part, axis=1, keepdims=True) for part in exponents)
+    weights = [(part / total).astype(bf16) for part in exponents]
+    picked[...] = jnp.dot(
+        jnp.concatenate(weights[:half], axis=0), pick[0], preferred_element_type=f32
+    ) + jnp.dot(jnp.concatenate(weights[half:], axis=0), pick[1], preferred_element_type=f32)
+    for k, message in enumerate(messages):
+        lanes = pl.ds(pl.multiple_of((place[1] ^ k) * SEGLEN, SEGLEN), SEGLEN)
+        message[: picked.shape[0], :] = picked[:, lanes].astype(bf16)
+        message[picked.shape[0] :, :] = piece[...]
+
+
+def flat_facts(group_rows, sub_rows, near, far, place, reg_rows, ordered, upright, flat):
+    shares = ordered.shape[0]
+    orients = shares * sub_rows
+    blocks = flat.shape[1]
+    lot = SEGLEN // orients
+    in_order(near, far, place, slice(group_rows, near.shape[1]), ordered)
+
+    def rows_of(first, count):
+        return [ordered[p, first : first + count, :SEGLEN] for p in range(shares)]
+
+    facts = rows_of(0, sub_rows) + rows_of(sub_rows, sub_rows)
+    for h in range(reg_rows):
+        facts += rows_of(2 * sub_rows + h, 1)
+    used = 2 * orients + shares * reg_rows
+    facts = jnp.concatenate(facts + [jnp.zeros((SEGLEN - used, SEGLEN), f32)], axis=0)
+    upright[...] = jnp.swapaxes(facts, 0, 1)
+    parts = [upright[pl.ds(b, blocks, stride=lot), :] for b in range(lot)]
+    for h in range(2):
+        lanes = slice(h * orients, (h + 1) * orients)
+        flat[h] = jnp.concatenate([part[:, lanes] for part in parts], axis=1)
+    run = blocks // (2 * shares)
+    taken = []
+    for p in range(shares):
+        share = place[0] ^ distance_of(p, shares)
+        taken += [h * (blocks // 2) + share * run + i for h in range(2) for i in range(run)]
+    slots = jnp.concatenate([flat[0, pl.ds(a, 1), :] for a in taken], axis=0)
+    owners = jnp.concatenate([flat[1, pl.ds(a, 1), :] for a in taken], axis=0)
+    return slots, owners
+
+
+def choice_kernel(
+    group_rows,
+    sub_rows,
+    near,
+    far,
+    after,
+    place,
+    chosen,
+    own_slots,
+    own_owner_lanes,
+    ordered,
+    upright,
+    flat,
+):
+    shares = ordered.shape[0]
+    row_count = own_slots.shape[1]
+    tiles = SEGLEN
+    slots, owners = flat_facts(group_rows, sub_rows, near, far, place, 0, ordered, upright, flat)
+    target = (owners.astype(jnp.int32) // 2).astype(f32) * float(row_count) + slots
+    pair_row = iota((chosen.shape[0], SEGLEN), 0).astype(f32)
+    for a in range(flat.shape[1]):
+        block = slice(a * SEGLEN, (a + 1) * SEGLEN)
+        chosen[:, block] = jnp.where(pair_row == target[a : a + 1, :], 1.0, 0.0).astype(bf16)
+    own = near[0, group_rows : near.shape[1], :SEGLEN]
+    own = jnp.concatenate([own, jnp.zeros((SEGLEN - own.shape[0], SEGLEN), f32)], axis=0)
+    own = jnp.swapaxes(own, 0, 1)
+    slot_lane = iota((tiles, row_count), 1).astype(f32)
+    for o in range(sub_rows):
+        rows = slice(o * tiles, (o + 1) * tiles)
+        own_slots[rows, :] = jnp.where(slot_lane == own[:, o : o + 1], 1.0, 0.0).astype(bf16)
+        own_owner_lanes[rows, :] = jnp.broadcast_to(
+            own[:, sub_rows + o : sub_rows + o + 1], (tiles, SEGLEN)
+        ).astype(bf16)
+
+
+def count_kernel(
+    group_rows,
+    sub_rows,
+    near,
+    far,
+    after,
+    place,
+    parity_lanes,
+    counts,
+    regularizer,
+    ordered,
+    upright,
+    flat,
+):
+    shares = ordered.shape[0]
+    row_count = regularizer.shape[0]
+    reg_rows = row_count // SEGLEN
+    orients = shares * sub_rows
+    blocks = flat.shape[1]
+    slots, owners = flat_facts(
+        group_rows, sub_rows, near, far, place, reg_rows, ordered, upright, flat
+    )
+    for h in range(reg_rows):
+        first = 2 * orients + h * shares
+        regularizer[h * SEGLEN : (h + 1) * SEGLEN, :] = upright[:, first : first + shares]
+    parity = (owners.astype(jnp.int32) % 2).astype(f32)
+    columns = jnp.concatenate(
+        [owners, parity, jnp.zeros((SEGLEN - 2 * blocks, SEGLEN), f32)], axis=0
+    )
+    columns = jnp.swapaxes(columns, 0, 1)
+    slot_row = iota((row_count, SEGLEN), 0).astype(f32)
+    count_lane = iota((SEGLEN, shares * orients), 1)
+    lane_owner = (count_lane // orients).astype(f32)
+    same = iota((SEGLEN, shares * orients), 0) % orients == count_lane % orients
+    total = jnp.zeros((row_count, shares * orients), f32)
+    for a in range(0, blocks, 2):
+        slot_chosen, owned = [], []
+        for b in (a, a + 1):
+            block = slice(b * SEGLEN, (b + 1) * SEGLEN)
+            parity_lanes[block, :] = jnp.broadcast_to(
+                columns[:, blocks + b : blocks + b + 1], (SEGLEN, SEGLEN)
+            ).astype(bf16)
+            slot_chosen.append(jnp.where(slot_row == slots[b : b + 1, :], 1.0, 0.0).astype(bf16))
+            holds = jnp.where(columns[:, b : b + 1] == lane_owner, 1.0, 0.0)
+            owned.append(jnp.where(same, holds, 0.0).astype(bf16))
+        total += jnp.dot(
+            jnp.concatenate(slot_chosen, axis=1),
+            jnp.concatenate(owned, axis=0),
+            preferred_element_type=f32,
+        )
+    counts[...] = total.astype(bf16)
+
+
+def slice_kernel(shift_count, group_rows, *refs):
+    *messages, tables, arrange, kernel, after, segments, masses = refs
+    length = tables.shape[2]
+    half = arrange.shape[1] // SEGLEN
+    orients = arrange.shape[0] // shift_count
+    lot = CHUNK // SEGLEN
+
+    stacked = jnp.concatenate(
+        [
+            jnp.concatenate(
+                [message[a * group_rows : (a + 1) * group_rows, :] for message in messages], axis=0
+            )
+            for a in range(half)
+        ],
+        axis=1,
+    )
+    weights = lax.dot_general(arrange[...], stacked, LANES, preferred_element_type=f32)
+    mass = jnp.sum(weights, axis=1, keepdims=True)
+    mass = sum(mass[s * orients : (s + 1) * orients] for s in range(shift_count))
+    masses[...] = jnp.broadcast_to(mass, masses.shape)
+    weights = weights.astype(bf16)
+
+    def images_at(tile):
+        row = (half + tile) * group_rows
+        return jnp.concatenate([message[row : row + group_rows, :] for message in messages], axis=0)
+
+    for t in range(length // CHUNK):
+        lanes = slice(t * CHUNK, (t + 1) * CHUNK)
+        tiles = range(t * lot, (t + 1) * lot)
+        real_part = jnp.concatenate([images_at(j) for j in tiles], axis=1)
+        imag_part = jnp.concatenate([images_at(length // SEGLEN + j) for j in tiles], axis=1)
+        summed_re = jnp.dot(weights, real_part, preferred_element_type=f32)
+        summed_im = jnp.dot(weights, imag_part, preferred_element_type=f32)
+        total_re = jnp.zeros((orients, CHUNK), f32)
+        total_im = jnp.zeros((orients, CHUNK), f32)
+        for s in range(shift_count):
+            c, d = tables[0, s : s + 1, lanes], tables[1, s : s + 1, lanes]
+            part_re = summed_re[s * orients : (s + 1) * orients]
+            part_im = summed_im[s * orients : (s + 1) * orients]
+            total_re += part_re * c + part_im * d
+            total_im += part_im * c - part_re * d
+        for h in range(lot):
+            lanes = slice(h * SEGLEN, (h + 1) * SEGLEN)
+            row = (t * lot + h) * orients
+            segments[row : row + orients, :] = total_re[:, lanes].astype(bf16)
+            row += length // SEGLEN * orients
+            segments[row : row + orients, :] = total_im[:, lanes].astype(bf16)
+    segments[2 * (length // SEGLEN) * orients :, :] = kernel[...].astype(bf16)
+
+
+def insert(shares, first, chosen, parity_lanes, segments):
+    rows = segments.shape[0] // shares.shape[0]
+    zero = jnp.zeros((rows, SEGLEN), bf16)
+    for p in range(shares.shape[0]):
+        part = shares[p, :rows, :]
+        parity = parity_lanes[(first + p) * rows : (first + p + 1) * rows, :]
+        for w in range(2):
+            segments[p * rows : (p + 1) * rows, w * SEGLEN : (w + 1) * SEGLEN] = jnp.where(
+                parity == float(w), part, zero
+            )
+    lanes = slice(first * rows, (first + shares.shape[0]) * rows)
+    return jnp.dot(chosen[:, lanes], segments[...], preferred_element_type=f32)
+
+
+def near_kernel(
+    near, chosen, parity_lanes, counts, regularizer, masses, inserted, inverse, segments
+):
+    inserted[...] = insert(near, 0, chosen, parity_lanes, segments)
+    shares = regularizer.shape[1]
+    mass = masses[...]
+    mass_hi = mass.astype(bf16).astype(f32)
+    lane = iota(mass.shape, 1)
+    both = jnp.where(lane < shares, mass_hi, jnp.where(lane < 2 * shares, mass - mass_hi, 0.0))
+    spread = jnp.concatenate([jnp.where(lane % shares == w, both, 0.0) for w in range(shares)], axis=0)
+    weight_sum = jnp.dot(counts[...], spread.astype(bf16), preferred_element_type=f32)
+    weight_sum = weight_sum[:, :shares] + weight_sum[:, shares : 2 * shares]
+    inverse[...] = 1.0 / (weight_sum + regularizer[...])
+
+
+def volume_kernel(
+    near,
+    far,
+    near_inserted,
+    chosen,
+    parity_lanes,
+    inverse,
+    own_slots,
+    own_owner_lanes,
+    place,
+    volume,
+    resampled,
+    segments,
+    mapped,
+    result,
+):
+    half = near.shape[0]
+    shares = 2 * half
+    rows = segments.shape[0] // half
+    row_count = volume.shape[0]
+    sub_rows = resampled.shape[0]
+    tiles = resampled.shape[1] // SEGLEN
+    inserted = insert(far, half, chosen, parity_lanes, segments) + near_inserted[...]
+    inserted = inserted.astype(bf16)
+    kernels = [near[p, rows:, :] for p in range(half)] + [far[p, rows:, :] for p in range(half)]
+    for p in range(shares):
+        mapped_at = place[0] ^ distance_of(p, shares)
+        mapped[mapped_at] = kernels[p]
+    back = []
+    for w in range(shares):
+        kernel = mapped[w]
+        part = inserted[
+            w // 2 * row_count : (w // 2 + 1) * row_count, w % 2 * SEGLEN : (w % 2 + 1) * SEGLEN
+        ]
+        brick = jnp.dot(part, kernel, preferred_element_type=f32) * inverse[:, w : w + 1]
+
+        @pl.when(place[0] == w)
+        def _():
+            volume[...] = brick
+
+        back.append(
+            lax.dot_general(
+                brick.astype(bf16), kernel, LANES, preferred_element_type=f32
+            ).astype(bf16)
+        )
+    taken = jnp.dot(own_slots[...], jnp.concatenate(back, axis=1), preferred_element_type=f32)
+    owner = own_owner_lanes[...].astype(f32)
+    total = jnp.zeros((sub_rows * tiles, SEGLEN), f32)
+    for w in range(shares):
+        total = jnp.where(owner == float(w), taken[:, w * SEGLEN : (w + 1) * SEGLEN], total)
+    result[...] = total
+    for j in range(tiles):
+        resampled[:, j * SEGLEN : (j + 1) * SEGLEN] = result[pl.ds(j, sub_rows, stride=tiles), :]
+
+
+def call(kernel, inputs, outputs, scratch=(), cost=1.0, small=(), space=pltpu.VMEM, room=24):
+    inside = pl.BlockSpec(memory_space=pltpu.VMEM)
+    scalars = pl.BlockSpec(memory_space=pltpu.SMEM)
+    return pl.pallas_call(
+        kernel,
+        out_shape=[jax.ShapeDtypeStruct(shape, dtype) for shape, dtype in outputs],
+        in_specs=[pl.BlockSpec(memory_space=space)] * len(inputs) + [scalars] * len(small),
+        out_specs=[inside] * len(outputs),
+        scratch_shapes=list(scratch),
+        compiler_params=pltpu.CompilerParams(vmem_limit_bytes=room * 2**20),
+        cost_estimate=pl.CostEstimate(
+            flops=int(cost * 1.15e9), bytes_accessed=0, transcendentals=0
+        ),
+    )(*inputs, *small)
+
+
+def whole_plane(images, references, shifts, owners, slot_rows, interpolation, regularizer):
+    ori_count, img_count = lax.axis_size("ori"), lax.axis_size("img")
+    ori, img = lax.axis_index("ori"), lax.axis_index("img")
+    shift_count = shifts.shape[0]
+    own_images, coef = images.shape
+    tiles = coef // SEGLEN
+    half = ori_count // 2
+    row_count = regularizer.shape[0]
+    orient_count = references.shape[0]
+    sub_rows = orient_count // img_count
+    group_rows = own_images * ori_count
+    columns = shift_count * orient_count
+    orients = ori_count * sub_rows
+    length = coef // 2 // ori_count
+    place = jnp.stack([ori, img]).astype(jnp.int32)
+
+    piece = images.reshape(own_images, tiles, SEGLEN).transpose(1, 0, 2).reshape(-1, SEGLEN)
+    column = np.arange(columns)
+    orient = column % orient_count
+    lane = orient // sub_rows * SEGLEN + column // orient_count * sub_rows + orient % sub_rows
+    pick = np.stack([lane + h * (SEGLEN // 2) for h in range(2)])[:, :, None]
+    pick = jnp.asarray(pick == np.arange(img_count * SEGLEN), bf16)
+    row = np.arange(shift_count * orients)
+    share = row % orients // sub_rows
+    source = share % half * SEGLEN + share // half * (SEGLEN // 2)
+    source += row // orients * sub_rows + row % sub_rows
+    arrange = jnp.asarray(source[:, None] == np.arange(half * SEGLEN), bf16)
+    phases, tables = call(
+        phase_kernel,
+        (shifts,),
+        (((2, 2, -(-shift_count // 8) * 8, CHUNK), f32), ((2, -(-shift_count // 8) * 8, length), f32)),
+        small=(place,),
+        cost=COST_PHASE,
+    )
+    near, far = gather_pair(piece, phases)
+    message_rows = group_rows + 16
+    message_lanes = -(-columns // SEGLEN) * SEGLEN
+    scores, part = call(
+        functools.partial(score_kernel, shift_count),
+        (
+            near,
+            far,
+            references,
+            phases,
+            slot_rows.reshape(-1, SEGLEN),
+            owners.reshape(-1, SEGLEN),
+            regularizer.reshape(-1, SEGLEN),
+        ),
+        (((message_rows, message_lanes), f32), ((2 * length // SEGLEN * group_rows, SEGLEN), bf16)),
+        scratch=(pltpu.VMEM((group_rows, coef), bf16), pltpu.VMEM(phases.shape[1:], f32)),
+        small=(place,),
+        cost=COST_SCORE,
+    )
+    near, far = gather_pair(scores)
+
+    messages = call(
+        functools.partial(weight_kernel, group_rows, columns),
+        (near, far, pick, part),
+        (((half * group_rows + part.shape[0], SEGLEN), bf16),) * img_count,
+        scratch=(
+            pltpu.VMEM((ori_count, group_rows, message_lanes), f32),
+            pltpu.VMEM((half * group_rows, img_count * SEGLEN), f32),
+        ),
+        small=(place,),
+        cost=COST_WEIGHT,
+    )
+    arrived = [messages[0]] + [hop(messages[k], "img", k) for k in range(1, img_count)]
+
+    fact_scratch = (
+        pltpu.VMEM((ori_count, 16, message_lanes), f32),
+        pltpu.VMEM((SEGLEN, SEGLEN), f32),
+        pltpu.VMEM((2, orients * tiles // SEGLEN, SEGLEN), f32),
+    )
+    parity_lanes, counts, regs = call(
+        functools.partial(count_kernel, group_rows, sub_rows),
+        (near, far, messages[0]),
+        (
+            ((orients * tiles, SEGLEN), bf16),
+            ((row_count, ori_count * orients), bf16),
+            ((row_count, ori_count), f32),
+        ),
+        scratch=fact_scratch,
+        small=(place,),
+        cost=COST_COUNT,
+    )
+    rows = 2 * (length // SEGLEN) * orients
+    segments, masses = call(
+        functools.partial(slice_kernel, shift_count, group_rows),
+        (*arrived, tables, arrange, interpolation, regs),
+        (((rows + SEGLEN, SEGLEN), bf16), ((orients, SEGLEN), f32)),
+        cost=COST_SLICE,
+    )
+    chosen, own_slots, own_owner_lanes = call(
+        functools.partial(choice_kernel, group_rows, sub_rows),
+        (near, far, masses),
+        (
+            ((half * row_count, orients * tiles), bf16),
+            ((sub_rows * tiles, row_count), bf16),
+            ((sub_rows * tiles, SEGLEN), bf16),
+        ),
+        scratch=fact_scratch,
+        small=(place,),
+        cost=COST_CHOICE,
+    )
+
+    near, far = gather_pair(segments, own_owner_lanes)
+    masked = pltpu.VMEM((half * rows, 2 * SEGLEN), bf16)
+    inserted, inverse = call(
+        near_kernel,
+        (near, chosen, parity_lanes, counts, regs, masses),
+        (((half * row_count, 2 * SEGLEN), f32), ((row_count, ori_count), f32)),
+        scratch=(masked,),
+        cost=COST_NEAR,
+    )
+    volume, resampled = call(
+        volume_kernel,
+        (near, far, inserted, chosen, parity_lanes, inverse, own_slots, own_owner_lanes),
+        (((row_count, SEGLEN), f32), ((sub_rows, coef), f32)),
+        scratch=(
+            masked,
+            pltpu.VMEM((ori_count, SEGLEN, SEGLEN), bf16),
+            pltpu.VMEM((sub_rows * tiles, SEGLEN), f32),
+        ),
+        small=(place,),
+        cost=COST_VOLUME,
+    )
+    return (volume, resampled)
+
+
+def shards(images, references, shifts, owners, slot_rows, interpolation, regularizer):
+    arguments = (images, references, shifts, owners, slot_rows, interpolation, regularizer)
+    whole_bytes = images.size * 2 * lax.axis_size("img") * lax.axis_size("ori")
+    if whole_bytes <= 4 * 2**20:
+        return whole_plane(*arguments)
+    return reduced(*arguments)
+
+
 def solution(mesh):
     in_specs = (
         P(("img", "ori"), None),

time: 77.5 us -> 51.3 us (0.66)
  Pallas kernels: 0 us -> 19.4 us
  matrix products: 13.1 us -> 0 us
  waiting for transfers between devices: 25.3 us -> 13.6 us
  other arithmetic: 11.1 us -> 0.07 us
  local copies, waits for them, and re-layouts: 6.56 us -> 0.81 us
  starting transfers between devices: 20.1 us -> 16.3 us
    pallas_call x0 -> x11, Pallas kernels: none -> 19.4 us  [call(): pl.pallas_call(kernel, out_shape=[jax.ShapeDtypeStruct(shape, dtype) for...]
    dot_general x29 -> x0, matrix products: 13.1 us -> none  [the longest x12 6.21 us: shards(): lax.dot_general(group_images, rotated, (((1,), (1,)), ((), ())), preferre...]
    ppermute x19 -> x15, waiting for transfers between devices: 25.3 us -> 13.6 us  [hop(): return lax.ppermute(value, axis, pairs)]
    another operation x10 -> x1, other arithmetic: 4.68 us -> 0.07 us  [whole_plane(): place = jnp.stack([ori, img]).astype(jnp.int32)]
    ppermute x19 -> x15, starting transfers between devices: 20.1 us -> 16.3 us  [hop(): return lax.ppermute(value, axis, pairs)]
    add x7 -> x0, other arithmetic: 2.93 us -> none  [the longest x1 1.42 us: backproject(): total_re = total_re + sum_re * cosine_table[s] + sum_im * sine_table[s]]
    cos x1 -> x0, other arithmetic: 1.94 us -> none  [phase_tables(): return (jnp.cos(angles), jnp.sin(angles))]
    concatenate x2 -> x0, local copies, waits for them, and re-layouts: 1.47 us -> none  [gather_plane(): return jnp.concatenate([near, hop(near, 'ori', 1)], axis=0)]
  transfers between devices with their start and end apart: 19 -> 15, of which waited for: 15 -> 10; matrix products, arithmetic and copies ran while one was open for 11% -> 2% of each run, Pallas kernels for 0% -> 18%
where the time goes in v3:
time: 51.3 us; the launch traced here: 51.1 us
  Pallas kernels  19.4 us (38%)
  starting transfers between devices  16.3 us (32%)
  waiting for transfers between devices  13.6 us (27%)
  local copies, waits for them, and re-layouts  0.81 us (2%)
  between operations  0.8 us (2%)
    pallas_call x11, Pallas kernels, call(): pl.pallas_call(kernel, out_shape=[jax.ShapeDtypeStruct(shape, dtype) for...  19.4 us
    ppermute x15, starting transfers between devices, hop(): return lax.ppermute(value, axis, pairs)  16.3 us
    ppermute x15, waiting for transfers between devices, hop(): return lax.ppermute(value, axis, pairs)  13.6 us
  transfers between devices with their start and end apart: 15, of which 10 were waited for; matrix products, arithmetic and copies ran while one was open for 2% of the time, Pallas kernels for 18%

profile of v3, /device:TPU:0, one launch (start us, length us, event | category | flops | bytes accessed | tf_op | source)
XLA Modules:
  0.0 51.1 jit_solution(14287223204646049576)
XLA Ops:
  0.6 4.0 %collective-permute-start.2 = (bf16[256,128]{1,0:T(8,128)(2,1)}, bf16[256,128]{1,0:T(8,128)(2,1)S(1)}, u32[]{:S(2)}, u32[]{:S(2)}) collective-permute-start(bf16[256,128]{1,0:T(8,128)(2,1)} %bitcast.10), channel_id=1, source_target_pairs={{0,6},{1,7},{2,4},{3,5},{4,2},{5,3},{6,0},{7,1},{8,14},{9,15},{10,... | collective-permute-start | bytes 196616 | tf_op jit(solution)/shard_map/ppermute | solution.py:33
  4.6 0.5 collective-permute-start.1
  5.1 0.1 collective-permute-start
  5.2 0.8 %copy.12.shifts = f32[12,2]{1,0:T(8,128)S(1)} copy(f32[12,2]{0,1:T(2,128)} %param.11) | data formatting | bytes 192 | tf_op args[2]
  6.0 0.1 pad_add_fusion.place
  6.1 0.0 copy-start.7
  6.1 0.0 copy-start.1
  6.1 0.0 copy-start.2
  6.1 0.0 copy-start.4
  6.1 0.9 %shard_map.104 = (f32[2,2,16,256]{3,2,1,0:T(8,128)S(1)}, f32[2,16,1024]{2,1,0:T(8,128)S(1)}) custom-call(f32[12,2]{1,0:T(8,128)S(1)} %copy.12.shifts, s32[2]{0:T(128)S(1)} %pad_add_fusion.place), custom_call_target="tpu_custom_call" | custom-call | flops 13799999488 | tf_op jit(solution)/shard_map/pallas_call | solution.py:618
  7.1 0.0 collective-permute-done.2.refs_3_
  7.1 2.0 %collective-permute-done.1.refs_2_ = bf16[256,128]{1,0:T(8,128)(2,1)S(1)} collective-permute-done((bf16[256,128]{1,0:T(8,128)(2,1)}, bf16[256,128]{1,0:T(8,128)(2,1)S(1)}, u32[]{:S(2)}, u32[]{:S(2)}) %collective-permute-start.1) | collective-permute-done | bytes 65568 | tf_op jit(solution)/shard_map/ppermute | solution.py:33
  9.1 0.5 collective-permute-done.refs_1_
  9.6 0.0 copy-done.3
  9.6 0.1 collective-permute-start.3
  9.7 1.5 %collective-permute-done.3.far = bf16[4,256,128]{2,1,0:T(8,128)(2,1)S(1)} collective-permute-done((bf16[4,256,128]{2,1,0:T(8,128)(2,1)S(1)}, bf16[4,256,128]{2,1,0:T(8,128)(2,1)S(1)}, u32[]{:S(2)}, u32[]{:S(2)}) %collective-permute-start.3) | collective-permute-done | bytes 262176 | tf_op jit(solution)/shard_map/ppermute | solution.py:33
  11.2 0.0 copy-done
  11.2 0.0 copy-done.5
  11.2 3.0 %shard_map.106 = (f32[32,256]{1,0:T(8,128)S(1)}, bf16[256,128]{1,0:T(8,128)(2,1)S(1)}) custom-call(bf16[4,256,128]{2,1,0:T(8,128)(2,1)S(1)} %shard_map.105.near, bf16[4,256,128]{2,1,0:T(8,128)(2,1)S(1)} %collective-permute-done.3.far, bf16[16,16384]{1,0:T(8,128)(2,1)S(1)} %copy-done, f32[2,2,16,256]{3,2,1,0:T(8,128)S(1)} %get-tuple-element.20.refs_4_.phases, ...), custom_call_target="tpu_custom_call" | custom-call | flops 1150000 | tf_op jit(solution)/shard_map/pallas_call | solution.py:618
  14.2 1.5 %collective-permute-start.6 = (f32[32,256]{1,0:T(8,128)S(1)}, f32[32,256]{1,0:T(8,128)S(1)}, u32[]{:S(2)}, u32[]{:S(2)}) collective-permute-start(f32[32,256]{1,0:T(8,128)S(1)} %get-tuple-element.21.refs_0_), channel_id=1, source_target_pairs={{0,6},{1,7},{2,4},{3,5},{4,2},{5,3},{6,0},{7,1},{8,14},{9,15},{10,... | collective-permute-start | bytes 98312 | tf_op jit(solution)/shard_map/ppermute | solution.py:33
  15.7 0.4 collective-permute-start.5
  16.2 1.6 %collective-permute-start.4 = (f32[32,256]{1,0:T(8,128)S(1)}, f32[32,256]{1,0:T(8,128)S(1)}, u32[]{:S(2)}, u32[]{:S(2)}) collective-permute-start(f32[32,256]{1,0:T(8,128)S(1)} %get-tuple-element.21.refs_0_), channel_id=1, source_target_pairs={{0,2},{1,3},{2,0},{3,1},{4,6},{5,7},{6,4},{7,5},{8,10},{9,11},{10,... | collective-permute-start | bytes 98312 | tf_op jit(solution)/shard_map/ppermute | solution.py:33
  17.7 1.3 %collective-permute-done.6.refs_3_ = f32[32,256]{1,0:T(8,128)S(1)} collective-permute-done((f32[32,256]{1,0:T(8,128)S(1)}, f32[32,256]{1,0:T(8,128)S(1)}, u32[]{:S(2)}, u32[]{:S(2)}) %collective-permute-start.6) | collective-permute-done | bytes 32800 | tf_op jit(solution)/shard_map/ppermute | solution.py:33
  19.1 0.6 %collective-permute-done.5.refs_2_ = f32[32,256]{1,0:T(8,128)S(1)} collective-permute-done((f32[32,256]{1,0:T(8,128)S(1)}, f32[32,256]{1,0:T(8,128)S(1)}, u32[]{:S(2)}, u32[]{:S(2)}) %collective-permute-start.5) | collective-permute-done | bytes 32800 | tf_op jit(solution)/shard_map/ppermute | solution.py:33
  19.6 0.4 collective-permute-done.4.refs_1_
  20.1 0.1 collective-permute-start.7
  20.2 1.3 %collective-permute-done.7.far = f32[4,32,256]{2,1,0:T(8,128)S(1)} collective-permute-done((f32[4,32,256]{2,1,0:T(8,128)S(1)}, f32[4,32,256]{2,1,0:T(8,128)S(1)}, u32[]{:S(2)}, u32[]{:S(2)}) %collective-permute-start.7) | collective-permute-done | bytes 131104 | tf_op jit(solution)/shard_map/ppermute | solution.py:33
  21.5 0.0 copy-done.1
  21.5 0.9 %shard_map.108 = (bf16[320,128]{1,0:T(8,128)(2,1)S(1)}, bf16[320,128]{1,0:T(8,128)(2,1)S(1)}, bf16[320,128]{1,0:T(8,128)(2,1)S(1)}, bf16[320,128]{1,0:T(8,128)(2,1)S(1)}) custom-call(f32[4,32,256]{2,1,0:T(8,128)S(1)} %shard_map.107.near, f32[4,32,256]{2,1,0:T(8,128)S(1)} %collective-permute-done.7.far, bf16[2,192,512]{2,1,0:T(8,128)(2,1)S(1)} %copy-done.1, ...), custom_call_target="tpu_custom_call" | custom-call | flops 1150000 | tf_op jit(solution)/shard_map/pallas_call | solution.py:618
  22.5 1.7 %collective-permute-start.8 = (bf16[320,128]{1,0:T(8,128)(2,1)S(1)}, bf16[320,128]{1,0:T(8,128)(2,1)S(1)}, u32[]{:S(2)}, u32[]{:S(2)}) collective-permute-start(bf16[320,128]{1,0:T(8,128)(2,1)S(1)} %get-tuple-element.24), channel_id=1, source_target_pairs={{0,8},{8,0},{16,24},{24,16},{1,9},{9,1},{17,25},{25,17},{2,10},{10... | collective-permute-start | bytes 245768 | tf_op jit(solution)/shard_map/ppermute | solution.py:33
  24.2 2.6 %collective-permute-start.9 = (bf16[320,128]{1,0:T(8,128)(2,1)S(1)}, bf16[320,128]{1,0:T(8,128)(2,1)S(1)}, u32[]{:S(2)}, u32[]{:S(2)}) collective-permute-start(bf16[320,128]{1,0:T(8,128)(2,1)S(1)} %get-tuple-element.25), channel_id=1, source_target_pairs={{0,16},{8,24},{16,0},{24,8},{1,17},{9,25},{17,1},{25,9},{2,18},{10... | collective-permute-start | bytes 245768 | tf_op jit(solution)/shard_map/ppermute | solution.py:33
  26.8 0.2 collective-permute-start.10
  26.9 2.2 %shard_map.109 = (bf16[4096,128]{1,0:T(8,128)(2,1)S(1)}, bf16[256,256]{1,0:T(8,128)(2,1)S(1)}, f32[256,8]{1,0:T(8,128)S(1)}) custom-call(f32[4,32,256]{2,1,0:T(8,128)S(1)} %shard_map.107.near, f32[4,32,256]{2,1,0:T(8,128)S(1)} %collective-permute-done.7.far, bf16[320,128]{1,0:T(8,128)(2,1)S(1)} %get-tuple-element.23.after.refs_0_, s32[2]{0:T(128)S(1)} %pad_add_fusion.place), custom_call_target="tpu_custom_call" | custom-call | flops 1150000 | tf_op jit(solution)/shard_map/pallas_call | solution.py:618
  29.1 0.0 collective-permute-done.8.refs_1_
  29.1 4.5 %collective-permute-done.9.refs_2_ = bf16[320,128]{1,0:T(8,128)(2,1)S(1)} collective-permute-done((bf16[320,128]{1,0:T(8,128)(2,1)S(1)}, bf16[320,128]{1,0:T(8,128)(2,1)S(1)}, u32[]{:S(2)}, u32[]{:S(2)}) %collective-permute-start.9) | collective-permute-done | bytes 81952 | tf_op jit(solution)/shard_map/ppermute | solution.py:33
  33.6 0.0 collective-permute-done.10.refs_3_
  33.7 0.9 %shard_map.110 = (bf16[640,128]{1,0:T(8,128)(2,1)S(1)}, f32[32,128]{1,0:T(8,128)S(1)}) custom-call(bf16[320,128]{1,0:T(8,128)(2,1)S(1)} %get-tuple-element.23.after.refs_0_, bf16[320,128]{1,0:T(8,128)(2,1)S(1)} %collective-permute-done.8.refs_1_, bf16[320,128]{1,0:T(8,128)(2,1)S(1)} %collective-permute-done.9.refs_2_, ...), custom_call_target="tpu_custom_call" | custom-call | flops 1150000 | tf_op jit(solution)/shard_map/pallas_call | solution.py:618
  34.6 2.5 %collective-permute-start.13 = (bf16[640,128]{1,0:T(8,128)(2,1)S(1)}, bf16[640,128]{1,0:T(8,128)(2,1)S(1)}, u32[]{:S(2)}, u32[]{:S(2)}) collective-permute-start(bf16[640,128]{1,0:T(8,128)(2,1)S(1)} %get-tuple-element.29.refs_0_), channel_id=1, source_target_pairs={{0,6},{1,7},{2,4},{3,5},{4,2},{5,3},{6,0},{7,1},{8,14},{9,15},{10,... | collective-permute-start | bytes 491528 | tf_op jit(solution)/shard_map/ppermute | solution.py:33
  37.1 0.5 collective-permute-start.12
  37.6 0.5 %collective-permute-start.11 = (bf16[640,128]{1,0:T(8,128)(2,1)S(1)}, bf16[640,128]{1,0:T(8,128)(2,1)S(1)}, u32[]{:S(2)}, u32[]{:S(2)}) collective-permute-start(bf16[640,128]{1,0:T(8,128)(2,1)S(1)} %get-tuple-element.29.refs_0_), channel_id=1, source_target_pairs={{0,2},{1,3},{2,0},{3,1},{4,6},{5,7},{6,4},{7,5},{8,10},{9,11},{10,... | collective-permute-start | bytes 491528 | tf_op jit(solution)/shard_map/ppermute | solution.py:33
  38.1 4.3 %shard_map.111 = (bf16[1024,4096]{1,0:T(8,128)(2,1)S(1)}, bf16[512,256]{1,0:T(8,128)(2,1)S(1)}, bf16[512,128]{1,0:T(8,128)(2,1)S(1)}) custom-call(f32[4,32,256]{2,1,0:T(8,128)S(1)} %shard_map.107.near, f32[4,32,256]{2,1,0:T(8,128)S(1)} %collective-permute-done.7.far, f32[32,128]{1,0:T(8,128)S(1)} %get-tuple-element.30.after.masses, s32[2]{0:T(128)S(1)} %pad_add_fusion.place), custom_call_target="tpu_custom_call" | custom-call | flops 1150000 | tf_op jit(solution)/shard_map/pallas_call | solution.py:618
  42.4 0.0 collective-permute-done.13.refs_3_
  42.4 0.9 %collective-permute-done.12.refs_2_ = bf16[640,128]{1,0:T(8,128)(2,1)S(1)} collective-permute-done((bf16[640,128]{1,0:T(8,128)(2,1)S(1)}, bf16[640,128]{1,0:T(8,128)(2,1)S(1)}, u32[]{:S(2)}, u32[]{:S(2)}) %collective-permute-start.12) | collective-permute-done | bytes 163872 | tf_op jit(solution)/shard_map/ppermute | solution.py:33
  43.3 0.0 collective-permute-done.11.refs_1_
  43.4 0.1 collective-permute-start.14
  43.5 1.6 %shard_map.113 = (f32[1024,256]{1,0:T(8,128)S(1)}, f32[256,8]{1,0:T(8,128)S(1)}) custom-call(bf16[4,640,128]{2,1,0:T(8,128)(2,1)S(1)} %shard_map.112.near, bf16[1024,4096]{1,0:T(8,128)(2,1)S(1)} %get-tuple-element.32.chosen, bf16[4096,128]{1,0:T(8,128)(2,1)S(1)} %get-tuple-element.33.parity_lanes, bf16[256,256]{1,0:T(8,128)(2,1)S(1)} %get-tuple-element.34.counts, ...), custom_call_target="tpu_custom_call" | custom-call | flops 1150000 | tf_op jit(solution)/shard_map/pallas_call | solution.py:618
  45.0 0.5 collective-permute-done.14.far
  45.6 5.5 %shard_map.114 = (f32[256,128]{1,0:T(8,128)}, f32[4,16384]{1,0:T(4,128)}) custom-call(bf16[4,640,128]{2,1,0:T(8,128)(2,1)S(1)} %shard_map.112.near, bf16[4,640,128]{2,1,0:T(8,128)(2,1)S(1)} %collective-permute-done.14.far, f32[1024,256]{1,0:T(8,128)S(1)} %get-tuple-element.35.near_inserted, bf16[1024,4096]{1,0:T(8,128)(2,1)S(1)} %get-tuple-element.32.chosen, ...), custom_call_target="tpu_custom_call" | custom-call | flops 1150000 | tf_op jit(solution)/shard_map/pallas_call | solution.py:618
  (11 shorter events, 0.1 us)
Async XLA Ops:
  0.6 6.5 %collective-permute-start.2 = (bf16[256,128]{1,0:T(8,128)(2,1)}, bf16[256,128]{1,0:T(8,128)(2,1)S(1)}, u32[]{:S(2)}, u32[]{:S(2)}) collective-permute-start(bf16[256,128]{1,0:T(8,128)(2,1)} %bitcast.10), channel_id=1, source_target_pairs={{0,6},{1,7},{2,4},{3,5},{4,2},{5,3},{6,0},{7,1},{8,14},{9,15},{10,... | collective-permute-start | bytes 196616 | tf_op jit(solution)/shard_map/ppermute | solution.py:33
  4.6 4.5 %collective-permute-start.1 = (bf16[256,128]{1,0:T(8,128)(2,1)}, bf16[256,128]{1,0:T(8,128)(2,1)S(1)}, u32[]{:S(2)}, u32[]{:S(2)}) collective-permute-start(bf16[256,128]{1,0:T(8,128)(2,1)} %bitcast.11), channel_id=1, source_target_pairs={{0,4},{1,5},{2,6},{3,7},{4,0},{5,1},{6,2},{7,3},{8,12},{9,13},{10,... | collective-permute-start | bytes 196616 | tf_op jit(solution)/shard_map/ppermute | solution.py:33
  5.1 4.5 %collective-permute-start = (bf16[256,128]{1,0:T(8,128)(2,1)}, bf16[256,128]{1,0:T(8,128)(2,1)S(1)}, u32[]{:S(2)}, u32[]{:S(2)}) collective-permute-start(bf16[256,128]{1,0:T(8,128)(2,1)} %bitcast.12), channel_id=1, source_target_pairs={{0,2},{1,3},{2,0},{3,1},{4,6},{5,7},{6,4},{7,5},{8,10},{9,11},{10,... | collective-permute-start | bytes 196616 | tf_op jit(solution)/shard_map/ppermute | solution.py:33
  6.1 3.5 %copy-start.3 = (bf16[2,16384]{1,0:T(2,128)(2,1)S(1)}, bf16[2,16384]{1,0:T(2,128)(2,1)}, u32[]{:S(2)}) copy-start(bf16[2,16384]{1,0:T(2,128)(2,1)} %param.9) | copy-start | bytes 196612
  6.1 5.1 %copy-start = (bf16[16,16384]{1,0:T(8,128)(2,1)S(1)}, bf16[16,16384]{1,0:T(8,128)(2,1)}, u32[]{:S(2)}) copy-start(bf16[16,16384]{1,0:T(8,128)(2,1)} %references.1) | copy-start | bytes 1572868
  6.1 5.1 %copy-start.5 = (s32[512]{0:T(512)S(1)}, s32[512]{0:T(512)}, u32[]{:S(2)}) copy-start(s32[512]{0:T(512)} %param.13) | copy-start | bytes 6148
  6.1 5.1 %copy-start.6 = (s32[512,1]{0,1:T(1,128)S(1)}, s32[512,1]{0,1:T(1,128)}, u32[]{:S(2)}) copy-start(s32[512,1]{0,1:T(1,128)} %param.12) | copy-start | bytes 6148
  6.1 5.1 %copy-start.7 = (f32[256]{0:T(256)S(1)}, f32[256]{0:T(256)}, u32[]{:S(2)}) copy-start(f32[256]{0:T(256)} %param.15) | copy-start | bytes 3076
  6.1 15.4 %copy-start.1 = (bf16[2,192,512]{2,1,0:T(8,128)(2,1)S(1)}, bf16[2,192,512]{2,1,0:T(8,128)(2,1)}, u32[]{:S(2)}) copy-start(bf16[2,192,512]{2,1,0:T(8,128)(2,1)} %constant.12.clone.pick) | copy-start | bytes 1179652
  6.1 27.5 %copy-start.2 = (bf16[384,512]{1,0:T(8,128)(2,1)S(1)}, bf16[384,512]{1,0:T(8,128)(2,1)}, u32[]{:S(2)}) copy-start(bf16[384,512]{1,0:T(8,128)(2,1)} %constant.13.clone.refs_5_) | copy-start | bytes 1179652
  6.1 27.5 %copy-start.4 = (f32[128,128]{1,0:T(8,128)S(1)}, f32[128,128]{1,0:T(8,128)}, u32[]{:S(2)}) copy-start(f32[128,128]{1,0:T(8,128)} %refs_6_.1) | copy-start | bytes 196612
  9.6 1.6 %collective-permute-start.3 = (bf16[4,256,128]{2,1,0:T(8,128)(2,1)S(1)}, bf16[4,256,128]{2,1,0:T(8,128)(2,1)S(1)}, u32[]{:S(2)}, u32[]{:S(2)}) collective-permute-start(bf16[4,256,128]{2,1,0:T(8,128)(2,1)S(1)} %shard_map.105.near), channel_id=1, source_target_pairs={{0,1},{1,0},{2,3},{3,2},{4,5},{5,4},{6,7},{7,6},{8,9},{9,8},{10,11... | collective-permute-start | bytes 786440 | tf_op jit(solution)/shard_map/ppermute | solution.py:33
  14.2 4.8 %collective-permute-start.6 = (f32[32,256]{1,0:T(8,128)S(1)}, f32[32,256]{1,0:T(8,128)S(1)}, u32[]{:S(2)}, u32[]{:S(2)}) collective-permute-start(f32[32,256]{1,0:T(8,128)S(1)} %get-tuple-element.21.refs_0_), channel_id=1, source_target_pairs={{0,6},{1,7},{2,4},{3,5},{4,2},{5,3},{6,0},{7,1},{8,14},{9,15},{10,... | collective-permute-start | bytes 98312 | tf_op jit(solution)/shard_map/ppermute | solution.py:33
  15.7 3.9 %collective-permute-start.5 = (f32[32,256]{1,0:T(8,128)S(1)}, f32[32,256]{1,0:T(8,128)S(1)}, u32[]{:S(2)}, u32[]{:S(2)}) collective-permute-start(f32[32,256]{1,0:T(8,128)S(1)} %get-tuple-element.21.refs_0_), channel_id=1, source_target_pairs={{0,4},{1,5},{2,6},{3,7},{4,0},{5,1},{6,2},{7,3},{8,12},{9,13},{10,... | collective-permute-start | bytes 98312 | tf_op jit(solution)/shard_map/ppermute | solution.py:33
  16.2 3.9 %collective-permute-start.4 = (f32[32,256]{1,0:T(8,128)S(1)}, f32[32,256]{1,0:T(8,128)S(1)}, u32[]{:S(2)}, u32[]{:S(2)}) collective-permute-start(f32[32,256]{1,0:T(8,128)S(1)} %get-tuple-element.21.refs_0_), channel_id=1, source_target_pairs={{0,2},{1,3},{2,0},{3,1},{4,6},{5,7},{6,4},{7,5},{8,10},{9,11},{10,... | collective-permute-start | bytes 98312 | tf_op jit(solution)/shard_map/ppermute | solution.py:33
  20.1 1.4 %collective-permute-start.7 = (f32[4,32,256]{2,1,0:T(8,128)S(1)}, f32[4,32,256]{2,1,0:T(8,128)S(1)}, u32[]{:S(2)}, u32[]{:S(2)}) collective-permute-start(f32[4,32,256]{2,1,0:T(8,128)S(1)} %shard_map.107.near), channel_id=1, source_target_pairs={{0,1},{1,0},{2,3},{3,2},{4,5},{5,4},{6,7},{7,6},{8,9},{9,8},{10,11... | collective-permute-start | bytes 393224 | tf_op jit(solution)/shard_map/ppermute | solution.py:33
  22.5 6.7 %collective-permute-start.8 = (bf16[320,128]{1,0:T(8,128)(2,1)S(1)}, bf16[320,128]{1,0:T(8,128)(2,1)S(1)}, u32[]{:S(2)}, u32[]{:S(2)}) collective-permute-start(bf16[320,128]{1,0:T(8,128)(2,1)S(1)} %get-tuple-element.24), channel_id=1, source_target_pairs={{0,8},{8,0},{16,24},{24,16},{1,9},{9,1},{17,25},{25,17},{2,10},{10... | collective-permute-start | bytes 245768 | tf_op jit(solution)/shard_map/ppermute | solution.py:33
  24.2 9.5 %collective-permute-start.9 = (bf16[320,128]{1,0:T(8,128)(2,1)S(1)}, bf16[320,128]{1,0:T(8,128)(2,1)S(1)}, u32[]{:S(2)}, u32[]{:S(2)}) collective-permute-start(bf16[320,128]{1,0:T(8,128)(2,1)S(1)} %get-tuple-element.25), channel_id=1, source_target_pairs={{0,16},{8,24},{16,0},{24,8},{1,17},{9,25},{17,1},{25,9},{2,18},{10... | collective-permute-start | bytes 245768 | tf_op jit(solution)/shard_map/ppermute | solution.py:33
  26.8 6.9 %collective-permute-start.10 = (bf16[320,128]{1,0:T(8,128)(2,1)S(1)}, bf16[320,128]{1,0:T(8,128)(2,1)S(1)}, u32[]{:S(2)}, u32[]{:S(2)}) collective-permute-start(bf16[320,128]{1,0:T(8,128)(2,1)S(1)} %get-tuple-element.26), channel_id=1, source_target_pairs={{0,24},{8,16},{16,8},{24,0},{1,25},{9,17},{17,9},{25,1},{2,26},{10... | collective-permute-start | bytes 245768 | tf_op jit(solution)/shard_map/ppermute | solution.py:33
  34.6 7.8 %collective-permute-start.13 = (bf16[640,128]{1,0:T(8,128)(2,1)S(1)}, bf16[640,128]{1,0:T(8,128)(2,1)S(1)}, u32[]{:S(2)}, u32[]{:S(2)}) collective-permute-start(bf16[640,128]{1,0:T(8,128)(2,1)S(1)} %get-tuple-element.29.refs_0_), channel_id=1, source_target_pairs={{0,6},{1,7},{2,4},{3,5},{4,2},{5,3},{6,0},{7,1},{8,14},{9,15},{10,... | collective-permute-start | bytes 491528 | tf_op jit(solution)/shard_map/ppermute | solution.py:33
  37.1 6.3 %collective-permute-start.12 = (bf16[640,128]{1,0:T(8,128)(2,1)S(1)}, bf16[640,128]{1,0:T(8,128)(2,1)S(1)}, u32[]{:S(2)}, u32[]{:S(2)}) collective-permute-start(bf16[640,128]{1,0:T(8,128)(2,1)S(1)} %get-tuple-element.29.refs_0_), channel_id=1, source_target_pairs={{0,4},{1,5},{2,6},{3,7},{4,0},{5,1},{6,2},{7,3},{8,12},{9,13},{10,... | collective-permute-start | bytes 491528 | tf_op jit(solution)/shard_map/ppermute | solution.py:33
  37.6 5.8 %collective-permute-start.11 = (bf16[640,128]{1,0:T(8,128)(2,1)S(1)}, bf16[640,128]{1,0:T(8,128)(2,1)S(1)}, u32[]{:S(2)}, u32[]{:S(2)}) collective-permute-start(bf16[640,128]{1,0:T(8,128)(2,1)S(1)} %get-tuple-element.29.refs_0_), channel_id=1, source_target_pairs={{0,2},{1,3},{2,0},{3,1},{4,6},{5,7},{6,4},{7,5},{8,10},{9,11},{10,... | collective-permute-start | bytes 491528 | tf_op jit(solution)/shard_map/ppermute | solution.py:33
  43.4 2.2 %collective-permute-start.14 = (bf16[4,640,128]{2,1,0:T(8,128)(2,1)S(1)}, bf16[4,640,128]{2,1,0:T(8,128)(2,1)S(1)}, u32[]{:S(2)}, u32[]{:S(2)}) collective-permute-start(bf16[4,640,128]{2,1,0:T(8,128)(2,1)S(1)} %shard_map.112.near), channel_id=1, source_target_pairs={{0,1},{1,0},{2,3},{3,2},{4,5},{5,4},{6,7},{7,6},{8,9},{9,8},{10,11... | collective-permute-start | bytes 1966088 | tf_op jit(solution)/shard_map/ppermute | solution.py:33

commit v4 on v3

--- a/solution.py
+++ b/solution.py
@@ -570,38 +570,44 @@
     volume,
     resampled,
     segments,
-    mapped,
+    kernels,
+    bricks,
     result,
+    rows_out,
+    signals,
 ):
     half = near.shape[0]
     shares = 2 * half
     rows = segments.shape[0] // half
-    row_count = volume.shape[0]
-    sub_rows = resampled.shape[0]
-    tiles = resampled.shape[1] // SEGLEN
+    row_count = bricks.shape[1]
+    sub_rows, coef = rows_out.shape
+    tiles = coef // SEGLEN
+    kernels[...] = jnp.zeros(kernels.shape, bf16)
+    for p in range(shares):
+        w = place[0] ^ distance_of(p, shares)
+        at = pl.ds(pl.multiple_of(w % 2 * SEGLEN, SEGLEN), SEGLEN)
+        kernels[w // 2, at, at] = near[p, rows:, :] if p < half else far[p - half, rows:, :]
     inserted = insert(far, half, chosen, parity_lanes, segments) + near_inserted[...]
     inserted = inserted.astype(bf16)
-    kernels = [near[p, rows:, :] for p in range(half)] + [far[p, rows:, :] for p in range(half)]
-    for p in range(shares):
-        mapped_at = place[0] ^ distance_of(p, shares)
-        mapped[mapped_at] = kernels[p]
-    back = []
-    for w in range(shares):
-        kernel = mapped[w]
-        part = inserted[
-            w // 2 * row_count : (w // 2 + 1) * row_count, w % 2 * SEGLEN : (w % 2 + 1) * SEGLEN
-        ]
-        brick = jnp.dot(part, kernel, preferred_element_type=f32) * inverse[:, w : w + 1]
-
-        @pl.when(place[0] == w)
-        def _():
-            volume[...] = brick
-
-        back.append(
-            lax.dot_general(
-                brick.astype(bf16), kernel, LANES, preferred_element_type=f32
-            ).astype(bf16)
+    mapped = []
+    for a in range(half):
+        pair = jnp.dot(
+            inserted[a * row_count : (a + 1) * row_count, :],
+            kernels[a],
+            preferred_element_type=f32,
         )
+        sides = []
+        for w in (2 * a, 2 * a + 1):
+            side = pair[:, w % 2 * SEGLEN : (w % 2 + 1) * SEGLEN] * inverse[:, w : w + 1]
+            bricks[w] = side
+            sides.append(side.astype(bf16))
+        mapped.append(jnp.concatenate(sides, axis=1))
+    own = pltpu.make_async_copy(bricks.at[place[0]], volume, signals.at[0])
+    own.start()
+    back = [
+        lax.dot_general(pair, kernels[a], LANES, preferred_element_type=f32).astype(bf16)
+        for a, pair in enumerate(mapped)
+    ]
     taken = jnp.dot(own_slots[...], jnp.concatenate(back, axis=1), preferred_element_type=f32)
     owner = own_owner_lanes[...].astype(f32)
     total = jnp.zeros((sub_rows * tiles, SEGLEN), f32)
@@ -609,19 +615,23 @@
         total = jnp.where(owner == float(w), taken[:, w * SEGLEN : (w + 1) * SEGLEN], total)
     result[...] = total
     for j in range(tiles):
-        resampled[:, j * SEGLEN : (j + 1) * SEGLEN] = result[pl.ds(j, sub_rows, stride=tiles), :]
-
-
-def call(kernel, inputs, outputs, scratch=(), cost=1.0, small=(), space=pltpu.VMEM, room=24):
+        rows_out[:, j * SEGLEN : (j + 1) * SEGLEN] = result[pl.ds(j, sub_rows, stride=tiles), :]
+    back_again = pltpu.make_async_copy(rows_out, resampled, signals.at[1])
+    back_again.start()
+    own.wait()
+    back_again.wait()
+
+
+def call(kernel, inputs, outputs, scratch=(), cost=1.0, small=(), out_space=pltpu.VMEM):
     inside = pl.BlockSpec(memory_space=pltpu.VMEM)
     scalars = pl.BlockSpec(memory_space=pltpu.SMEM)
     return pl.pallas_call(
         kernel,
         out_shape=[jax.ShapeDtypeStruct(shape, dtype) for shape, dtype in outputs],
-        in_specs=[pl.BlockSpec(memory_space=space)] * len(inputs) + [scalars] * len(small),
-        out_specs=[inside] * len(outputs),
+        in_specs=[inside] * len(inputs) + [scalars] * len(small),
+        out_specs=[pl.BlockSpec(memory_space=out_space)] * len(outputs),
         scratch_shapes=list(scratch),
-        compiler_params=pltpu.CompilerParams(vmem_limit_bytes=room * 2**20),
+        compiler_params=pltpu.CompilerParams(vmem_limit_bytes=24 * 2**20),
         cost_estimate=pl.CostEstimate(
             flops=int(cost * 1.15e9), bytes_accessed=0, transcendentals=0
         ),
@@ -748,11 +758,15 @@
         (((row_count, SEGLEN), f32), ((sub_rows, coef), f32)),
         scratch=(
             masked,
-            pltpu.VMEM((ori_count, SEGLEN, SEGLEN), bf16),
+            pltpu.VMEM((half, 2 * SEGLEN, 2 * SEGLEN), bf16),
+            pltpu.VMEM((ori_count, row_count, SEGLEN), f32),
             pltpu.VMEM((sub_rows * tiles, SEGLEN), f32),
+            pltpu.VMEM((sub_rows, coef), f32),
+            pltpu.SemaphoreType.DMA((2,)),
         ),
         small=(place,),
         cost=COST_VOLUME,
+        out_space=pl.ANY,
     )
     return (volume, resampled)
 

time: 51.3 us -> 50.1 us (0.977)
  Pallas kernels: 19.4 us -> 18.2 us
    pallas_call x11, Pallas kernels: 19.4 us -> 18.2 us  [call(): pl.pallas_call(kernel, out_shape=[jax.ShapeDtypeStruct(shape, dtype) for...]
where the time goes in v4:
time: 50.1 us; the launch traced here: 49.9 us
  Pallas kernels  18.2 us (36%)
  starting transfers between devices  16.3 us (33%)
  waiting for transfers between devices  13.6 us (27%)
  local copies, waits for them, and re-layouts  0.81 us (2%)
  between operations  0.8 us (2%)
    pallas_call x11, Pallas kernels, call(): pl.pallas_call(kernel, out_shape=[jax.ShapeDtypeStruct(shape, dtype) for...  18.2 us
    ppermute x15, starting transfers between devices, hop(): return lax.ppermute(value, axis, pairs)  16.3 us
    ppermute x15, waiting for transfers between devices, hop(): return lax.ppermute(value, axis, pairs)  13.6 us
  transfers between devices with their start and end apart: 15, of which 10 were waited for; matrix products, arithmetic and copies ran while one was open for 2% of the time, Pallas kernels for 18%

profile of v4, /device:TPU:0, one launch (start us, length us, event | category | flops | bytes accessed | tf_op | source)
XLA Modules:
  0.0 49.9 jit_solution(3400707758576970151)
XLA Ops:
  0.6 4.0 %collective-permute-start.2 = (bf16[256,128]{1,0:T(8,128)(2,1)}, bf16[256,128]{1,0:T(8,128)(2,1)S(1)}, u32[]{:S(2)}, u32[]{:S(2)}) collective-permute-start(bf16[256,128]{1,0:T(8,128)(2,1)} %bitcast.10), channel_id=1, source_target_pairs={{0,6},{1,7},{2,4},{3,5},{4,2},{5,3},{6,0},{7,1},{8,14},{9,15},{10,... | collective-permute-start | bytes 196616 | tf_op jit(solution)/shard_map/ppermute | solution.py:33
  4.6 0.5 %collective-permute-start.1 = (bf16[256,128]{1,0:T(8,128)(2,1)}, bf16[256,128]{1,0:T(8,128)(2,1)S(1)}, u32[]{:S(2)}, u32[]{:S(2)}) collective-permute-start(bf16[256,128]{1,0:T(8,128)(2,1)} %bitcast.11), channel_id=1, source_target_pairs={{0,4},{1,5},{2,6},{3,7},{4,0},{5,1},{6,2},{7,3},{8,12},{9,13},{10,... | collective-permute-start | bytes 196616 | tf_op jit(solution)/shard_map/ppermute | solution.py:33
  5.1 0.1 collective-permute-start
  5.2 0.8 %copy.12.shifts = f32[12,2]{1,0:T(8,128)S(1)} copy(f32[12,2]{0,1:T(2,128)} %param.11) | data formatting | bytes 192 | tf_op args[2]
  6.0 0.1 pad_add_fusion.place
  6.1 0.0 copy-start.7
  6.1 0.0 copy-start.1
  6.1 0.0 copy-start.2
  6.1 0.0 copy-start.4
  6.1 0.9 %shard_map.104 = (f32[2,2,16,256]{3,2,1,0:T(8,128)S(1)}, f32[2,16,1024]{2,1,0:T(8,128)S(1)}) custom-call(f32[12,2]{1,0:T(8,128)S(1)} %copy.12.shifts, s32[2]{0:T(128)S(1)} %pad_add_fusion.place), custom_call_target="tpu_custom_call" | custom-call | flops 13799999488 | tf_op jit(solution)/shard_map/pallas_call | solution.py:628
  7.1 0.0 collective-permute-done.2.refs_3_
  7.1 2.0 %collective-permute-done.1.refs_2_ = bf16[256,128]{1,0:T(8,128)(2,1)S(1)} collective-permute-done((bf16[256,128]{1,0:T(8,128)(2,1)}, bf16[256,128]{1,0:T(8,128)(2,1)S(1)}, u32[]{:S(2)}, u32[]{:S(2)}) %collective-permute-start.1) | collective-permute-done | bytes 65568 | tf_op jit(solution)/shard_map/ppermute | solution.py:33
  9.1 0.5 %collective-permute-done.refs_1_ = bf16[256,128]{1,0:T(8,128)(2,1)S(1)} collective-permute-done((bf16[256,128]{1,0:T(8,128)(2,1)}, bf16[256,128]{1,0:T(8,128)(2,1)S(1)}, u32[]{:S(2)}, u32[]{:S(2)}) %collective-permute-start) | collective-permute-done | bytes 65568 | tf_op jit(solution)/shard_map/ppermute | solution.py:33
  9.6 0.0 copy-done.3
  9.6 0.1 collective-permute-start.3
  9.7 1.5 %collective-permute-done.3.far = bf16[4,256,128]{2,1,0:T(8,128)(2,1)S(1)} collective-permute-done((bf16[4,256,128]{2,1,0:T(8,128)(2,1)S(1)}, bf16[4,256,128]{2,1,0:T(8,128)(2,1)S(1)}, u32[]{:S(2)}, u32[]{:S(2)}) %collective-permute-start.3) | collective-permute-done | bytes 262176 | tf_op jit(solution)/shard_map/ppermute | solution.py:33
  11.2 0.0 copy-done.6
  11.2 0.0 copy-done.7
  11.2 3.0 %shard_map.106 = (f32[32,256]{1,0:T(8,128)S(1)}, bf16[256,128]{1,0:T(8,128)(2,1)S(1)}) custom-call(bf16[4,256,128]{2,1,0:T(8,128)(2,1)S(1)} %shard_map.105.near, bf16[4,256,128]{2,1,0:T(8,128)(2,1)S(1)} %collective-permute-done.3.far, bf16[16,16384]{1,0:T(8,128)(2,1)S(1)} %copy-done, f32[2,2,16,256]{3,2,1,0:T(8,128)S(1)} %get-tuple-element.20.refs_4_.phases, ...), custom_call_target="tpu_custom_call" | custom-call | flops 1150000 | tf_op jit(solution)/shard_map/pallas_call | solution.py:628
  14.2 1.5 %collective-permute-start.6 = (f32[32,256]{1,0:T(8,128)S(1)}, f32[32,256]{1,0:T(8,128)S(1)}, u32[]{:S(2)}, u32[]{:S(2)}) collective-permute-start(f32[32,256]{1,0:T(8,128)S(1)} %get-tuple-element.21.refs_0_), channel_id=1, source_target_pairs={{0,6},{1,7},{2,4},{3,5},{4,2},{5,3},{6,0},{7,1},{8,14},{9,15},{10,... | collective-permute-start | bytes 98312 | tf_op jit(solution)/shard_map/ppermute | solution.py:33
  15.7 0.4 collective-permute-start.5
  16.2 1.6 %collective-permute-start.4 = (f32[32,256]{1,0:T(8,128)S(1)}, f32[32,256]{1,0:T(8,128)S(1)}, u32[]{:S(2)}, u32[]{:S(2)}) collective-permute-start(f32[32,256]{1,0:T(8,128)S(1)} %get-tuple-element.21.refs_0_), channel_id=1, source_target_pairs={{0,2},{1,3},{2,0},{3,1},{4,6},{5,7},{6,4},{7,5},{8,10},{9,11},{10,... | collective-permute-start | bytes 98312 | tf_op jit(solution)/shard_map/ppermute | solution.py:33
  17.7 1.3 %collective-permute-done.6.refs_3_ = f32[32,256]{1,0:T(8,128)S(1)} collective-permute-done((f32[32,256]{1,0:T(8,128)S(1)}, f32[32,256]{1,0:T(8,128)S(1)}, u32[]{:S(2)}, u32[]{:S(2)}) %collective-permute-start.6) | collective-permute-done | bytes 32800 | tf_op jit(solution)/shard_map/ppermute | solution.py:33
  19.1 0.6 %collective-permute-done.5.refs_2_ = f32[32,256]{1,0:T(8,128)S(1)} collective-permute-done((f32[32,256]{1,0:T(8,128)S(1)}, f32[32,256]{1,0:T(8,128)S(1)}, u32[]{:S(2)}, u32[]{:S(2)}) %collective-permute-start.5) | collective-permute-done | bytes 32800 | tf_op jit(solution)/shard_map/ppermute | solution.py:33
  19.6 0.4 collective-permute-done.4.refs_1_
  20.1 0.1 collective-permute-start.7
  20.2 1.3 %collective-permute-done.7.far = f32[4,32,256]{2,1,0:T(8,128)S(1)} collective-permute-done((f32[4,32,256]{2,1,0:T(8,128)S(1)}, f32[4,32,256]{2,1,0:T(8,128)S(1)}, u32[]{:S(2)}, u32[]{:S(2)}) %collective-permute-start.7) | collective-permute-done | bytes 131104 | tf_op jit(solution)/shard_map/ppermute | solution.py:33
  21.5 0.9 %shard_map.108 = (bf16[320,128]{1,0:T(8,128)(2,1)S(1)}, bf16[320,128]{1,0:T(8,128)(2,1)S(1)}, bf16[320,128]{1,0:T(8,128)(2,1)S(1)}, bf16[320,128]{1,0:T(8,128)(2,1)S(1)}) custom-call(f32[4,32,256]{2,1,0:T(8,128)S(1)} %shard_map.107.near, f32[4,32,256]{2,1,0:T(8,128)S(1)} %collective-permute-done.7.far, bf16[2,192,512]{2,1,0:T(8,128)(2,1)S(1)} %copy-done.1, ...), custom_call_target="tpu_custom_call" | custom-call | flops 1150000 | tf_op jit(solution)/shard_map/pallas_call | solution.py:628
  22.5 1.7 %collective-permute-start.8 = (bf16[320,128]{1,0:T(8,128)(2,1)S(1)}, bf16[320,128]{1,0:T(8,128)(2,1)S(1)}, u32[]{:S(2)}, u32[]{:S(2)}) collective-permute-start(bf16[320,128]{1,0:T(8,128)(2,1)S(1)} %get-tuple-element.24), channel_id=1, source_target_pairs={{0,8},{8,0},{16,24},{24,16},{1,9},{9,1},{17,25},{25,17},{2,10},{10... | collective-permute-start | bytes 245768 | tf_op jit(solution)/shard_map/ppermute | solution.py:33
  24.2 2.6 %collective-permute-start.9 = (bf16[320,128]{1,0:T(8,128)(2,1)S(1)}, bf16[320,128]{1,0:T(8,128)(2,1)S(1)}, u32[]{:S(2)}, u32[]{:S(2)}) collective-permute-start(bf16[320,128]{1,0:T(8,128)(2,1)S(1)} %get-tuple-element.25), channel_id=1, source_target_pairs={{0,16},{8,24},{16,0},{24,8},{1,17},{9,25},{17,1},{25,9},{2,18},{10... | collective-permute-start | bytes 245768 | tf_op jit(solution)/shard_map/ppermute | solution.py:33
  26.8 0.2 collective-permute-start.10
  26.9 2.2 %shard_map.109 = (bf16[4096,128]{1,0:T(8,128)(2,1)S(1)}, bf16[256,256]{1,0:T(8,128)(2,1)S(1)}, f32[256,8]{1,0:T(8,128)S(1)}) custom-call(f32[4,32,256]{2,1,0:T(8,128)S(1)} %shard_map.107.near, f32[4,32,256]{2,1,0:T(8,128)S(1)} %collective-permute-done.7.far, bf16[320,128]{1,0:T(8,128)(2,1)S(1)} %get-tuple-element.23.after.refs_0_, s32[2]{0:T(128)S(1)} %pad_add_fusion.place), custom_call_target="tpu_custom_call" | custom-call | flops 1150000 | tf_op jit(solution)/shard_map/pallas_call | solution.py:628
  29.1 0.0 collective-permute-done.8.refs_1_
  29.1 4.5 %collective-permute-done.9.refs_2_ = bf16[320,128]{1,0:T(8,128)(2,1)S(1)} collective-permute-done((bf16[320,128]{1,0:T(8,128)(2,1)S(1)}, bf16[320,128]{1,0:T(8,128)(2,1)S(1)}, u32[]{:S(2)}, u32[]{:S(2)}) %collective-permute-start.9) | collective-permute-done | bytes 81952 | tf_op jit(solution)/shard_map/ppermute | solution.py:33
  33.6 0.0 collective-permute-done.10.refs_3_
  33.6 0.0 copy-done.2
  33.7 0.9 %shard_map.110 = (bf16[640,128]{1,0:T(8,128)(2,1)S(1)}, f32[32,128]{1,0:T(8,128)S(1)}) custom-call(bf16[320,128]{1,0:T(8,128)(2,1)S(1)} %get-tuple-element.23.after.refs_0_, bf16[320,128]{1,0:T(8,128)(2,1)S(1)} %collective-permute-done.8.refs_1_, bf16[320,128]{1,0:T(8,128)(2,1)S(1)} %collective-permute-done.9.refs_2_, ...), custom_call_target="tpu_custom_call" | custom-call | flops 1150000 | tf_op jit(solution)/shard_map/pallas_call | solution.py:628
  34.6 2.5 %collective-permute-start.13 = (bf16[640,128]{1,0:T(8,128)(2,1)S(1)}, bf16[640,128]{1,0:T(8,128)(2,1)S(1)}, u32[]{:S(2)}, u32[]{:S(2)}) collective-permute-start(bf16[640,128]{1,0:T(8,128)(2,1)S(1)} %get-tuple-element.29.refs_0_), channel_id=1, source_target_pairs={{0,6},{1,7},{2,4},{3,5},{4,2},{5,3},{6,0},{7,1},{8,14},{9,15},{10,... | collective-permute-start | bytes 491528 | tf_op jit(solution)/shard_map/ppermute | solution.py:33
  37.1 0.5 %collective-permute-start.12 = (bf16[640,128]{1,0:T(8,128)(2,1)S(1)}, bf16[640,128]{1,0:T(8,128)(2,1)S(1)}, u32[]{:S(2)}, u32[]{:S(2)}) collective-permute-start(bf16[640,128]{1,0:T(8,128)(2,1)S(1)} %get-tuple-element.29.refs_0_), channel_id=1, source_target_pairs={{0,4},{1,5},{2,6},{3,7},{4,0},{5,1},{6,2},{7,3},{8,12},{9,13},{10,... | collective-permute-start | bytes 491528 | tf_op jit(solution)/shard_map/ppermute | solution.py:33
  37.6 0.5 %collective-permute-start.11 = (bf16[640,128]{1,0:T(8,128)(2,1)S(1)}, bf16[640,128]{1,0:T(8,128)(2,1)S(1)}, u32[]{:S(2)}, u32[]{:S(2)}) collective-permute-start(bf16[640,128]{1,0:T(8,128)(2,1)S(1)} %get-tuple-element.29.refs_0_), channel_id=1, source_target_pairs={{0,2},{1,3},{2,0},{3,1},{4,6},{5,7},{6,4},{7,5},{8,10},{9,11},{10,... | collective-permute-start | bytes 491528 | tf_op jit(solution)/shard_map/ppermute | solution.py:33
  38.1 4.3 %shard_map.111 = (bf16[1024,4096]{1,0:T(8,128)(2,1)S(1)}, bf16[512,256]{1,0:T(8,128)(2,1)S(1)}, bf16[512,128]{1,0:T(8,128)(2,1)S(1)}) custom-call(f32[4,32,256]{2,1,0:T(8,128)S(1)} %shard_map.107.near, f32[4,32,256]{2,1,0:T(8,128)S(1)} %collective-permute-done.7.far, f32[32,128]{1,0:T(8,128)S(1)} %get-tuple-element.30.after.masses, s32[2]{0:T(128)S(1)} %pad_add_fusion.place), custom_call_target="tpu_custom_call" | custom-call | flops 1150000 | tf_op jit(solution)/shard_map/pallas_call | solution.py:628
  42.4 0.0 collective-permute-done.13.refs_3_
  42.4 0.9 %collective-permute-done.12.refs_2_ = bf16[640,128]{1,0:T(8,128)(2,1)S(1)} collective-permute-done((bf16[640,128]{1,0:T(8,128)(2,1)S(1)}, bf16[640,128]{1,0:T(8,128)(2,1)S(1)}, u32[]{:S(2)}, u32[]{:S(2)}) %collective-permute-start.12) | collective-permute-done | bytes 163872 | tf_op jit(solution)/shard_map/ppermute | solution.py:33
  43.3 0.0 collective-permute-done.11.refs_1_
  43.4 0.1 collective-permute-start.14
  43.5 1.6 %shard_map.113 = (f32[1024,256]{1,0:T(8,128)S(1)}, f32[256,8]{1,0:T(8,128)S(1)}) custom-call(bf16[4,640,128]{2,1,0:T(8,128)(2,1)S(1)} %shard_map.112.near, bf16[1024,4096]{1,0:T(8,128)(2,1)S(1)} %get-tuple-element.32.chosen, bf16[4096,128]{1,0:T(8,128)(2,1)S(1)} %get-tuple-element.33.parity_lanes, bf16[256,256]{1,0:T(8,128)(2,1)S(1)} %get-tuple-element.34.counts, ...), custom_call_target="tpu_custom_call" | custom-call | flops 1150000 | tf_op jit(solution)/shard_map/pallas_call | solution.py:628
  45.0 0.5 %collective-permute-done.14.far = bf16[4,640,128]{2,1,0:T(8,128)(2,1)S(1)} collective-permute-done((bf16[4,640,128]{2,1,0:T(8,128)(2,1)S(1)}, bf16[4,640,128]{2,1,0:T(8,128)(2,1)S(1)}, u32[]{:S(2)}, u32[]{:S(2)}) %collective-permute-start.14) | collective-permute-done | bytes 655392 | tf_op jit(solution)/shard_map/ppermute | solution.py:33
  45.6 4.3 %shard_map.114 = (f32[256,128]{1,0:T(8,128)}, f32[4,16384]{1,0:T(4,128)}) custom-call(bf16[4,640,128]{2,1,0:T(8,128)(2,1)S(1)} %shard_map.112.near, bf16[4,640,128]{2,1,0:T(8,128)(2,1)S(1)} %collective-permute-done.14.far, f32[1024,256]{1,0:T(8,128)S(1)} %get-tuple-element.35.near_inserted, bf16[1024,4096]{1,0:T(8,128)(2,1)S(1)} %get-tuple-element.32.chosen, ...), custom_call_target="tpu_custom_call" | custom-call | flops 1150000 | tf_op jit(solution)/shard_map/pallas_call | solution.py:628
  (11 shorter events, 0.1 us)
Async XLA Ops:
  0.6 6.5 %collective-permute-start.2 = (bf16[256,128]{1,0:T(8,128)(2,1)}, bf16[256,128]{1,0:T(8,128)(2,1)S(1)}, u32[]{:S(2)}, u32[]{:S(2)}) collective-permute-start(bf16[256,128]{1,0:T(8,128)(2,1)} %bitcast.10), channel_id=1, source_target_pairs={{0,6},{1,7},{2,4},{3,5},{4,2},{5,3},{6,0},{7,1},{8,14},{9,15},{10,... | collective-permute-start | bytes 196616 | tf_op jit(solution)/shard_map/ppermute | solution.py:33
  4.6 4.5 %collective-permute-start.1 = (bf16[256,128]{1,0:T(8,128)(2,1)}, bf16[256,128]{1,0:T(8,128)(2,1)S(1)}, u32[]{:S(2)}, u32[]{:S(2)}) collective-permute-start(bf16[256,128]{1,0:T(8,128)(2,1)} %bitcast.11), channel_id=1, source_target_pairs={{0,4},{1,5},{2,6},{3,7},{4,0},{5,1},{6,2},{7,3},{8,12},{9,13},{10,... | collective-permute-start | bytes 196616 | tf_op jit(solution)/shard_map/ppermute | solution.py:33
  5.1 4.5 %collective-permute-start = (bf16[256,128]{1,0:T(8,128)(2,1)}, bf16[256,128]{1,0:T(8,128)(2,1)S(1)}, u32[]{:S(2)}, u32[]{:S(2)}) collective-permute-start(bf16[256,128]{1,0:T(8,128)(2,1)} %bitcast.12), channel_id=1, source_target_pairs={{0,2},{1,3},{2,0},{3,1},{4,6},{5,7},{6,4},{7,5},{8,10},{9,11},{10,... | collective-permute-start | bytes 196616 | tf_op jit(solution)/shard_map/ppermute | solution.py:33
  6.1 3.5 %copy-start.3 = (bf16[2,16384]{1,0:T(2,128)(2,1)S(1)}, bf16[2,16384]{1,0:T(2,128)(2,1)}, u32[]{:S(2)}) copy-start(bf16[2,16384]{1,0:T(2,128)(2,1)} %param.9) | copy-start | bytes 196612
  6.1 5.1 %copy-start = (bf16[16,16384]{1,0:T(8,128)(2,1)S(1)}, bf16[16,16384]{1,0:T(8,128)(2,1)}, u32[]{:S(2)}) copy-start(bf16[16,16384]{1,0:T(8,128)(2,1)} %references.1) | copy-start | bytes 1572868
  6.1 5.1 %copy-start.5 = (s32[512]{0:T(512)S(1)}, s32[512]{0:T(512)}, u32[]{:S(2)}) copy-start(s32[512]{0:T(512)} %param.13) | copy-start | bytes 6148
  6.1 5.1 %copy-start.6 = (s32[512,1]{0,1:T(1,128)S(1)}, s32[512,1]{0,1:T(1,128)}, u32[]{:S(2)}) copy-start(s32[512,1]{0,1:T(1,128)} %param.12) | copy-start | bytes 6148
  6.1 5.1 %copy-start.7 = (f32[256]{0:T(256)S(1)}, f32[256]{0:T(256)}, u32[]{:S(2)}) copy-start(f32[256]{0:T(256)} %param.15) | copy-start | bytes 3076
  6.1 15.4 %copy-start.1 = (bf16[2,192,512]{2,1,0:T(8,128)(2,1)S(1)}, bf16[2,192,512]{2,1,0:T(8,128)(2,1)}, u32[]{:S(2)}) copy-start(bf16[2,192,512]{2,1,0:T(8,128)(2,1)} %constant.12.clone.pick) | copy-start | bytes 1179652
  6.1 27.5 %copy-start.2 = (bf16[384,512]{1,0:T(8,128)(2,1)S(1)}, bf16[384,512]{1,0:T(8,128)(2,1)}, u32[]{:S(2)}) copy-start(bf16[384,512]{1,0:T(8,128)(2,1)} %constant.13.clone.refs_5_) | copy-start | bytes 1179652
  6.1 27.5 %copy-start.4 = (f32[128,128]{1,0:T(8,128)S(1)}, f32[128,128]{1,0:T(8,128)}, u32[]{:S(2)}) copy-start(f32[128,128]{1,0:T(8,128)} %refs_6_.1) | copy-start | bytes 196612
  9.6 1.6 %collective-permute-start.3 = (bf16[4,256,128]{2,1,0:T(8,128)(2,1)S(1)}, bf16[4,256,128]{2,1,0:T(8,128)(2,1)S(1)}, u32[]{:S(2)}, u32[]{:S(2)}) collective-permute-start(bf16[4,256,128]{2,1,0:T(8,128)(2,1)S(1)} %shard_map.105.near), channel_id=1, source_target_pairs={{0,1},{1,0},{2,3},{3,2},{4,5},{5,4},{6,7},{7,6},{8,9},{9,8},{10,11... | collective-permute-start | bytes 786440 | tf_op jit(solution)/shard_map/ppermute | solution.py:33
  14.2 4.8 %collective-permute-start.6 = (f32[32,256]{1,0:T(8,128)S(1)}, f32[32,256]{1,0:T(8,128)S(1)}, u32[]{:S(2)}, u32[]{:S(2)}) collective-permute-start(f32[32,256]{1,0:T(8,128)S(1)} %get-tuple-element.21.refs_0_), channel_id=1, source_target_pairs={{0,6},{1,7},{2,4},{3,5},{4,2},{5,3},{6,0},{7,1},{8,14},{9,15},{10,... | collective-permute-start | bytes 98312 | tf_op jit(solution)/shard_map/ppermute | solution.py:33
  15.7 3.9 %collective-permute-start.5 = (f32[32,256]{1,0:T(8,128)S(1)}, f32[32,256]{1,0:T(8,128)S(1)}, u32[]{:S(2)}, u32[]{:S(2)}) collective-permute-start(f32[32,256]{1,0:T(8,128)S(1)} %get-tuple-element.21.refs_0_), channel_id=1, source_target_pairs={{0,4},{1,5},{2,6},{3,7},{4,0},{5,1},{6,2},{7,3},{8,12},{9,13},{10,... | collective-permute-start | bytes 98312 | tf_op jit(solution)/shard_map/ppermute | solution.py:33
  16.2 3.9 %collective-permute-start.4 = (f32[32,256]{1,0:T(8,128)S(1)}, f32[32,256]{1,0:T(8,128)S(1)}, u32[]{:S(2)}, u32[]{:S(2)}) collective-permute-start(f32[32,256]{1,0:T(8,128)S(1)} %get-tuple-element.21.refs_0_), channel_id=1, source_target_pairs={{0,2},{1,3},{2,0},{3,1},{4,6},{5,7},{6,4},{7,5},{8,10},{9,11},{10,... | collective-permute-start | bytes 98312 | tf_op jit(solution)/shard_map/ppermute | solution.py:33
  20.1 1.4 %collective-permute-start.7 = (f32[4,32,256]{2,1,0:T(8,128)S(1)}, f32[4,32,256]{2,1,0:T(8,128)S(1)}, u32[]{:S(2)}, u32[]{:S(2)}) collective-permute-start(f32[4,32,256]{2,1,0:T(8,128)S(1)} %shard_map.107.near), channel_id=1, source_target_pairs={{0,1},{1,0},{2,3},{3,2},{4,5},{5,4},{6,7},{7,6},{8,9},{9,8},{10,11... | collective-permute-start | bytes 393224 | tf_op jit(solution)/shard_map/ppermute | solution.py:33
  22.5 6.7 %collective-permute-start.8 = (bf16[320,128]{1,0:T(8,128)(2,1)S(1)}, bf16[320,128]{1,0:T(8,128)(2,1)S(1)}, u32[]{:S(2)}, u32[]{:S(2)}) collective-permute-start(bf16[320,128]{1,0:T(8,128)(2,1)S(1)} %get-tuple-element.24), channel_id=1, source_target_pairs={{0,8},{8,0},{16,24},{24,16},{1,9},{9,1},{17,25},{25,17},{2,10},{10... | collective-permute-start | bytes 245768 | tf_op jit(solution)/shard_map/ppermute | solution.py:33
  24.2 9.5 %collective-permute-start.9 = (bf16[320,128]{1,0:T(8,128)(2,1)S(1)}, bf16[320,128]{1,0:T(8,128)(2,1)S(1)}, u32[]{:S(2)}, u32[]{:S(2)}) collective-permute-start(bf16[320,128]{1,0:T(8,128)(2,1)S(1)} %get-tuple-element.25), channel_id=1, source_target_pairs={{0,16},{8,24},{16,0},{24,8},{1,17},{9,25},{17,1},{25,9},{2,18},{10... | collective-permute-start | bytes 245768 | tf_op jit(solution)/shard_map/ppermute | solution.py:33
  26.8 6.9 %collective-permute-start.10 = (bf16[320,128]{1,0:T(8,128)(2,1)S(1)}, bf16[320,128]{1,0:T(8,128)(2,1)S(1)}, u32[]{:S(2)}, u32[]{:S(2)}) collective-permute-start(bf16[320,128]{1,0:T(8,128)(2,1)S(1)} %get-tuple-element.26), channel_id=1, source_target_pairs={{0,24},{8,16},{16,8},{24,0},{1,25},{9,17},{17,9},{25,1},{2,26},{10... | collective-permute-start | bytes 245768 | tf_op jit(solution)/shard_map/ppermute | solution.py:33
  34.6 7.8 %collective-permute-start.13 = (bf16[640,128]{1,0:T(8,128)(2,1)S(1)}, bf16[640,128]{1,0:T(8,128)(2,1)S(1)}, u32[]{:S(2)}, u32[]{:S(2)}) collective-permute-start(bf16[640,128]{1,0:T(8,128)(2,1)S(1)} %get-tuple-element.29.refs_0_), channel_id=1, source_target_pairs={{0,6},{1,7},{2,4},{3,5},{4,2},{5,3},{6,0},{7,1},{8,14},{9,15},{10,... | collective-permute-start | bytes 491528 | tf_op jit(solution)/shard_map/ppermute | solution.py:33
  37.1 6.3 %collective-permute-start.12 = (bf16[640,128]{1,0:T(8,128)(2,1)S(1)}, bf16[640,128]{1,0:T(8,128)(2,1)S(1)}, u32[]{:S(2)}, u32[]{:S(2)}) collective-permute-start(bf16[640,128]{1,0:T(8,128)(2,1)S(1)} %get-tuple-element.29.refs_0_), channel_id=1, source_target_pairs={{0,4},{1,5},{2,6},{3,7},{4,0},{5,1},{6,2},{7,3},{8,12},{9,13},{10,... | collective-permute-start | bytes 491528 | tf_op jit(solution)/shard_map/ppermute | solution.py:33
  37.6 5.8 %collective-permute-start.11 = (bf16[640,128]{1,0:T(8,128)(2,1)S(1)}, bf16[640,128]{1,0:T(8,128)(2,1)S(1)}, u32[]{:S(2)}, u32[]{:S(2)}) collective-permute-start(bf16[640,128]{1,0:T(8,128)(2,1)S(1)} %get-tuple-element.29.refs_0_), channel_id=1, source_target_pairs={{0,2},{1,3},{2,0},{3,1},{4,6},{5,7},{6,4},{7,5},{8,10},{9,11},{10,... | collective-permute-start | bytes 491528 | tf_op jit(solution)/shard_map/ppermute | solution.py:33
  43.4 2.2 %collective-permute-start.14 = (bf16[4,640,128]{2,1,0:T(8,128)(2,1)S(1)}, bf16[4,640,128]{2,1,0:T(8,128)(2,1)S(1)}, u32[]{:S(2)}, u32[]{:S(2)}) collective-permute-start(bf16[4,640,128]{2,1,0:T(8,128)(2,1)S(1)} %shard_map.112.near), channel_id=1, source_target_pairs={{0,1},{1,0},{2,3},{3,2},{4,5},{5,4},{6,7},{7,6},{8,9},{9,8},{10,11... | collective-permute-start | bytes 1966088 | tf_op jit(solution)/shard_map/ppermute | solution.py:33

commit v5 on v4

--- a/solution.py
+++ b/solution.py
@@ -18,9 +18,8 @@
 COST_SCORE = 0.001
 COST_WEIGHT = 0.001
 COST_STACK = 0.001
-COST_FETCH = 0.001
-COST_CHOICE = 0.001
-COST_COUNT = 0.001
+COST_BESIDE = 30.0
+COST_FACT = 0.001
 COST_SLICE = 0.001
 COST_NEAR = 0.001
 COST_VOLUME = 0.001
@@ -208,7 +207,7 @@
     parts += [hop(value, "ori", k) for k in even_distances()]
     (near,) = call(
         functools.partial(stack_kernel, len(parts)),
-        (*parts, *after),
+        (*reversed(parts), *after),
         (((len(parts), *value.shape), value.dtype),),
         cost=COST_STACK,
     )
@@ -217,7 +216,7 @@
 
 def stack_kernel(count, *refs):
     for place in range(count):
-        refs[-1][place] = refs[place][...]
+        refs[-1][count - 1 - place] = refs[place][...]
 
 
 def phase_kernel(shifts, place, phases, tables):
@@ -280,9 +279,9 @@
     far,
     references,
     phases,
+    pick,
     slots,
     owners,
-    regularizer,
     place,
     message,
     piece,
@@ -324,57 +323,75 @@
     total = lax.fori_loop(
         0, half_len // CHUNK, step, jnp.zeros((columns, group_rows), f32), unroll=True
     )
-    message[...] = jnp.zeros(message.shape, f32)
-    message[:group_rows, :columns] = jnp.swapaxes(total, 0, 1) * (2.0 / math.sqrt(coef))
-    row = group_rows
-    for fact in (slots, owners, regularizer):
-        message[row : row + fact.shape[0], :SEGLEN] = fact[...].astype(f32)
-        row += fact.shape[0]
-
-
-def in_order(near, far, place, rows, out):
-    half = near.shape[0]
-    for p in range(2 * half):
-        part = near[p, rows, :] if p < half else far[p - half, rows, :]
-        out[place[0] ^ distance_of(p, 2 * half)] = part
-
-
-def weight_kernel(group_rows, columns, near, far, pick, piece, place, *refs):
-    *messages, scores, picked = refs
-    shares = scores.shape[0]
-    half = shares // 2
-    in_order(near, far, place, slice(0, group_rows), scores)
-    parts = [scores[p, :, :columns] for p in range(shares)]
-    peak = jnp.max(parts[0], axis=1, keepdims=True)
-    for part in parts[1:]:
-        peak = jnp.maximum(peak, jnp.max(part, axis=1, keepdims=True))
-    exponents = [jnp.exp(part - peak) for part in parts]
-    total = sum(jnp.sum(part, axis=1, keepdims=True) for part in exponents)
-    weights = [(part / total).astype(bf16) for part in exponents]
-    picked[...] = jnp.dot(
-        jnp.concatenate(weights[:half], axis=0), pick[0], preferred_element_type=f32
-    ) + jnp.dot(jnp.concatenate(weights[half:], axis=0), pick[1], preferred_element_type=f32)
-    for k, message in enumerate(messages):
-        lanes = pl.ds(pl.multiple_of((place[1] ^ k) * SEGLEN, SEGLEN), SEGLEN)
-        message[: picked.shape[0], :] = picked[:, lanes].astype(bf16)
-        message[picked.shape[0] :, :] = piece[...]
-
-
-def flat_facts(group_rows, sub_rows, near, far, place, reg_rows, ordered, upright, flat):
-    shares = ordered.shape[0]
+    scores = jnp.swapaxes(total, 0, 1) * (2.0 / math.sqrt(coef))
+    peak = jnp.max(scores, axis=1, keepdims=True)
+    exponents = jnp.exp(scores - peak)
+    total = jnp.sum(exponents, axis=1, keepdims=True)
+    picked = jnp.dot(exponents.astype(bf16), pick[...], preferred_element_type=f32)
+    blocks = pick.shape[1] // SEGLEN
+    shares = message.shape[0] // blocks
+    valid = columns // blocks
+    lane = iota((group_rows, SEGLEN), 1)
+    rest = jnp.concatenate(
+        [
+            part
+            for fact in (slots, owners)
+            for part in (
+                pltpu.roll(fact[...].astype(f32), SEGLEN // 2, 1),
+                fact[...].astype(f32),
+            )
+        ],
+        axis=0,
+    )
+    at = valid
+    for value in (peak, total):
+        for _ in range(3):
+            part = value.astype(bf16).astype(f32)
+            rest = jnp.where(lane == at, part, rest)
+            value = value - part
+            at += 1
+    for b in range(blocks):
+        block = picked[:, b * SEGLEN : (b + 1) * SEGLEN]
+        block = jnp.where(lane < valid, block, rest).astype(bf16)
+        for p in range(shares):
+            message[b * shares + p] = block
+
+
+def beside_kernel(rows, *refs):
+    *parts, kernel, regularizer, out, brick = refs
+    brick[:SEGLEN, :] = kernel[...].astype(bf16)
+    high = regularizer[...].astype(bf16).astype(f32)
+    spare = jnp.zeros((brick.shape[0] - SEGLEN - 2 * high.shape[0], SEGLEN), f32)
+    brick[SEGLEN:, :] = jnp.concatenate([high, regularizer[...] - high, spare], axis=0).astype(bf16)
+    count = len(parts)
+    for tile in range(parts[0].shape[0] // rows):
+        for k, part in enumerate(parts):
+            row = (tile * count + k) * rows
+            out[row : row + rows, :] = part[tile * rows : (tile + 1) * rows, :]
+
+
+def facts_of(got, share, sub_rows):
+    part = got[share].astype(f32)
+    rolled = pltpu.roll(part, SEGLEN // 2, 1)
+    lane = iota((sub_rows, SEGLEN), 1)
+
+    def rows(first):
+        return jnp.where(
+            lane < SEGLEN // 2,
+            rolled[first : first + sub_rows],
+            part[first + sub_rows : first + 2 * sub_rows],
+        )
+
+    return rows(0), rows(2 * sub_rows)
+
+
+def flat_facts(sub_rows, shares, got, place, upright, flat):
     orients = shares * sub_rows
     blocks = flat.shape[1]
     lot = SEGLEN // orients
-    in_order(near, far, place, slice(group_rows, near.shape[1]), ordered)
-
-    def rows_of(first, count):
-        return [ordered[p, first : first + count, :SEGLEN] for p in range(shares)]
-
-    facts = rows_of(0, sub_rows) + rows_of(sub_rows, sub_rows)
-    for h in range(reg_rows):
-        facts += rows_of(2 * sub_rows + h, 1)
-    used = 2 * orients + shares * reg_rows
-    facts = jnp.concatenate(facts + [jnp.zeros((SEGLEN - used, SEGLEN), f32)], axis=0)
+    pairs = [facts_of(got, place[1] * shares + p, sub_rows) for p in range(shares)]
+    facts = [pair[h] for h in range(2) for pair in pairs]
+    facts = jnp.concatenate(facts + [jnp.zeros((SEGLEN - 2 * orients, SEGLEN), f32)], axis=0)
     upright[...] = jnp.swapaxes(facts, 0, 1)
     parts = [upright[pl.ds(b, blocks, stride=lot), :] for b in range(lot)]
     for h in range(2):
@@ -390,30 +407,64 @@
     return slots, owners
 
 
-def choice_kernel(
-    group_rows,
+def fact_kernel(
     sub_rows,
-    near,
-    far,
+    shares,
+    got,
     after,
     place,
     chosen,
+    parity_lanes,
+    counts,
     own_slots,
     own_owner_lanes,
-    ordered,
     upright,
     flat,
 ):
-    shares = ordered.shape[0]
     row_count = own_slots.shape[1]
+    orients = shares * sub_rows
+    blocks = flat.shape[1]
     tiles = SEGLEN
-    slots, owners = flat_facts(group_rows, sub_rows, near, far, place, 0, ordered, upright, flat)
-    target = (owners.astype(jnp.int32) // 2).astype(f32) * float(row_count) + slots
-    pair_row = iota((chosen.shape[0], SEGLEN), 0).astype(f32)
-    for a in range(flat.shape[1]):
-        block = slice(a * SEGLEN, (a + 1) * SEGLEN)
-        chosen[:, block] = jnp.where(pair_row == target[a : a + 1, :], 1.0, 0.0).astype(bf16)
-    own = near[0, group_rows : near.shape[1], :SEGLEN]
+    pairs = shares // 2
+    slots, owners = flat_facts(sub_rows, shares, got, place, upright, flat)
+    pair = (owners.astype(jnp.int32) // 2).astype(f32)
+    parity = owners - 2.0 * pair
+    columns = jnp.concatenate(
+        [owners, parity, jnp.zeros((SEGLEN - 2 * blocks, SEGLEN), f32)], axis=0
+    )
+    columns = jnp.swapaxes(columns, 0, 1)
+    groups = row_count // 16
+    slot_row = iota((row_count, SEGLEN), 0).astype(f32).astype(bf16).reshape(groups, 16, SEGLEN)
+    zeros = jnp.zeros((groups, 16, SEGLEN), bf16)
+    ones = jnp.ones((groups, 16, SEGLEN), bf16)
+    count_lane = iota((SEGLEN, shares * orients), 1)
+    lane_owner = (count_lane // orients).astype(f32)
+    same = iota((SEGLEN, shares * orients), 0) % orients == count_lane % orients
+    lane_owner = jnp.where(same, lane_owner, -1.0)
+    total = jnp.zeros((row_count, shares * orients), f32)
+    for a in range(0, blocks, 2):
+        slot_chosen, owned = [], []
+        for b in (a, a + 1):
+            block = slice(b * SEGLEN, (b + 1) * SEGLEN)
+            slot = jnp.broadcast_to(slots[b : b + 1, :], (16, SEGLEN)).astype(bf16)
+            match = slot_row == slot[None]
+            for q in range(pairs):
+                held = jnp.broadcast_to(pair[b : b + 1, :], (16, SEGLEN))
+                held = jnp.where(held == float(q), 1.0, 0.0).astype(bf16)
+                part = jnp.where(match, jnp.broadcast_to(held[None], zeros.shape), zeros)
+                chosen[q * row_count : (q + 1) * row_count, block] = part.reshape(row_count, SEGLEN)
+            slot_chosen.append(jnp.where(match, ones, zeros).reshape(row_count, SEGLEN))
+            parity_lanes[block, :] = jnp.broadcast_to(
+                columns[:, blocks + b : blocks + b + 1], (SEGLEN, SEGLEN)
+            ).astype(bf16)
+            owned.append(jnp.where(columns[:, b : b + 1] == lane_owner, 1.0, 0.0).astype(bf16))
+        total += jnp.dot(
+            jnp.concatenate(slot_chosen, axis=1),
+            jnp.concatenate(owned, axis=0),
+            preferred_element_type=f32,
+        )
+    counts[...] = total.astype(bf16)
+    own = jnp.concatenate(facts_of(got, place[1] * shares + place[0], sub_rows), axis=0)
     own = jnp.concatenate([own, jnp.zeros((SEGLEN - own.shape[0], SEGLEN), f32)], axis=0)
     own = jnp.swapaxes(own, 0, 1)
     slot_lane = iota((tiles, row_count), 1).astype(f32)
@@ -425,72 +476,36 @@
         ).astype(bf16)
 
 
-def count_kernel(
-    group_rows,
-    sub_rows,
-    near,
-    far,
-    after,
-    place,
-    parity_lanes,
-    counts,
-    regularizer,
-    ordered,
-    upright,
-    flat,
-):
-    shares = ordered.shape[0]
-    row_count = regularizer.shape[0]
-    reg_rows = row_count // SEGLEN
-    orients = shares * sub_rows
-    blocks = flat.shape[1]
-    slots, owners = flat_facts(
-        group_rows, sub_rows, near, far, place, reg_rows, ordered, upright, flat
-    )
-    for h in range(reg_rows):
-        first = 2 * orients + h * shares
-        regularizer[h * SEGLEN : (h + 1) * SEGLEN, :] = upright[:, first : first + shares]
-    parity = (owners.astype(jnp.int32) % 2).astype(f32)
-    columns = jnp.concatenate(
-        [owners, parity, jnp.zeros((SEGLEN - 2 * blocks, SEGLEN), f32)], axis=0
-    )
-    columns = jnp.swapaxes(columns, 0, 1)
-    slot_row = iota((row_count, SEGLEN), 0).astype(f32)
-    count_lane = iota((SEGLEN, shares * orients), 1)
-    lane_owner = (count_lane // orients).astype(f32)
-    same = iota((SEGLEN, shares * orients), 0) % orients == count_lane % orients
-    total = jnp.zeros((row_count, shares * orients), f32)
-    for a in range(0, blocks, 2):
-        slot_chosen, owned = [], []
-        for b in (a, a + 1):
-            block = slice(b * SEGLEN, (b + 1) * SEGLEN)
-            parity_lanes[block, :] = jnp.broadcast_to(
-                columns[:, blocks + b : blocks + b + 1], (SEGLEN, SEGLEN)
-            ).astype(bf16)
-            slot_chosen.append(jnp.where(slot_row == slots[b : b + 1, :], 1.0, 0.0).astype(bf16))
-            holds = jnp.where(columns[:, b : b + 1] == lane_owner, 1.0, 0.0)
-            owned.append(jnp.where(same, holds, 0.0).astype(bf16))
-        total += jnp.dot(
-            jnp.concatenate(slot_chosen, axis=1),
-            jnp.concatenate(owned, axis=0),
-            preferred_element_type=f32,
-        )
-    counts[...] = total.astype(bf16)
-
-
 def slice_kernel(shift_count, group_rows, *refs):
-    *messages, tables, arrange, kernel, after, segments, masses = refs
+    got, images, tables, arrange, after, place, segments, masses = refs
     length = tables.shape[2]
-    half = arrange.shape[1] // SEGLEN
+    shares = 2 * arrange.shape[1] // SEGLEN
     orients = arrange.shape[0] // shift_count
     lot = CHUNK // SEGLEN
-
+    valid = shift_count * orients // shares
+    img_count = got.shape[0] // shares
+    image_rows = img_count * group_rows
+    everything = jnp.concatenate(
+        [got[(place[1] ^ k) * shares + p] for p in range(shares) for k in range(img_count)], axis=0
+    )
+    row, lane = iota((SEGLEN, 2 * SEGLEN), 0), iota((SEGLEN, 2 * SEGLEN), 1)
+    first = jnp.where(lane < SEGLEN, valid, valid + 3)
+    spread = jnp.where((row >= first) & (row < first + 3), 1.0, 0.0).astype(bf16)
+    values = jnp.dot(everything, spread, preferred_element_type=f32)
+    parts = [slice(p * image_rows, (p + 1) * image_rows) for p in range(shares)]
+    peak = functools.reduce(jnp.maximum, [values[part, :SEGLEN] for part in parts])
+    factors = [jnp.exp(values[part, :SEGLEN] - peak) for part in parts]
+    total = sum(values[part, SEGLEN:] * factor for part, factor in zip(parts, factors, strict=True))
+    inverse = 1.0 / total
+    lane = iota((image_rows, SEGLEN), 1)
+    weighted = [
+        jnp.where(lane < valid, everything[part].astype(f32) * (factor * inverse), 0.0)
+        for part, factor in zip(parts, factors, strict=True)
+    ]
     stacked = jnp.concatenate(
         [
-            jnp.concatenate(
-                [message[a * group_rows : (a + 1) * group_rows, :] for message in messages], axis=0
-            )
-            for a in range(half)
+            (weighted[p] + pltpu.roll(weighted[p + 1], SEGLEN // 2, 1)).astype(bf16)
+            for p in range(0, shares, 2)
         ],
         axis=1,
     )
@@ -501,8 +516,7 @@
     weights = weights.astype(bf16)
 
     def images_at(tile):
-        row = (half + tile) * group_rows
-        return jnp.concatenate([message[row : row + group_rows, :] for message in messages], axis=0)
+        return images[tile * image_rows : (tile + 1) * image_rows, :]
 
     for t in range(length // CHUNK):
         lanes = slice(t * CHUNK, (t + 1) * CHUNK)
@@ -525,7 +539,6 @@
             segments[row : row + orients, :] = total_re[:, lanes].astype(bf16)
             row += length // SEGLEN * orients
             segments[row : row + orients, :] = total_im[:, lanes].astype(bf16)
-    segments[2 * (length // SEGLEN) * orients :, :] = kernel[...].astype(bf16)
 
 
 def insert(shares, first, chosen, parity_lanes, segments):
@@ -542,28 +555,26 @@
     return jnp.dot(chosen[:, lanes], segments[...], preferred_element_type=f32)
 
 
-def near_kernel(
-    near, chosen, parity_lanes, counts, regularizer, masses, inserted, inverse, segments
-):
+def near_kernel(near, chosen, parity_lanes, counts, masses, inserted, weight_sum, segments):
     inserted[...] = insert(near, 0, chosen, parity_lanes, segments)
-    shares = regularizer.shape[1]
+    shares = weight_sum.shape[1]
     mass = masses[...]
     mass_hi = mass.astype(bf16).astype(f32)
     lane = iota(mass.shape, 1)
     both = jnp.where(lane < shares, mass_hi, jnp.where(lane < 2 * shares, mass - mass_hi, 0.0))
     spread = jnp.concatenate([jnp.where(lane % shares == w, both, 0.0) for w in range(shares)], axis=0)
-    weight_sum = jnp.dot(counts[...], spread.astype(bf16), preferred_element_type=f32)
-    weight_sum = weight_sum[:, :shares] + weight_sum[:, shares : 2 * shares]
-    inverse[...] = 1.0 / (weight_sum + regularizer[...])
+    total = jnp.dot(counts[...], spread.astype(bf16), preferred_element_type=f32)
+    weight_sum[...] = total[:, :shares] + total[:, shares : 2 * shares]
 
 
 def volume_kernel(
-    near,
     far,
+    near_bricks,
+    far_bricks,
     near_inserted,
     chosen,
     parity_lanes,
-    inverse,
+    weight_sum,
     own_slots,
     own_owner_lanes,
     place,
@@ -574,19 +585,31 @@
     bricks,
     result,
     rows_out,
+    regularizer,
     signals,
 ):
-    half = near.shape[0]
+    half = far.shape[0]
     shares = 2 * half
     rows = segments.shape[0] // half
     row_count = bricks.shape[1]
     sub_rows, coef = rows_out.shape
     tiles = coef // SEGLEN
+    reg_rows = row_count // SEGLEN
     kernels[...] = jnp.zeros(kernels.shape, bf16)
+    regularizer[...] = jnp.zeros(regularizer.shape, f32)
     for p in range(shares):
         w = place[0] ^ distance_of(p, shares)
         at = pl.ds(pl.multiple_of(w % 2 * SEGLEN, SEGLEN), SEGLEN)
-        kernels[w // 2, at, at] = near[p, rows:, :] if p < half else far[p - half, rows:, :]
+        brick = near_bricks[p] if p < half else far_bricks[p - half]
+        kernels[w // 2, at, at] = brick[:SEGLEN]
+        parts = brick[SEGLEN:].astype(f32)
+        for h in range(reg_rows):
+            regularizer[pl.ds(h * shares + w, 1), :] = (
+                parts[h : h + 1, :] + parts[reg_rows + h : reg_rows + h + 1, :]
+            )
+    columns = jnp.swapaxes(regularizer[...], 0, 1)
+    columns = [columns[:, h * shares : (h + 1) * shares] for h in range(reg_rows)]
+    inverse = 1.0 / (weight_sum[...] + jnp.concatenate(columns, axis=0))
     inserted = insert(far, half, chosen, parity_lanes, segments) + near_inserted[...]
     inserted = inserted.astype(bf16)
     mapped = []
@@ -658,12 +681,9 @@
     column = np.arange(columns)
     orient = column % orient_count
     lane = orient // sub_rows * SEGLEN + column // orient_count * sub_rows + orient % sub_rows
-    pick = np.stack([lane + h * (SEGLEN // 2) for h in range(2)])[:, :, None]
-    pick = jnp.asarray(pick == np.arange(img_count * SEGLEN), bf16)
+    pick = jnp.asarray(lane[:, None] == np.arange(img_count * SEGLEN), bf16)
     row = np.arange(shift_count * orients)
-    share = row % orients // sub_rows
-    source = share % half * SEGLEN + share // half * (SEGLEN // 2)
-    source += row // orients * sub_rows + row % sub_rows
+    source = row % orients // sub_rows * (SEGLEN // 2) + row // orients * sub_rows + row % sub_rows
     arrange = jnp.asarray(source[:, None] == np.arange(half * SEGLEN), bf16)
     phases, tables = call(
         phase_kernel,
@@ -673,88 +693,83 @@
         cost=COST_PHASE,
     )
     near, far = gather_pair(piece, phases)
-    message_rows = group_rows + 16
-    message_lanes = -(-columns // SEGLEN) * SEGLEN
-    scores, part = call(
+    message, part = call(
         functools.partial(score_kernel, shift_count),
         (
             near,
             far,
             references,
             phases,
+            pick,
             slot_rows.reshape(-1, SEGLEN),
             owners.reshape(-1, SEGLEN),
-            regularizer.reshape(-1, SEGLEN),
         ),
-        (((message_rows, message_lanes), f32), ((2 * length // SEGLEN * group_rows, SEGLEN), bf16)),
+        (
+            ((img_count * ori_count, group_rows, SEGLEN), bf16),
+            ((2 * length // SEGLEN * group_rows, SEGLEN), bf16),
+        ),
         scratch=(pltpu.VMEM((group_rows, coef), bf16), pltpu.VMEM(phases.shape[1:], f32)),
         small=(place,),
         cost=COST_SCORE,
     )
-    near, far = gather_pair(scores)
-
-    messages = call(
-        functools.partial(weight_kernel, group_rows, columns),
-        (near, far, pick, part),
-        (((half * group_rows + part.shape[0], SEGLEN), bf16),) * img_count,
-        scratch=(
-            pltpu.VMEM((ori_count, group_rows, message_lanes), f32),
-            pltpu.VMEM((half * group_rows, img_count * SEGLEN), f32),
-        ),
-        small=(place,),
-        cost=COST_WEIGHT,
-    )
-    arrived = [messages[0]] + [hop(messages[k], "img", k) for k in range(1, img_count)]
-
-    fact_scratch = (
-        pltpu.VMEM((ori_count, 16, message_lanes), f32),
-        pltpu.VMEM((SEGLEN, SEGLEN), f32),
-        pltpu.VMEM((2, orients * tiles // SEGLEN, SEGLEN), f32),
-    )
-    parity_lanes, counts, regs = call(
-        functools.partial(count_kernel, group_rows, sub_rows),
-        (near, far, messages[0]),
-        (
-            ((orients * tiles, SEGLEN), bf16),
-            ((row_count, ori_count * orients), bf16),
-            ((row_count, ori_count), f32),
-        ),
-        scratch=fact_scratch,
-        small=(place,),
-        cost=COST_COUNT,
-    )
+    got = lax.all_to_all(message, ("img", "ori"), split_axis=0, concat_axis=0, tiled=True)
+    pieces = [part] + [hop(part, "img", k) for k in range(1, img_count)]
+    beside, brick = call(
+        functools.partial(beside_kernel, group_rows),
+        (*pieces, interpolation, regularizer.reshape(-1, SEGLEN)),
+        (((img_count * part.shape[0], SEGLEN), bf16), ((SEGLEN + 16, SEGLEN), bf16)),
+        cost=COST_BESIDE,
+    )
+    near_bricks, far_bricks = gather_pair(brick)
+
     rows = 2 * (length // SEGLEN) * orients
     segments, masses = call(
         functools.partial(slice_kernel, shift_count, group_rows),
-        (*arrived, tables, arrange, interpolation, regs),
-        (((rows + SEGLEN, SEGLEN), bf16), ((orients, SEGLEN), f32)),
+        (got, beside, tables, arrange, near_bricks),
+        (((rows, SEGLEN), bf16), ((orients, SEGLEN), f32)),
+        small=(place,),
         cost=COST_SLICE,
     )
-    chosen, own_slots, own_owner_lanes = call(
-        functools.partial(choice_kernel, group_rows, sub_rows),
-        (near, far, masses),
+    chosen, parity_lanes, counts, own_slots, own_owner_lanes = call(
+        functools.partial(fact_kernel, sub_rows, ori_count),
+        (got, masses),
         (
             ((half * row_count, orients * tiles), bf16),
+            ((orients * tiles, SEGLEN), bf16),
+            ((row_count, ori_count * orients), bf16),
             ((sub_rows * tiles, row_count), bf16),
             ((sub_rows * tiles, SEGLEN), bf16),
         ),
-        scratch=fact_scratch,
+        scratch=(
+            pltpu.VMEM((SEGLEN, SEGLEN), f32),
+            pltpu.VMEM((2, orients * tiles // SEGLEN, SEGLEN), f32),
+        ),
         small=(place,),
-        cost=COST_CHOICE,
-    )
-
-    near, far = gather_pair(segments, own_owner_lanes)
+        cost=COST_FACT,
+    )
+
+    near, far = gather_pair(segments, counts)
     masked = pltpu.VMEM((half * rows, 2 * SEGLEN), bf16)
-    inserted, inverse = call(
+    inserted, weight_sum = call(
         near_kernel,
-        (near, chosen, parity_lanes, counts, regs, masses),
+        (near, chosen, parity_lanes, counts, masses),
         (((half * row_count, 2 * SEGLEN), f32), ((row_count, ori_count), f32)),
         scratch=(masked,),
         cost=COST_NEAR,
     )
     volume, resampled = call(
         volume_kernel,
-        (near, far, inserted, chosen, parity_lanes, inverse, own_slots, own_owner_lanes),
+        (
+            far,
+            near_bricks,
+            far_bricks,
+            inserted,
+            chosen,
+            parity_lanes,
+            weight_sum,
+            own_slots,
+            own_owner_lanes,
+        ),
         (((row_count, SEGLEN), f32), ((sub_rows, coef), f32)),
         scratch=(
             masked,
@@ -762,6 +777,7 @@
             pltpu.VMEM((ori_count, row_count, SEGLEN), f32),
             pltpu.VMEM((sub_rows * tiles, SEGLEN), f32),
             pltpu.VMEM((sub_rows, coef), f32),
+            pltpu.VMEM((SEGLEN, SEGLEN), f32),
             pltpu.SemaphoreType.DMA((2,)),
         ),
         small=(place,),

time: 50.1 us -> 49.8 us (level)
  starting transfers between devices: 16.3 us -> 21.7 us
  Pallas kernels: 18.2 us -> 15.4 us
  waiting for transfers between devices: 13.6 us -> 10.9 us
    all_to_all x0 -> x1, starting transfers between devices: none -> 4.92 us  [whole_plane(): lax.all_to_all(message, ('img', 'ori'), split_axis=0, concat_axis=0, tile...]
    ppermute x15, waiting for transfers between devices: 13.6 us -> 10.1 us  [hop(): return lax.ppermute(value, axis, pairs)]
    pallas_call x11 -> x10, Pallas kernels: 18.2 us -> 15.4 us  [call(): pl.pallas_call(kernel, out_shape=[jax.ShapeDtypeStruct(shape, dtype) for...]
    all_to_all x0 -> x1, waiting for transfers between devices: none -> 0.78 us  [whole_plane(): lax.all_to_all(message, ('img', 'ori'), split_axis=0, concat_axis=0, tile...]
  transfers between devices with their start and end apart: 15 -> 16, of which waited for: 10 -> 10; matrix products, arithmetic and copies ran while one was open for 2% -> 2% of each run, Pallas kernels for 18% -> 11%
where the time goes in v5:
time: 49.8 us; the launch traced here: 49.6 us
  starting transfers between devices  21.7 us (44%)
  Pallas kernels  15.4 us (31%)
  waiting for transfers between devices  10.9 us (22%)
  local copies, waits for them, and re-layouts  0.8 us (2%)
  between operations  0.77 us (2%)
    ppermute x15, starting transfers between devices, hop(): return lax.ppermute(value, axis, pairs)  16.7 us
    pallas_call x10, Pallas kernels, call(): pl.pallas_call(kernel, out_shape=[jax.ShapeDtypeStruct(shape, dtype) for...  15.4 us
    ppermute x15, waiting for transfers between devices, hop(): return lax.ppermute(value, axis, pairs)  10.1 us
    all_to_all x1, starting transfers between devices, whole_plane(): lax.all_to_all(message, ('img', 'ori'), split_axis=0, concat_axis=0, tile...  4.92 us
  transfers between devices with their start and end apart: 16, of which 10 were waited for; matrix products, arithmetic and copies ran while one was open for 2% of the time, Pallas kernels for 11%

profile of v5, /device:TPU:0, one launch (start us, length us, event | category | flops | bytes accessed | tf_op | source)
XLA Modules:
  0.0 49.6 jit_solution(8071167545953502308)
XLA Ops:
  0.6 4.0 %collective-permute-start = (bf16[256,128]{1,0:T(8,128)(2,1)}, bf16[256,128]{1,0:T(8,128)(2,1)S(1)}, u32[]{:S(2)}, u32[]{:S(2)}) collective-permute-start(bf16[256,128]{1,0:T(8,128)(2,1)} %bitcast.10), channel_id=1, source_target_pairs={{0,6},{1,7},{2,4},{3,5},{4,2},{5,3},{6,0},{7,1},{8,14},{9,15},{10,... | collective-permute-start | bytes 196616 | tf_op jit(solution)/shard_map/ppermute | solution.py:32
  4.6 0.5 %collective-permute-start.1 = (bf16[256,128]{1,0:T(8,128)(2,1)}, bf16[256,128]{1,0:T(8,128)(2,1)S(1)}, u32[]{:S(2)}, u32[]{:S(2)}) collective-permute-start(bf16[256,128]{1,0:T(8,128)(2,1)} %bitcast.11), channel_id=1, source_target_pairs={{0,4},{1,5},{2,6},{3,7},{4,0},{5,1},{6,2},{7,3},{8,12},{9,13},{10,... | collective-permute-start | bytes 196616 | tf_op jit(solution)/shard_map/ppermute | solution.py:32
  5.1 0.1 collective-permute-start.2
  5.2 0.8 %copy.12.shifts = f32[12,2]{1,0:T(8,128)S(1)} copy(f32[12,2]{0,1:T(2,128)} %param.11) | data formatting | bytes 192 | tf_op args[2]
  6.0 0.1 pad_add_fusion.place.refs_5_
  6.1 0.0 copy-start.5
  6.1 0.0 copy-start.6
  6.1 0.0 copy-start.7
  6.1 0.9 %shard_map.104 = (f32[2,2,16,256]{3,2,1,0:T(8,128)S(1)}, f32[2,16,1024]{2,1,0:T(8,128)S(1)}) custom-call(f32[12,2]{1,0:T(8,128)S(1)} %copy.12.shifts, s32[2]{0:T(128)S(1)} %pad_add_fusion.place.refs_5_), custom_call_target="tpu_custom_call" | custom-call | flops 13799999488 | tf_op jit(solution)/shard_map/pallas_call | solution.py:651
  7.1 0.0 collective-permute-done.refs_0_
  7.1 2.0 %collective-permute-done.1.refs_1_ = bf16[256,128]{1,0:T(8,128)(2,1)S(1)} collective-permute-done((bf16[256,128]{1,0:T(8,128)(2,1)}, bf16[256,128]{1,0:T(8,128)(2,1)S(1)}, u32[]{:S(2)}, u32[]{:S(2)}) %collective-permute-start.1) | collective-permute-done | bytes 65568 | tf_op jit(solution)/shard_map/ppermute | solution.py:32
  9.1 0.5 %collective-permute-done.2.refs_2_ = bf16[256,128]{1,0:T(8,128)(2,1)S(1)} collective-permute-done((bf16[256,128]{1,0:T(8,128)(2,1)}, bf16[256,128]{1,0:T(8,128)(2,1)S(1)}, u32[]{:S(2)}, u32[]{:S(2)}) %collective-permute-start.2) | collective-permute-done | bytes 65568 | tf_op jit(solution)/shard_map/ppermute | solution.py:32
  9.6 0.0 copy-done.3
  9.6 0.1 collective-permute-start.3
  9.7 1.5 %collective-permute-done.3.far = bf16[4,256,128]{2,1,0:T(8,128)(2,1)S(1)} collective-permute-done((bf16[4,256,128]{2,1,0:T(8,128)(2,1)S(1)}, bf16[4,256,128]{2,1,0:T(8,128)(2,1)S(1)}, u32[]{:S(2)}, u32[]{:S(2)}) %collective-permute-start.3) | collective-permute-done | bytes 262176 | tf_op jit(solution)/shard_map/ppermute | solution.py:32
  11.2 0.0 copy-done
  11.2 0.0 copy-done.2
  11.2 0.0 copy-done.4
  11.2 3.8 %shard_map.106 = (bf16[32,16,128]{2,1,0:T(8,128)(2,1)}, bf16[256,128]{1,0:T(8,128)(2,1)S(1)}) custom-call(bf16[4,256,128]{2,1,0:T(8,128)(2,1)S(1)} %shard_map.105.near, bf16[4,256,128]{2,1,0:T(8,128)(2,1)S(1)} %collective-permute-done.3.far, bf16[16,16384]{1,0:T(8,128)(2,1)S(1)} %copy-done, f32[2,2,16,256]{3,2,1,0:T(8,128)S(1)} %get-tuple-element.17.refs_4_.phases, ...), custom_call_target="tpu_custom_call" | custom-call | flops 1150000 | tf_op jit(solution)/shard_map/pallas_call | solution.py:651
  15.1 1.6 %collective-permute-start.4 = (bf16[256,128]{1,0:T(8,128)(2,1)S(1)}, bf16[256,128]{1,0:T(8,128)(2,1)S(1)}, u32[]{:S(2)}, u32[]{:S(2)}) collective-permute-start(bf16[256,128]{1,0:T(8,128)(2,1)S(1)} %get-tuple-element.19.refs_0_), channel_id=1, source_target_pairs={{0,8},{8,0},{16,24},{24,16},{1,9},{9,1},{17,25},{25,17},{2,10},{10... | collective-permute-start | bytes 196616 | tf_op jit(solution)/shard_map/ppermute | solution.py:32
  16.6 2.6 %collective-permute-start.5 = (bf16[256,128]{1,0:T(8,128)(2,1)S(1)}, bf16[256,128]{1,0:T(8,128)(2,1)S(1)}, u32[]{:S(2)}, u32[]{:S(2)}) collective-permute-start(bf16[256,128]{1,0:T(8,128)(2,1)S(1)} %get-tuple-element.19.refs_0_), channel_id=1, source_target_pairs={{0,16},{8,24},{16,0},{24,8},{1,17},{9,25},{17,1},{25,9},{2,18},{10... | collective-permute-start | bytes 196616 | tf_op jit(solution)/shard_map/ppermute | solution.py:32
  19.2 0.2 collective-permute-start.6
  19.4 4.9 %all-to-all-start = ((bf16[32,16,128]{2,1,0:T(8,128)(2,1)}), bf16[32,16,128]{2,1,0:T(8,128)(2,1)S(1)}, u32[]{:S(2)}, u32[]{:S(2)}) async-start(bf16[32,16,128]{2,1,0:T(8,128)(2,1)} %get-tuple-element.18), calls=%async_computation | async-start | bytes 262144 | tf_op jit(solution)/shard_map/all_to_all | solution.py:715
  24.4 0.0 collective-permute-done.4.refs_1_
  24.4 0.0 collective-permute-done.5.refs_2_
  24.4 1.0 %collective-permute-done.6.refs_3_ = bf16[256,128]{1,0:T(8,128)(2,1)S(1)} collective-permute-done((bf16[256,128]{1,0:T(8,128)(2,1)S(1)}, bf16[256,128]{1,0:T(8,128)(2,1)S(1)}, u32[]{:S(2)}, u32[]{:S(2)}) %collective-permute-start.6) | collective-permute-done | bytes 65568 | tf_op jit(solution)/shard_map/ppermute | solution.py:32
  25.4 0.0 copy-done.6
  25.4 1.8 %collective-permute-start.7 = (bf16[144,128]{1,0:T(8,128)(2,1)S(1)}, bf16[144,128]{1,0:T(8,128)(2,1)S(1)}, u32[]{:S(2)}, u32[]{:S(2)}) collective-permute-start(bf16[144,128]{1,0:T(8,128)(2,1)S(1)} %get-tuple-element.22.refs_3_), channel_id=1, source_target_pairs={{0,6},{1,7},{2,4},{3,5},{4,2},{5,3},{6,0},{7,1},{8,14},{9,15},{10,... | collective-permute-start | bytes 110600 | tf_op jit(solution)/shard_map/ppermute | solution.py:32
  27.2 0.6 %collective-permute-start.8 = (bf16[144,128]{1,0:T(8,128)(2,1)S(1)}, bf16[144,128]{1,0:T(8,128)(2,1)S(1)}, u32[]{:S(2)}, u32[]{:S(2)}) collective-permute-start(bf16[144,128]{1,0:T(8,128)(2,1)S(1)} %get-tuple-element.22.refs_3_), channel_id=1, source_target_pairs={{0,4},{1,5},{2,6},{3,7},{4,0},{5,1},{6,2},{7,3},{8,12},{9,13},{10,... | collective-permute-start | bytes 110600 | tf_op jit(solution)/shard_map/ppermute | solution.py:32
  27.8 1.2 %collective-permute-start.9 = (bf16[144,128]{1,0:T(8,128)(2,1)S(1)}, bf16[144,128]{1,0:T(8,128)(2,1)S(1)}, u32[]{:S(2)}, u32[]{:S(2)}) collective-permute-start(bf16[144,128]{1,0:T(8,128)(2,1)S(1)} %get-tuple-element.22.refs_3_), channel_id=1, source_target_pairs={{0,2},{1,3},{2,0},{3,1},{4,6},{5,7},{6,4},{7,5},{8,10},{9,11},{10,... | collective-permute-start | bytes 110600 | tf_op jit(solution)/shard_map/ppermute | solution.py:32
  29.0 1.6 %collective-permute-done.7.refs_0_ = bf16[144,128]{1,0:T(8,128)(2,1)S(1)} collective-permute-done((bf16[144,128]{1,0:T(8,128)(2,1)S(1)}, bf16[144,128]{1,0:T(8,128)(2,1)S(1)}, u32[]{:S(2)}, u32[]{:S(2)}) %collective-permute-start.7) | collective-permute-done | bytes 36896 | tf_op jit(solution)/shard_map/ppermute | solution.py:32
  30.6 0.7 %collective-permute-done.8.refs_1_ = bf16[144,128]{1,0:T(8,128)(2,1)S(1)} collective-permute-done((bf16[144,128]{1,0:T(8,128)(2,1)S(1)}, bf16[144,128]{1,0:T(8,128)(2,1)S(1)}, u32[]{:S(2)}, u32[]{:S(2)}) %collective-permute-start.8) | collective-permute-done | bytes 36896 | tf_op jit(solution)/shard_map/ppermute | solution.py:32
  31.3 0.5 %collective-permute-done.9.refs_2_ = bf16[144,128]{1,0:T(8,128)(2,1)S(1)} collective-permute-done((bf16[144,128]{1,0:T(8,128)(2,1)S(1)}, bf16[144,128]{1,0:T(8,128)(2,1)S(1)}, u32[]{:S(2)}, u32[]{:S(2)}) %collective-permute-start.9) | collective-permute-done | bytes 36896 | tf_op jit(solution)/shard_map/ppermute | solution.py:32
  31.8 0.8 %all-to-all-done.refs_0_.got = bf16[32,16,128]{2,1,0:T(8,128)(2,1)S(1)} async-done(((bf16[32,16,128]{2,1,0:T(8,128)(2,1)}), bf16[32,16,128]{2,1,0:T(8,128)(2,1)S(1)}, u32[]{:S(2)}, u32[]{:S(2)}) %all-to-all-start) | async-done | bytes 131104 | tf_op jit(solution)/shard_map/all_to_all | solution.py:715
  32.6 1.7 %shard_map.109 = (bf16[512,128]{1,0:T(8,128)(2,1)S(1)}, f32[32,128]{1,0:T(8,128)S(1)}) custom-call(bf16[32,16,128]{2,1,0:T(8,128)(2,1)S(1)} %all-to-all-done.refs_0_.got, bf16[1024,128]{1,0:T(8,128)(2,1)S(1)} %get-tuple-element.20.refs_1_, f32[2,16,1024]{2,1,0:T(8,128)S(1)} %get-tuple-element.21.refs_2_, bf16[384,512]{1,0:T(8,128)(2,1)S(1)} %copy-done.1, ...), custom_call_target="tpu_custom_call" | custom-call | flops 1150000 | tf_op jit(solution)/shard_map/pallas_call | solution.py:651
  34.3 1.4 %collective-permute-start.10 = (bf16[512,128]{1,0:T(8,128)(2,1)S(1)}, bf16[512,128]{1,0:T(8,128)(2,1)S(1)}, u32[]{:S(2)}, u32[]{:S(2)}) collective-permute-start(bf16[512,128]{1,0:T(8,128)(2,1)S(1)} %get-tuple-element.23.refs_3_), channel_id=1, source_target_pairs={{0,6},{1,7},{2,4},{3,5},{4,2},{5,3},{6,0},{7,1},{8,14},{9,15},{10,... | collective-permute-start | bytes 393224 | tf_op jit(solution)/shard_map/ppermute | solution.py:32
  35.7 0.6 %collective-permute-start.11 = (bf16[512,128]{1,0:T(8,128)(2,1)S(1)}, bf16[512,128]{1,0:T(8,128)(2,1)S(1)}, u32[]{:S(2)}, u32[]{:S(2)}) collective-permute-start(bf16[512,128]{1,0:T(8,128)(2,1)S(1)} %get-tuple-element.23.refs_3_), channel_id=1, source_target_pairs={{0,4},{1,5},{2,6},{3,7},{4,0},{5,1},{6,2},{7,3},{8,12},{9,13},{10,... | collective-permute-start | bytes 393224 | tf_op jit(solution)/shard_map/ppermute | solution.py:32
  36.3 1.6 %collective-permute-start.12 = (bf16[512,128]{1,0:T(8,128)(2,1)S(1)}, bf16[512,128]{1,0:T(8,128)(2,1)S(1)}, u32[]{:S(2)}, u32[]{:S(2)}) collective-permute-start(bf16[512,128]{1,0:T(8,128)(2,1)S(1)} %get-tuple-element.23.refs_3_), channel_id=1, source_target_pairs={{0,2},{1,3},{2,0},{3,1},{4,6},{5,7},{6,4},{7,5},{8,10},{9,11},{10,... | collective-permute-start | bytes 393224 | tf_op jit(solution)/shard_map/ppermute | solution.py:32
  37.9 3.0 %shard_map.110 = (bf16[1024,4096]{1,0:T(8,128)(2,1)S(1)}, bf16[4096,128]{1,0:T(8,128)(2,1)S(1)}, bf16[256,256]{1,0:T(8,128)(2,1)S(1)}, bf16[512,256]{1,0:T(8,128)(2,1)S(1)}, bf16[512,128]{1,0:T(8,128)(2,1)S(1)}) custom-call(bf16[32,16,128]{2,1,0:T(8,128)(2,1)S(1)} %all-to-all-done.refs_0_.got, f32[32,128]{1,0:T(8,128)S(1)} %get-tuple-element.24.after.masses, ...), custom_call_target="tpu_custom_call" | custom-call | flops 1150000 | tf_op jit(solution)/shard_map/pallas_call | solution.py:651
  40.8 0.8 %collective-permute-done.10.refs_0_ = bf16[512,128]{1,0:T(8,128)(2,1)S(1)} collective-permute-done((bf16[512,128]{1,0:T(8,128)(2,1)S(1)}, bf16[512,128]{1,0:T(8,128)(2,1)S(1)}, u32[]{:S(2)}, u32[]{:S(2)}) %collective-permute-start.10) | collective-permute-done | bytes 131104 | tf_op jit(solution)/shard_map/ppermute | solution.py:32
  41.6 1.4 %collective-permute-done.11.refs_1_ = bf16[512,128]{1,0:T(8,128)(2,1)S(1)} collective-permute-done((bf16[512,128]{1,0:T(8,128)(2,1)S(1)}, bf16[512,128]{1,0:T(8,128)(2,1)S(1)}, u32[]{:S(2)}, u32[]{:S(2)}) %collective-permute-start.11) | collective-permute-done | bytes 131104 | tf_op jit(solution)/shard_map/ppermute | solution.py:32
  43.0 0.0 collective-permute-done.12.refs_2_
  43.1 0.1 collective-permute-start.13
  43.2 0.5 %collective-permute-start.14 = (bf16[4,144,128]{2,1,0:T(8,128)(2,1)S(1)}, bf16[4,144,128]{2,1,0:T(8,128)(2,1)S(1)}, u32[]{:S(2)}, u32[]{:S(2)}) collective-permute-start(bf16[4,144,128]{2,1,0:T(8,128)(2,1)S(1)} %shard_map.108.refs_4_.near_bricks), channel_id=1, source_target_pairs={{0,1},{1,0},{2,3},{3,2},{4,5},{5,4},{6,7},{7,6},{8,9},{9,8},{10,11... | collective-permute-start | bytes 442376 | tf_op jit(solution)/shard_map/ppermute | solution.py:32
  43.7 1.6 %shard_map.112 = (f32[1024,256]{1,0:T(8,128)S(1)}, f32[256,8]{1,0:T(8,128)S(1)}) custom-call(bf16[4,512,128]{2,1,0:T(8,128)(2,1)S(1)} %shard_map.111.near, bf16[1024,4096]{1,0:T(8,128)(2,1)S(1)} %get-tuple-element.26.chosen, bf16[4096,128]{1,0:T(8,128)(2,1)S(1)} %get-tuple-element.27.parity_lanes, bf16[256,256]{1,0:T(8,128)(2,1)S(1)} %get-tuple-element.25.refs_4_.counts, ...), custom_call_target="tpu_custom_call" | custom-call | flops 1150000 | tf_op jit(solution)/shard_map/pallas_call | solution.py:651
  45.2 0.0 collective-permute-done.14.far_bricks
  45.3 0.0 collective-permute-done.13.far
  45.3 4.3 %shard_map.113 = (f32[256,128]{1,0:T(8,128)}, f32[4,16384]{1,0:T(4,128)}) custom-call(bf16[4,512,128]{2,1,0:T(8,128)(2,1)S(1)} %collective-permute-done.13.far, bf16[4,144,128]{2,1,0:T(8,128)(2,1)S(1)} %shard_map.108.refs_4_.near_bricks, bf16[4,144,128]{2,1,0:T(8,128)(2,1)S(1)} %collective-permute-done.14.far_bricks, ...), custom_call_target="tpu_custom_call" | custom-call | flops 1150000 | tf_op jit(solution)/shard_map/pallas_call | solution.py:651
  (12 shorter events, 0.1 us)
Async XLA Ops:
  0.6 6.4 %collective-permute-start = (bf16[256,128]{1,0:T(8,128)(2,1)}, bf16[256,128]{1,0:T(8,128)(2,1)S(1)}, u32[]{:S(2)}, u32[]{:S(2)}) collective-permute-start(bf16[256,128]{1,0:T(8,128)(2,1)} %bitcast.10), channel_id=1, source_target_pairs={{0,6},{1,7},{2,4},{3,5},{4,2},{5,3},{6,0},{7,1},{8,14},{9,15},{10,... | collective-permute-start | bytes 196616 | tf_op jit(solution)/shard_map/ppermute | solution.py:32
  4.6 4.5 %collective-permute-start.1 = (bf16[256,128]{1,0:T(8,128)(2,1)}, bf16[256,128]{1,0:T(8,128)(2,1)S(1)}, u32[]{:S(2)}, u32[]{:S(2)}) collective-permute-start(bf16[256,128]{1,0:T(8,128)(2,1)} %bitcast.11), channel_id=1, source_target_pairs={{0,4},{1,5},{2,6},{3,7},{4,0},{5,1},{6,2},{7,3},{8,12},{9,13},{10,... | collective-permute-start | bytes 196616 | tf_op jit(solution)/shard_map/ppermute | solution.py:32
  5.1 4.5 %collective-permute-start.2 = (bf16[256,128]{1,0:T(8,128)(2,1)}, bf16[256,128]{1,0:T(8,128)(2,1)S(1)}, u32[]{:S(2)}, u32[]{:S(2)}) collective-permute-start(bf16[256,128]{1,0:T(8,128)(2,1)} %bitcast.12), channel_id=1, source_target_pairs={{0,2},{1,3},{2,0},{3,1},{4,6},{5,7},{6,4},{7,5},{8,10},{9,11},{10,... | collective-permute-start | bytes 196616 | tf_op jit(solution)/shard_map/ppermute | solution.py:32
  6.1 3.5 %copy-start.3 = (bf16[2,16384]{1,0:T(2,128)(2,1)S(1)}, bf16[2,16384]{1,0:T(2,128)(2,1)}, u32[]{:S(2)}) copy-start(bf16[2,16384]{1,0:T(2,128)(2,1)} %param.9) | copy-start | bytes 196612
  6.1 5.1 %copy-start = (bf16[16,16384]{1,0:T(8,128)(2,1)S(1)}, bf16[16,16384]{1,0:T(8,128)(2,1)}, u32[]{:S(2)}) copy-start(bf16[16,16384]{1,0:T(8,128)(2,1)} %references.1) | copy-start | bytes 1572868
  6.1 5.1 %copy-start.2 = (bf16[192,512]{1,0:T(8,128)(2,1)S(1)}, bf16[192,512]{1,0:T(8,128)(2,1)}, u32[]{:S(2)}) copy-start(bf16[192,512]{1,0:T(8,128)(2,1)} %constant.12.clone.pick) | copy-start | bytes 589828
  6.1 5.1 %copy-start.4 = (s32[512]{0:T(512)S(1)}, s32[512]{0:T(512)}, u32[]{:S(2)}) copy-start(s32[512]{0:T(512)} %param.13) | copy-start | bytes 6148
  6.1 5.1 %copy-start.5 = (s32[512,1]{0,1:T(1,128)S(1)}, s32[512,1]{0,1:T(1,128)}, u32[]{:S(2)}) copy-start(s32[512,1]{0,1:T(1,128)} %param.12) | copy-start | bytes 6148
  6.1 19.3 %copy-start.6 = (f32[128,128]{1,0:T(8,128)S(1)}, f32[128,128]{1,0:T(8,128)}, u32[]{:S(2)}) copy-start(f32[128,128]{1,0:T(8,128)} %refs_4_.1) | copy-start | bytes 196612
  6.1 19.3 %copy-start.7 = (f32[256]{0:T(256)S(1)}, f32[256]{0:T(256)}, u32[]{:S(2)}) copy-start(f32[256]{0:T(256)} %param.15) | copy-start | bytes 3076
  9.6 1.6 %collective-permute-start.3 = (bf16[4,256,128]{2,1,0:T(8,128)(2,1)S(1)}, bf16[4,256,128]{2,1,0:T(8,128)(2,1)S(1)}, u32[]{:S(2)}, u32[]{:S(2)}) collective-permute-start(bf16[4,256,128]{2,1,0:T(8,128)(2,1)S(1)} %shard_map.105.near), channel_id=1, source_target_pairs={{0,1},{1,0},{2,3},{3,2},{4,5},{5,4},{6,7},{7,6},{8,9},{9,8},{10,11... | collective-permute-start | bytes 786440 | tf_op jit(solution)/shard_map/ppermute | solution.py:32
  15.1 9.3 %collective-permute-start.4 = (bf16[256,128]{1,0:T(8,128)(2,1)S(1)}, bf16[256,128]{1,0:T(8,128)(2,1)S(1)}, u32[]{:S(2)}, u32[]{:S(2)}) collective-permute-start(bf16[256,128]{1,0:T(8,128)(2,1)S(1)} %get-tuple-element.19.refs_0_), channel_id=1, source_target_pairs={{0,8},{8,0},{16,24},{24,16},{1,9},{9,1},{17,25},{25,17},{2,10},{10... | collective-permute-start | bytes 196616 | tf_op jit(solution)/shard_map/ppermute | solution.py:32
  16.6 7.8 %collective-permute-start.5 = (bf16[256,128]{1,0:T(8,128)(2,1)S(1)}, bf16[256,128]{1,0:T(8,128)(2,1)S(1)}, u32[]{:S(2)}, u32[]{:S(2)}) collective-permute-start(bf16[256,128]{1,0:T(8,128)(2,1)S(1)} %get-tuple-element.19.refs_0_), channel_id=1, source_target_pairs={{0,16},{8,24},{16,0},{24,8},{1,17},{9,25},{17,1},{25,9},{2,18},{10... | collective-permute-start | bytes 196616 | tf_op jit(solution)/shard_map/ppermute | solution.py:32
  19.2 6.2 %collective-permute-start.6 = (bf16[256,128]{1,0:T(8,128)(2,1)S(1)}, bf16[256,128]{1,0:T(8,128)(2,1)S(1)}, u32[]{:S(2)}, u32[]{:S(2)}) collective-permute-start(bf16[256,128]{1,0:T(8,128)(2,1)S(1)} %get-tuple-element.19.refs_0_), channel_id=1, source_target_pairs={{0,24},{8,16},{16,8},{24,0},{1,25},{9,17},{17,9},{25,1},{2,26},{10... | collective-permute-start | bytes 196616 | tf_op jit(solution)/shard_map/ppermute | solution.py:32
  19.4 13.2 %all-to-all-start = ((bf16[32,16,128]{2,1,0:T(8,128)(2,1)}), bf16[32,16,128]{2,1,0:T(8,128)(2,1)S(1)}, u32[]{:S(2)}, u32[]{:S(2)}) async-start(bf16[32,16,128]{2,1,0:T(8,128)(2,1)} %get-tuple-element.18), calls=%async_computation | async-start | bytes 262144 | tf_op jit(solution)/shard_map/all_to_all | solution.py:715
  25.4 7.2 %copy-start.1 = (bf16[384,512]{1,0:T(8,128)(2,1)S(1)}, bf16[384,512]{1,0:T(8,128)(2,1)}, u32[]{:S(2)}) copy-start(bf16[384,512]{1,0:T(8,128)(2,1)} %constant.13.clone.refs_3_) | copy-start | bytes 1179652
  25.4 5.1 %collective-permute-start.7 = (bf16[144,128]{1,0:T(8,128)(2,1)S(1)}, bf16[144,128]{1,0:T(8,128)(2,1)S(1)}, u32[]{:S(2)}, u32[]{:S(2)}) collective-permute-start(bf16[144,128]{1,0:T(8,128)(2,1)S(1)} %get-tuple-element.22.refs_3_), channel_id=1, source_target_pairs={{0,6},{1,7},{2,4},{3,5},{4,2},{5,3},{6,0},{7,1},{8,14},{9,15},{10,... | collective-permute-start | bytes 110600 | tf_op jit(solution)/shard_map/ppermute | solution.py:32
  27.2 4.1 %collective-permute-start.8 = (bf16[144,128]{1,0:T(8,128)(2,1)S(1)}, bf16[144,128]{1,0:T(8,128)(2,1)S(1)}, u32[]{:S(2)}, u32[]{:S(2)}) collective-permute-start(bf16[144,128]{1,0:T(8,128)(2,1)S(1)} %get-tuple-element.22.refs_3_), channel_id=1, source_target_pairs={{0,4},{1,5},{2,6},{3,7},{4,0},{5,1},{6,2},{7,3},{8,12},{9,13},{10,... | collective-permute-start | bytes 110600 | tf_op jit(solution)/shard_map/ppermute | solution.py:32
  27.8 4.0 %collective-permute-start.9 = (bf16[144,128]{1,0:T(8,128)(2,1)S(1)}, bf16[144,128]{1,0:T(8,128)(2,1)S(1)}, u32[]{:S(2)}, u32[]{:S(2)}) collective-permute-start(bf16[144,128]{1,0:T(8,128)(2,1)S(1)} %get-tuple-element.22.refs_3_), channel_id=1, source_target_pairs={{0,2},{1,3},{2,0},{3,1},{4,6},{5,7},{6,4},{7,5},{8,10},{9,11},{10,... | collective-permute-start | bytes 110600 | tf_op jit(solution)/shard_map/ppermute | solution.py:32
  34.3 7.3 %collective-permute-start.10 = (bf16[512,128]{1,0:T(8,128)(2,1)S(1)}, bf16[512,128]{1,0:T(8,128)(2,1)S(1)}, u32[]{:S(2)}, u32[]{:S(2)}) collective-permute-start(bf16[512,128]{1,0:T(8,128)(2,1)S(1)} %get-tuple-element.23.refs_3_), channel_id=1, source_target_pairs={{0,6},{1,7},{2,4},{3,5},{4,2},{5,3},{6,0},{7,1},{8,14},{9,15},{10,... | collective-permute-start | bytes 393224 | tf_op jit(solution)/shard_map/ppermute | solution.py:32
  35.7 7.4 %collective-permute-start.11 = (bf16[512,128]{1,0:T(8,128)(2,1)S(1)}, bf16[512,128]{1,0:T(8,128)(2,1)S(1)}, u32[]{:S(2)}, u32[]{:S(2)}) collective-permute-start(bf16[512,128]{1,0:T(8,128)(2,1)S(1)} %get-tuple-element.23.refs_3_), channel_id=1, source_target_pairs={{0,4},{1,5},{2,6},{3,7},{4,0},{5,1},{6,2},{7,3},{8,12},{9,13},{10,... | collective-permute-start | bytes 393224 | tf_op jit(solution)/shard_map/ppermute | solution.py:32
  36.3 6.8 %collective-permute-start.12 = (bf16[512,128]{1,0:T(8,128)(2,1)S(1)}, bf16[512,128]{1,0:T(8,128)(2,1)S(1)}, u32[]{:S(2)}, u32[]{:S(2)}) collective-permute-start(bf16[512,128]{1,0:T(8,128)(2,1)S(1)} %get-tuple-element.23.refs_3_), channel_id=1, source_target_pairs={{0,2},{1,3},{2,0},{3,1},{4,6},{5,7},{6,4},{7,5},{8,10},{9,11},{10,... | collective-permute-start | bytes 393224 | tf_op jit(solution)/shard_map/ppermute | solution.py:32
  43.1 2.2 %collective-permute-start.13 = (bf16[4,512,128]{2,1,0:T(8,128)(2,1)S(1)}, bf16[4,512,128]{2,1,0:T(8,128)(2,1)S(1)}, u32[]{:S(2)}, u32[]{:S(2)}) collective-permute-start(bf16[4,512,128]{2,1,0:T(8,128)(2,1)S(1)} %shard_map.111.near), channel_id=1, source_target_pairs={{0,1},{1,0},{2,3},{3,2},{4,5},{5,4},{6,7},{7,6},{8,9},{9,8},{10,11... | collective-permute-start | bytes 1572872 | tf_op jit(solution)/shard_map/ppermute | solution.py:32
  43.2 2.1 %collective-permute-start.14 = (bf16[4,144,128]{2,1,0:T(8,128)(2,1)S(1)}, bf16[4,144,128]{2,1,0:T(8,128)(2,1)S(1)}, u32[]{:S(2)}, u32[]{:S(2)}) collective-permute-start(bf16[4,144,128]{2,1,0:T(8,128)(2,1)S(1)} %shard_map.108.refs_4_.near_bricks), channel_id=1, source_target_pairs={{0,1},{1,0},{2,3},{3,2},{4,5},{5,4},{6,7},{7,6},{8,9},{9,8},{10,11... | collective-permute-start | bytes 442376 | tf_op jit(solution)/shard_map/ppermute | solution.py:32

commit v6 on v5

--- a/solution.py
+++ b/solution.py
@@ -196,27 +196,33 @@
 
 
 def distance_of(place, shares):
-    half = shares // 2
-    if isinstance(place, int):
-        return 2 * place if place < half else 2 * (place - half) + 1
-    return jnp.where(place < half, 2 * place, 2 * (place - half) + 1)
-
-
-def gather_pair(value, *after, own=None):
-    parts = [value if own is None else own]
-    parts += [hop(value, "ori", k) for k in even_distances()]
+    even = (shares - 2 * place) & (shares - 1)
+    return even ^ (place // (shares // 2))
+
+
+def hops_in_plane(value):
+    count = lax.axis_size("ori")
+    return [hop(value, "ori", distance) for distance in range(count - 2, 0, -2)]
+
+
+def stacks(value, others, *after):
+    count = len(others) + 1
     (near,) = call(
-        functools.partial(stack_kernel, len(parts)),
-        (*reversed(parts), *after),
-        (((len(parts), *value.shape), value.dtype),),
+        functools.partial(stack_kernel, count),
+        (*others, value, *after),
+        (((count, *value.shape), value.dtype),),
         cost=COST_STACK,
     )
     return near, hop(near, "ori", 1)
+
+
+def gather_pair(value, *after):
+    return stacks(value, hops_in_plane(value), *after)
 
 
 def stack_kernel(count, *refs):
     for place in range(count):
-        refs[-1][count - 1 - place] = refs[place][...]
+        refs[-1][(place + 1) % count] = refs[place][...]
 
 
 def phase_kernel(shifts, place, phases, tables):
@@ -542,21 +548,29 @@
 
 
 def insert(shares, first, chosen, parity_lanes, segments):
-    rows = segments.shape[0] // shares.shape[0]
+    rows = segments.shape[0] // len(shares)
     zero = jnp.zeros((rows, SEGLEN), bf16)
-    for p in range(shares.shape[0]):
-        part = shares[p, :rows, :]
+    for p in range(len(shares)):
+        part = shares[p][:rows, :]
         parity = parity_lanes[(first + p) * rows : (first + p + 1) * rows, :]
         for w in range(2):
             segments[p * rows : (p + 1) * rows, w * SEGLEN : (w + 1) * SEGLEN] = jnp.where(
                 parity == float(w), part, zero
             )
-    lanes = slice(first * rows, (first + shares.shape[0]) * rows)
+    lanes = slice(first * rows, (first + len(shares)) * rows)
     return jnp.dot(chosen[:, lanes], segments[...], preferred_element_type=f32)
 
 
-def near_kernel(near, chosen, parity_lanes, counts, masses, inserted, weight_sum, segments):
-    inserted[...] = insert(near, 0, chosen, parity_lanes, segments)
+def next_kernel(first, *refs):
+    *shares, chosen, parity_lanes, before, inserted, segments = refs
+    inserted[...] = before[...] + insert(shares, first, chosen, parity_lanes, segments)
+
+
+def near_kernel(
+    own, other, chosen, parity_lanes, counts, masses, inserted, weight_sum, sent, segments
+):
+    sent[...] = own[...]
+    inserted[...] = insert([own, other], 0, chosen, parity_lanes, segments)
     shares = weight_sum.shape[1]
     mass = masses[...]
     mass_hi = mass.astype(bf16).astype(f32)
@@ -567,28 +581,28 @@
     weight_sum[...] = total[:, :shares] + total[:, shares : 2 * shares]
 
 
-def volume_kernel(
-    far,
-    near_bricks,
-    far_bricks,
-    near_inserted,
-    chosen,
-    parity_lanes,
-    weight_sum,
-    own_slots,
-    own_owner_lanes,
-    place,
-    volume,
-    resampled,
-    segments,
-    kernels,
-    bricks,
-    result,
-    rows_out,
-    regularizer,
-    signals,
-):
-    half = far.shape[0]
+def volume_kernel(half, *refs):
+    far, refs = refs[:half], refs[half:]
+    (
+        near_bricks,
+        far_bricks,
+        near_inserted,
+        chosen,
+        parity_lanes,
+        weight_sum,
+        own_slots,
+        own_owner_lanes,
+        place,
+        volume,
+        resampled,
+        segments,
+        kernels,
+        bricks,
+        result,
+        rows_out,
+        regularizer,
+        signals,
+    ) = refs
     shares = 2 * half
     rows = segments.shape[0] // half
     row_count = bricks.shape[1]
@@ -748,19 +762,31 @@
         cost=COST_FACT,
     )
 
-    near, far = gather_pair(segments, counts)
-    masked = pltpu.VMEM((half * rows, 2 * SEGLEN), bf16)
-    inserted, weight_sum = call(
+    others = hops_in_plane(segments)
+
+    def masked(count):
+        return pltpu.VMEM((count * rows, 2 * SEGLEN), bf16)
+
+    shape = ((half * row_count, 2 * SEGLEN), f32)
+    inserted, weight_sum, sent = call(
         near_kernel,
-        (near, chosen, parity_lanes, counts, masses),
-        (((half * row_count, 2 * SEGLEN), f32), ((row_count, ori_count), f32)),
-        scratch=(masked,),
+        (segments, others[0], chosen, parity_lanes, counts, masses),
+        (shape, ((row_count, ori_count), f32), (segments.shape, bf16)),
+        scratch=(masked(2),),
         cost=COST_NEAR,
     )
+    far = [hop(part, "ori", 1) for part in [sent, *others]]
+    (inserted,) = call(
+        functools.partial(next_kernel, 2),
+        (*others[1:], chosen, parity_lanes, inserted),
+        (shape,),
+        scratch=(masked(half - 2),),
+        cost=COST_NEAR,
+    )
     volume, resampled = call(
-        volume_kernel,
+        functools.partial(volume_kernel, half),
         (
-            far,
+            *far,
             near_bricks,
             far_bricks,
             inserted,
@@ -772,7 +798,7 @@
         ),
         (((row_count, SEGLEN), f32), ((sub_rows, coef), f32)),
         scratch=(
-            masked,
+            masked(half),
             pltpu.VMEM((half, 2 * SEGLEN, 2 * SEGLEN), bf16),
             pltpu.VMEM((ori_count, row_count, SEGLEN), f32),
             pltpu.VMEM((sub_rows * tiles, SEGLEN), f32),

time: 49.8 us -> 49.2 us (0.988)
  waiting for transfers between devices: 10.9 us -> 9.59 us
  starting transfers between devices: 21.7 us -> 22.2 us
    ppermute x15 -> x18, waiting for transfers between devices: 10.1 us -> 8.82 us  [hop(): return lax.ppermute(value, axis, pairs)]
    ppermute x15 -> x18, starting transfers between devices: 16.7 us -> 17.3 us  [hop(): return lax.ppermute(value, axis, pairs)]
  transfers between devices with their start and end apart: 16 -> 19, of which waited for: 10 -> 10; matrix products, arithmetic and copies ran while one was open for 2% -> 2% of each run, Pallas kernels for 11% -> 12%
where the time goes in v6:
time: 49.2 us; the launch traced here: 49 us
  starting transfers between devices  22.2 us (45%)
  Pallas kernels  15.6 us (32%)
  waiting for transfers between devices  9.59 us (19%)
  between operations  0.81 us (2%)
  local copies, waits for them, and re-layouts  0.8 us (2%)
    ppermute x18, starting transfers between devices, hop(): return lax.ppermute(value, axis, pairs)  17.3 us
    pallas_call x10, Pallas kernels, call(): pl.pallas_call(kernel, out_shape=[jax.ShapeDtypeStruct(shape, dtype) for...  15.6 us
    ppermute x18, waiting for transfers between devices, hop(): return lax.ppermute(value, axis, pairs)  8.82 us
    all_to_all x1, starting transfers between devices, whole_plane(): lax.all_to_all(message, ('img', 'ori'), split_axis=0, concat_axis=0, tile...  4.92 us
  transfers between devices with their start and end apart: 19, of which 10 were waited for; matrix products, arithmetic and copies ran while one was open for 2% of the time, Pallas kernels for 12%

profile of v6, /device:TPU:0, one launch (start us, length us, event | category | flops | bytes accessed | tf_op | source)
XLA Modules:
  0.0 49.0 jit_solution(12136922679631776596)
XLA Ops:
  0.6 4.0 %collective-permute-start = (bf16[256,128]{1,0:T(8,128)(2,1)}, bf16[256,128]{1,0:T(8,128)(2,1)S(1)}, u32[]{:S(2)}, u32[]{:S(2)}) collective-permute-start(bf16[256,128]{1,0:T(8,128)(2,1)} %bitcast.10), channel_id=1, source_target_pairs={{0,6},{1,7},{2,4},{3,5},{4,2},{5,3},{6,0},{7,1},{8,14},{9,15},{10,... | collective-permute-start | bytes 196616 | tf_op jit(solution)/shard_map/ppermute | solution.py:32
  4.6 0.5 %collective-permute-start.1 = (bf16[256,128]{1,0:T(8,128)(2,1)}, bf16[256,128]{1,0:T(8,128)(2,1)S(1)}, u32[]{:S(2)}, u32[]{:S(2)}) collective-permute-start(bf16[256,128]{1,0:T(8,128)(2,1)} %bitcast.11), channel_id=1, source_target_pairs={{0,4},{1,5},{2,6},{3,7},{4,0},{5,1},{6,2},{7,3},{8,12},{9,13},{10,... | collective-permute-start | bytes 196616 | tf_op jit(solution)/shard_map/ppermute | solution.py:32
  5.1 0.1 collective-permute-start.2
  5.2 0.8 %copy.12.shifts = f32[12,2]{1,0:T(8,128)S(1)} copy(f32[12,2]{0,1:T(2,128)} %param.11) | data formatting | bytes 192 | tf_op args[2]
  6.0 0.1 pad_add_fusion.place.refs_5_.refs_12_
  6.1 0.0 copy-start.5
  6.1 0.0 copy-start.6
  6.1 0.0 copy-start.7
  6.1 0.9 %shard_map.104 = (f32[2,2,16,256]{3,2,1,0:T(8,128)S(1)}, f32[2,16,1024]{2,1,0:T(8,128)S(1)}) custom-call(f32[12,2]{1,0:T(8,128)S(1)} %copy.12.shifts, s32[2]{0:T(128)S(1)} %pad_add_fusion.place.refs_5_.refs_12_), custom_call_target="tpu_custom_call" | custom-call | flops 13799999488 | tf_op jit(solution)/shard_map/pallas_call | solution.py:665
  7.1 0.0 collective-permute-done.refs_0_
  7.1 2.0 %collective-permute-done.1.refs_1_ = bf16[256,128]{1,0:T(8,128)(2,1)S(1)} collective-permute-done((bf16[256,128]{1,0:T(8,128)(2,1)}, bf16[256,128]{1,0:T(8,128)(2,1)S(1)}, u32[]{:S(2)}, u32[]{:S(2)}) %collective-permute-start.1) | collective-permute-done | bytes 65568 | tf_op jit(solution)/shard_map/ppermute | solution.py:32
  9.1 0.5 %collective-permute-done.2.refs_2_ = bf16[256,128]{1,0:T(8,128)(2,1)S(1)} collective-permute-done((bf16[256,128]{1,0:T(8,128)(2,1)}, bf16[256,128]{1,0:T(8,128)(2,1)S(1)}, u32[]{:S(2)}, u32[]{:S(2)}) %collective-permute-start.2) | collective-permute-done | bytes 65568 | tf_op jit(solution)/shard_map/ppermute | solution.py:32
  9.6 0.1 collective-permute-start.3
  9.7 1.5 %collective-permute-done.3.far = bf16[4,256,128]{2,1,0:T(8,128)(2,1)S(1)} collective-permute-done((bf16[4,256,128]{2,1,0:T(8,128)(2,1)S(1)}, bf16[4,256,128]{2,1,0:T(8,128)(2,1)S(1)}, u32[]{:S(2)}, u32[]{:S(2)}) %collective-permute-start.3) | collective-permute-done | bytes 262176 | tf_op jit(solution)/shard_map/ppermute | solution.py:32
  11.2 3.8 %shard_map.106 = (bf16[32,16,128]{2,1,0:T(8,128)(2,1)}, bf16[256,128]{1,0:T(8,128)(2,1)S(1)}) custom-call(bf16[4,256,128]{2,1,0:T(8,128)(2,1)S(1)} %shard_map.105.near, bf16[4,256,128]{2,1,0:T(8,128)(2,1)S(1)} %collective-permute-done.3.far, bf16[16,16384]{1,0:T(8,128)(2,1)S(1)} %copy-done, f32[2,2,16,256]{3,2,1,0:T(8,128)S(1)} %get-tuple-element.18.refs_4_.phases, ...), custom_call_target="tpu_custom_call" | custom-call | flops 1150000 | tf_op jit(solution)/shard_map/pallas_call | solution.py:665
  15.1 1.6 %collective-permute-start.4 = (bf16[256,128]{1,0:T(8,128)(2,1)S(1)}, bf16[256,128]{1,0:T(8,128)(2,1)S(1)}, u32[]{:S(2)}, u32[]{:S(2)}) collective-permute-start(bf16[256,128]{1,0:T(8,128)(2,1)S(1)} %get-tuple-element.20.refs_0_), channel_id=1, source_target_pairs={{0,8},{8,0},{16,24},{24,16},{1,9},{9,1},{17,25},{25,17},{2,10},{10... | collective-permute-start | bytes 196616 | tf_op jit(solution)/shard_map/ppermute | solution.py:32
  16.6 2.6 %collective-permute-start.5 = (bf16[256,128]{1,0:T(8,128)(2,1)S(1)}, bf16[256,128]{1,0:T(8,128)(2,1)S(1)}, u32[]{:S(2)}, u32[]{:S(2)}) collective-permute-start(bf16[256,128]{1,0:T(8,128)(2,1)S(1)} %get-tuple-element.20.refs_0_), channel_id=1, source_target_pairs={{0,16},{8,24},{16,0},{24,8},{1,17},{9,25},{17,1},{25,9},{2,18},{10... | collective-permute-start | bytes 196616 | tf_op jit(solution)/shard_map/ppermute | solution.py:32
  19.2 0.2 collective-permute-start.6
  19.5 4.9 %all-to-all-start = ((bf16[32,16,128]{2,1,0:T(8,128)(2,1)}), bf16[32,16,128]{2,1,0:T(8,128)(2,1)S(1)}, u32[]{:S(2)}, u32[]{:S(2)}) async-start(bf16[32,16,128]{2,1,0:T(8,128)(2,1)} %get-tuple-element.19), calls=%async_computation | async-start | bytes 262144 | tf_op jit(solution)/shard_map/all_to_all | solution.py:729
  24.4 0.0 collective-permute-done.4.refs_1_
  24.4 0.0 collective-permute-done.5.refs_2_
  24.4 1.0 %collective-permute-done.6.refs_3_ = bf16[256,128]{1,0:T(8,128)(2,1)S(1)} collective-permute-done((bf16[256,128]{1,0:T(8,128)(2,1)S(1)}, bf16[256,128]{1,0:T(8,128)(2,1)S(1)}, u32[]{:S(2)}, u32[]{:S(2)}) %collective-permute-start.6) | collective-permute-done | bytes 65568 | tf_op jit(solution)/shard_map/ppermute | solution.py:32
  25.4 1.8 %collective-permute-start.7 = (bf16[144,128]{1,0:T(8,128)(2,1)S(1)}, bf16[144,128]{1,0:T(8,128)(2,1)S(1)}, u32[]{:S(2)}, u32[]{:S(2)}) collective-permute-start(bf16[144,128]{1,0:T(8,128)(2,1)S(1)} %get-tuple-element.23.refs_3_), channel_id=1, source_target_pairs={{0,6},{1,7},{2,4},{3,5},{4,2},{5,3},{6,0},{7,1},{8,14},{9,15},{10,... | collective-permute-start | bytes 110600 | tf_op jit(solution)/shard_map/ppermute | solution.py:32
  27.2 0.6 %collective-permute-start.8 = (bf16[144,128]{1,0:T(8,128)(2,1)S(1)}, bf16[144,128]{1,0:T(8,128)(2,1)S(1)}, u32[]{:S(2)}, u32[]{:S(2)}) collective-permute-start(bf16[144,128]{1,0:T(8,128)(2,1)S(1)} %get-tuple-element.23.refs_3_), channel_id=1, source_target_pairs={{0,4},{1,5},{2,6},{3,7},{4,0},{5,1},{6,2},{7,3},{8,12},{9,13},{10,... | collective-permute-start | bytes 110600 | tf_op jit(solution)/shard_map/ppermute | solution.py:32
  27.8 1.2 %collective-permute-start.9 = (bf16[144,128]{1,0:T(8,128)(2,1)S(1)}, bf16[144,128]{1,0:T(8,128)(2,1)S(1)}, u32[]{:S(2)}, u32[]{:S(2)}) collective-permute-start(bf16[144,128]{1,0:T(8,128)(2,1)S(1)} %get-tuple-element.23.refs_3_), channel_id=1, source_target_pairs={{0,2},{1,3},{2,0},{3,1},{4,6},{5,7},{6,4},{7,5},{8,10},{9,11},{10,... | collective-permute-start | bytes 110600 | tf_op jit(solution)/shard_map/ppermute | solution.py:32
  29.0 1.6 %collective-permute-done.7.refs_0_ = bf16[144,128]{1,0:T(8,128)(2,1)S(1)} collective-permute-done((bf16[144,128]{1,0:T(8,128)(2,1)S(1)}, bf16[144,128]{1,0:T(8,128)(2,1)S(1)}, u32[]{:S(2)}, u32[]{:S(2)}) %collective-permute-start.7) | collective-permute-done | bytes 36896 | tf_op jit(solution)/shard_map/ppermute | solution.py:32
  30.6 0.7 %collective-permute-done.8.refs_1_ = bf16[144,128]{1,0:T(8,128)(2,1)S(1)} collective-permute-done((bf16[144,128]{1,0:T(8,128)(2,1)S(1)}, bf16[144,128]{1,0:T(8,128)(2,1)S(1)}, u32[]{:S(2)}, u32[]{:S(2)}) %collective-permute-start.8) | collective-permute-done | bytes 36896 | tf_op jit(solution)/shard_map/ppermute | solution.py:32
  31.3 0.5 %collective-permute-done.9.refs_2_ = bf16[144,128]{1,0:T(8,128)(2,1)S(1)} collective-permute-done((bf16[144,128]{1,0:T(8,128)(2,1)S(1)}, bf16[144,128]{1,0:T(8,128)(2,1)S(1)}, u32[]{:S(2)}, u32[]{:S(2)}) %collective-permute-start.9) | collective-permute-done | bytes 36896 | tf_op jit(solution)/shard_map/ppermute | solution.py:32
  31.8 0.8 %all-to-all-done.refs_0_.got = bf16[32,16,128]{2,1,0:T(8,128)(2,1)S(1)} async-done(((bf16[32,16,128]{2,1,0:T(8,128)(2,1)}), bf16[32,16,128]{2,1,0:T(8,128)(2,1)S(1)}, u32[]{:S(2)}, u32[]{:S(2)}) %all-to-all-start) | async-done | bytes 131104 | tf_op jit(solution)/shard_map/all_to_all | solution.py:729
  32.6 1.7 %shard_map.109 = (bf16[512,128]{1,0:T(8,128)(2,1)S(1)}, f32[32,128]{1,0:T(8,128)S(1)}) custom-call(bf16[32,16,128]{2,1,0:T(8,128)(2,1)S(1)} %all-to-all-done.refs_0_.got, bf16[1024,128]{1,0:T(8,128)(2,1)S(1)} %get-tuple-element.21.refs_1_, f32[2,16,1024]{2,1,0:T(8,128)S(1)} %get-tuple-element.22.refs_2_, bf16[384,512]{1,0:T(8,128)(2,1)S(1)} %copy-done.1, ...), custom_call_target="tpu_custom_call" | custom-call | flops 1150000 | tf_op jit(solution)/shard_map/pallas_call | solution.py:665
  34.3 1.4 %collective-permute-start.10 = (bf16[512,128]{1,0:T(8,128)(2,1)S(1)}, bf16[512,128]{1,0:T(8,128)(2,1)S(1)}, u32[]{:S(2)}, u32[]{:S(2)}) collective-permute-start(bf16[512,128]{1,0:T(8,128)(2,1)S(1)} %get-tuple-element.24.own), channel_id=1, source_target_pairs={{0,6},{1,7},{2,4},{3,5},{4,2},{5,3},{6,0},{7,1},{8,14},{9,15},{10,... | collective-permute-start | bytes 393224 | tf_op jit(solution)/shard_map/ppermute | solution.py:32
  35.7 0.6 %collective-permute-start.13 = (bf16[512,128]{1,0:T(8,128)(2,1)S(1)}, bf16[512,128]{1,0:T(8,128)(2,1)S(1)}, u32[]{:S(2)}, u32[]{:S(2)}) collective-permute-start(bf16[512,128]{1,0:T(8,128)(2,1)S(1)} %get-tuple-element.24.own), channel_id=1, source_target_pairs={{0,4},{1,5},{2,6},{3,7},{4,0},{5,1},{6,2},{7,3},{8,12},{9,13},{10,... | collective-permute-start | bytes 393224 | tf_op jit(solution)/shard_map/ppermute | solution.py:32
  36.3 1.6 %collective-permute-start.15 = (bf16[512,128]{1,0:T(8,128)(2,1)S(1)}, bf16[512,128]{1,0:T(8,128)(2,1)S(1)}, u32[]{:S(2)}, u32[]{:S(2)}) collective-permute-start(bf16[512,128]{1,0:T(8,128)(2,1)S(1)} %get-tuple-element.24.own), channel_id=1, source_target_pairs={{0,2},{1,3},{2,0},{3,1},{4,6},{5,7},{6,4},{7,5},{8,10},{9,11},{10,... | collective-permute-start | bytes 393224 | tf_op jit(solution)/shard_map/ppermute | solution.py:32
  37.9 0.0 collective-permute-start.17
  37.9 3.0 %shard_map.110 = (bf16[1024,4096]{1,0:T(8,128)(2,1)S(1)}, bf16[4096,128]{1,0:T(8,128)(2,1)S(1)}, bf16[256,256]{1,0:T(8,128)(2,1)S(1)}, bf16[512,256]{1,0:T(8,128)(2,1)S(1)}, bf16[512,128]{1,0:T(8,128)(2,1)S(1)}) custom-call(bf16[32,16,128]{2,1,0:T(8,128)(2,1)S(1)} %all-to-all-done.refs_0_.got, f32[32,128]{1,0:T(8,128)S(1)} %get-tuple-element.25.after.masses, ...), custom_call_target="tpu_custom_call" | custom-call | flops 1150000 | tf_op jit(solution)/shard_map/pallas_call | solution.py:665
  40.8 0.8 %collective-permute-done.10.other = bf16[512,128]{1,0:T(8,128)(2,1)S(1)} collective-permute-done((bf16[512,128]{1,0:T(8,128)(2,1)S(1)}, bf16[512,128]{1,0:T(8,128)(2,1)S(1)}, u32[]{:S(2)}, u32[]{:S(2)}) %collective-permute-start.10) | collective-permute-done | bytes 131104 | tf_op jit(solution)/shard_map/ppermute | solution.py:32
  41.6 0.9 %shard_map.111 = (f32[1024,256]{1,0:T(8,128)S(1)}, f32[256,8]{1,0:T(8,128)S(1)}, bf16[512,128]{1,0:T(8,128)(2,1)S(1)}) custom-call(bf16[512,128]{1,0:T(8,128)(2,1)S(1)} %get-tuple-element.24.own, bf16[512,128]{1,0:T(8,128)(2,1)S(1)} %collective-permute-done.10.other, bf16[1024,4096]{1,0:T(8,128)(2,1)S(1)} %get-tuple-element.26.chosen.refs_2_.refs_7_, ...), custom_call_target="tpu_custom_call" | custom-call | flops 1150000 | tf_op jit(solution)/shard_map/pallas_call | solution.py:665
  42.6 0.1 collective-permute-start.11
  42.7 0.5 %collective-permute-start.12 = (bf16[512,128]{1,0:T(8,128)(2,1)S(1)}, bf16[512,128]{1,0:T(8,128)(2,1)S(1)}, u32[]{:S(2)}, u32[]{:S(2)}) collective-permute-start(bf16[512,128]{1,0:T(8,128)(2,1)S(1)} %collective-permute-done.10.other), channel_id=1, source_target_pairs={{0,1},{1,0},{2,3},{3,2},{4,5},{5,4},{6,7},{7,6},{8,9},{9,8},{10,11... | collective-permute-start | bytes 393224 | tf_op jit(solution)/shard_map/ppermute | solution.py:32
  43.2 0.0 collective-permute-done.13.refs_0_
  43.2 0.1 collective-permute-start.14
  43.2 0.0 collective-permute-done.15.refs_1_
  43.2 0.4 collective-permute-start.16
  43.7 0.8 %shard_map.112.refs_6_ = f32[1024,256]{1,0:T(8,128)S(1)} custom-call(bf16[512,128]{1,0:T(8,128)(2,1)S(1)} %collective-permute-done.13.refs_0_, bf16[512,128]{1,0:T(8,128)(2,1)S(1)} %collective-permute-done.15.refs_1_, bf16[1024,4096]{1,0:T(8,128)(2,1)S(1)} %get-tuple-element.26.chosen.refs_2_.refs_7_, ...), custom_call_target="tpu_custom_call" | custom-call | flops 1150000 | tf_op jit(solution)/shard_map/pallas_call | solution.py:665
  44.5 0.0 collective-permute-done.11.refs_0_
  44.5 0.0 collective-permute-done.12.refs_1_
  44.5 0.2 collective-permute-done.16.refs_3_
  44.7 4.3 %shard_map.113 = (f32[256,128]{1,0:T(8,128)}, f32[4,16384]{1,0:T(4,128)}) custom-call(bf16[512,128]{1,0:T(8,128)(2,1)S(1)} %collective-permute-done.11.refs_0_, bf16[512,128]{1,0:T(8,128)(2,1)S(1)} %collective-permute-done.12.refs_1_, bf16[512,128]{1,0:T(8,128)(2,1)S(1)} %collective-permute-done.14.refs_2_, ...), custom_call_target="tpu_custom_call" | custom-call | flops 1150000 | tf_op jit(solution)/shard_map/pallas_call | solution.py:665
  (18 shorter events, 0.1 us)
Async XLA Ops:
  0.6 6.4 %collective-permute-start = (bf16[256,128]{1,0:T(8,128)(2,1)}, bf16[256,128]{1,0:T(8,128)(2,1)S(1)}, u32[]{:S(2)}, u32[]{:S(2)}) collective-permute-start(bf16[256,128]{1,0:T(8,128)(2,1)} %bitcast.10), channel_id=1, source_target_pairs={{0,6},{1,7},{2,4},{3,5},{4,2},{5,3},{6,0},{7,1},{8,14},{9,15},{10,... | collective-permute-start | bytes 196616 | tf_op jit(solution)/shard_map/ppermute | solution.py:32
  4.6 4.5 %collective-permute-start.1 = (bf16[256,128]{1,0:T(8,128)(2,1)}, bf16[256,128]{1,0:T(8,128)(2,1)S(1)}, u32[]{:S(2)}, u32[]{:S(2)}) collective-permute-start(bf16[256,128]{1,0:T(8,128)(2,1)} %bitcast.11), channel_id=1, source_target_pairs={{0,4},{1,5},{2,6},{3,7},{4,0},{5,1},{6,2},{7,3},{8,12},{9,13},{10,... | collective-permute-start | bytes 196616 | tf_op jit(solution)/shard_map/ppermute | solution.py:32
  5.1 4.5 %collective-permute-start.2 = (bf16[256,128]{1,0:T(8,128)(2,1)}, bf16[256,128]{1,0:T(8,128)(2,1)S(1)}, u32[]{:S(2)}, u32[]{:S(2)}) collective-permute-start(bf16[256,128]{1,0:T(8,128)(2,1)} %bitcast.12), channel_id=1, source_target_pairs={{0,2},{1,3},{2,0},{3,1},{4,6},{5,7},{6,4},{7,5},{8,10},{9,11},{10,... | collective-permute-start | bytes 196616 | tf_op jit(solution)/shard_map/ppermute | solution.py:32
  6.1 3.5 %copy-start.3 = (bf16[2,16384]{1,0:T(2,128)(2,1)S(1)}, bf16[2,16384]{1,0:T(2,128)(2,1)}, u32[]{:S(2)}) copy-start(bf16[2,16384]{1,0:T(2,128)(2,1)} %param.9) | copy-start | bytes 196612
  6.1 5.1 %copy-start = (bf16[16,16384]{1,0:T(8,128)(2,1)S(1)}, bf16[16,16384]{1,0:T(8,128)(2,1)}, u32[]{:S(2)}) copy-start(bf16[16,16384]{1,0:T(8,128)(2,1)} %references.1) | copy-start | bytes 1572868
  6.1 5.1 %copy-start.2 = (bf16[192,512]{1,0:T(8,128)(2,1)S(1)}, bf16[192,512]{1,0:T(8,128)(2,1)}, u32[]{:S(2)}) copy-start(bf16[192,512]{1,0:T(8,128)(2,1)} %constant.12.clone.pick) | copy-start | bytes 589828
  6.1 5.1 %copy-start.4 = (s32[512]{0:T(512)S(1)}, s32[512]{0:T(512)}, u32[]{:S(2)}) copy-start(s32[512]{0:T(512)} %param.13) | copy-start | bytes 6148
  6.1 5.1 %copy-start.5 = (s32[512,1]{0,1:T(1,128)S(1)}, s32[512,1]{0,1:T(1,128)}, u32[]{:S(2)}) copy-start(s32[512,1]{0,1:T(1,128)} %param.12) | copy-start | bytes 6148
  6.1 19.3 %copy-start.6 = (f32[128,128]{1,0:T(8,128)S(1)}, f32[128,128]{1,0:T(8,128)}, u32[]{:S(2)}) copy-start(f32[128,128]{1,0:T(8,128)} %refs_4_.1) | copy-start | bytes 196612
  6.1 19.3 %copy-start.7 = (f32[256]{0:T(256)S(1)}, f32[256]{0:T(256)}, u32[]{:S(2)}) copy-start(f32[256]{0:T(256)} %param.15) | copy-start | bytes 3076
  9.6 1.6 %collective-permute-start.3 = (bf16[4,256,128]{2,1,0:T(8,128)(2,1)S(1)}, bf16[4,256,128]{2,1,0:T(8,128)(2,1)S(1)}, u32[]{:S(2)}, u32[]{:S(2)}) collective-permute-start(bf16[4,256,128]{2,1,0:T(8,128)(2,1)S(1)} %shard_map.105.near), channel_id=1, source_target_pairs={{0,1},{1,0},{2,3},{3,2},{4,5},{5,4},{6,7},{7,6},{8,9},{9,8},{10,11... | collective-permute-start | bytes 786440 | tf_op jit(solution)/shard_map/ppermute | solution.py:32
  15.1 9.3 %collective-permute-start.4 = (bf16[256,128]{1,0:T(8,128)(2,1)S(1)}, bf16[256,128]{1,0:T(8,128)(2,1)S(1)}, u32[]{:S(2)}, u32[]{:S(2)}) collective-permute-start(bf16[256,128]{1,0:T(8,128)(2,1)S(1)} %get-tuple-element.20.refs_0_), channel_id=1, source_target_pairs={{0,8},{8,0},{16,24},{24,16},{1,9},{9,1},{17,25},{25,17},{2,10},{10... | collective-permute-start | bytes 196616 | tf_op jit(solution)/shard_map/ppermute | solution.py:32
  16.6 7.8 %collective-permute-start.5 = (bf16[256,128]{1,0:T(8,128)(2,1)S(1)}, bf16[256,128]{1,0:T(8,128)(2,1)S(1)}, u32[]{:S(2)}, u32[]{:S(2)}) collective-permute-start(bf16[256,128]{1,0:T(8,128)(2,1)S(1)} %get-tuple-element.20.refs_0_), channel_id=1, source_target_pairs={{0,16},{8,24},{16,0},{24,8},{1,17},{9,25},{17,1},{25,9},{2,18},{10... | collective-permute-start | bytes 196616 | tf_op jit(solution)/shard_map/ppermute | solution.py:32
  19.2 6.2 %collective-permute-start.6 = (bf16[256,128]{1,0:T(8,128)(2,1)S(1)}, bf16[256,128]{1,0:T(8,128)(2,1)S(1)}, u32[]{:S(2)}, u32[]{:S(2)}) collective-permute-start(bf16[256,128]{1,0:T(8,128)(2,1)S(1)} %get-tuple-element.20.refs_0_), channel_id=1, source_target_pairs={{0,24},{8,16},{16,8},{24,0},{1,25},{9,17},{17,9},{25,1},{2,26},{10... | collective-permute-start | bytes 196616 | tf_op jit(solution)/shard_map/ppermute | solution.py:32
  19.5 13.2 %all-to-all-start = ((bf16[32,16,128]{2,1,0:T(8,128)(2,1)}), bf16[32,16,128]{2,1,0:T(8,128)(2,1)S(1)}, u32[]{:S(2)}, u32[]{:S(2)}) async-start(bf16[32,16,128]{2,1,0:T(8,128)(2,1)} %get-tuple-element.19), calls=%async_computation | async-start | bytes 262144 | tf_op jit(solution)/shard_map/all_to_all | solution.py:729
  25.4 7.2 %copy-start.1 = (bf16[384,512]{1,0:T(8,128)(2,1)S(1)}, bf16[384,512]{1,0:T(8,128)(2,1)}, u32[]{:S(2)}) copy-start(bf16[384,512]{1,0:T(8,128)(2,1)} %constant.13.clone.refs_3_) | copy-start | bytes 1179652
  25.4 5.1 %collective-permute-start.7 = (bf16[144,128]{1,0:T(8,128)(2,1)S(1)}, bf16[144,128]{1,0:T(8,128)(2,1)S(1)}, u32[]{:S(2)}, u32[]{:S(2)}) collective-permute-start(bf16[144,128]{1,0:T(8,128)(2,1)S(1)} %get-tuple-element.23.refs_3_), channel_id=1, source_target_pairs={{0,6},{1,7},{2,4},{3,5},{4,2},{5,3},{6,0},{7,1},{8,14},{9,15},{10,... | collective-permute-start | bytes 110600 | tf_op jit(solution)/shard_map/ppermute | solution.py:32
  27.2 4.1 %collective-permute-start.8 = (bf16[144,128]{1,0:T(8,128)(2,1)S(1)}, bf16[144,128]{1,0:T(8,128)(2,1)S(1)}, u32[]{:S(2)}, u32[]{:S(2)}) collective-permute-start(bf16[144,128]{1,0:T(8,128)(2,1)S(1)} %get-tuple-element.23.refs_3_), channel_id=1, source_target_pairs={{0,4},{1,5},{2,6},{3,7},{4,0},{5,1},{6,2},{7,3},{8,12},{9,13},{10,... | collective-permute-start | bytes 110600 | tf_op jit(solution)/shard_map/ppermute | solution.py:32
  27.8 4.0 %collective-permute-start.9 = (bf16[144,128]{1,0:T(8,128)(2,1)S(1)}, bf16[144,128]{1,0:T(8,128)(2,1)S(1)}, u32[]{:S(2)}, u32[]{:S(2)}) collective-permute-start(bf16[144,128]{1,0:T(8,128)(2,1)S(1)} %get-tuple-element.23.refs_3_), channel_id=1, source_target_pairs={{0,2},{1,3},{2,0},{3,1},{4,6},{5,7},{6,4},{7,5},{8,10},{9,11},{10,... | collective-permute-start | bytes 110600 | tf_op jit(solution)/shard_map/ppermute | solution.py:32
  34.3 7.3 %collective-permute-start.10 = (bf16[512,128]{1,0:T(8,128)(2,1)S(1)}, bf16[512,128]{1,0:T(8,128)(2,1)S(1)}, u32[]{:S(2)}, u32[]{:S(2)}) collective-permute-start(bf16[512,128]{1,0:T(8,128)(2,1)S(1)} %get-tuple-element.24.own), channel_id=1, source_target_pairs={{0,6},{1,7},{2,4},{3,5},{4,2},{5,3},{6,0},{7,1},{8,14},{9,15},{10,... | collective-permute-start | bytes 393224 | tf_op jit(solution)/shard_map/ppermute | solution.py:32
  35.7 7.5 %collective-permute-start.13 = (bf16[512,128]{1,0:T(8,128)(2,1)S(1)}, bf16[512,128]{1,0:T(8,128)(2,1)S(1)}, u32[]{:S(2)}, u32[]{:S(2)}) collective-permute-start(bf16[512,128]{1,0:T(8,128)(2,1)S(1)} %get-tuple-element.24.own), channel_id=1, source_target_pairs={{0,4},{1,5},{2,6},{3,7},{4,0},{5,1},{6,2},{7,3},{8,12},{9,13},{10,... | collective-permute-start | bytes 393224 | tf_op jit(solution)/shard_map/ppermute | solution.py:32
  36.3 7.0 %collective-permute-start.15 = (bf16[512,128]{1,0:T(8,128)(2,1)S(1)}, bf16[512,128]{1,0:T(8,128)(2,1)S(1)}, u32[]{:S(2)}, u32[]{:S(2)}) collective-permute-start(bf16[512,128]{1,0:T(8,128)(2,1)S(1)} %get-tuple-element.24.own), channel_id=1, source_target_pairs={{0,2},{1,3},{2,0},{3,1},{4,6},{5,7},{6,4},{7,5},{8,10},{9,11},{10,... | collective-permute-start | bytes 393224 | tf_op jit(solution)/shard_map/ppermute | solution.py:32
  37.9 6.6 %collective-permute-start.17 = (bf16[4,144,128]{2,1,0:T(8,128)(2,1)S(1)}, bf16[4,144,128]{2,1,0:T(8,128)(2,1)S(1)}, u32[]{:S(2)}, u32[]{:S(2)}) collective-permute-start(bf16[4,144,128]{2,1,0:T(8,128)(2,1)S(1)} %shard_map.108.refs_4_), channel_id=1, source_target_pairs={{0,1},{1,0},{2,3},{3,2},{4,5},{5,4},{6,7},{7,6},{8,9},{9,8},{10,11... | collective-permute-start | bytes 442376 | tf_op jit(solution)/shard_map/ppermute | solution.py:32
  42.6 1.9 %collective-permute-start.11 = (bf16[512,128]{1,0:T(8,128)(2,1)S(1)}, bf16[512,128]{1,0:T(8,128)(2,1)S(1)}, u32[]{:S(2)}, u32[]{:S(2)}) collective-permute-start(bf16[512,128]{1,0:T(8,128)(2,1)S(1)} %get-tuple-element.29), channel_id=1, source_target_pairs={{0,1},{1,0},{2,3},{3,2},{4,5},{5,4},{6,7},{7,6},{8,9},{9,8},{10,11... | collective-permute-start | bytes 393224 | tf_op jit(solution)/shard_map/ppermute | solution.py:32
  42.7 1.9 %collective-permute-start.12 = (bf16[512,128]{1,0:T(8,128)(2,1)S(1)}, bf16[512,128]{1,0:T(8,128)(2,1)S(1)}, u32[]{:S(2)}, u32[]{:S(2)}) collective-permute-start(bf16[512,128]{1,0:T(8,128)(2,1)S(1)} %collective-permute-done.10.other), channel_id=1, source_target_pairs={{0,1},{1,0},{2,3},{3,2},{4,5},{5,4},{6,7},{7,6},{8,9},{9,8},{10,11... | collective-permute-start | bytes 393224 | tf_op jit(solution)/shard_map/ppermute | solution.py:32
  43.2 1.4 %collective-permute-start.14 = (bf16[512,128]{1,0:T(8,128)(2,1)S(1)}, bf16[512,128]{1,0:T(8,128)(2,1)S(1)}, u32[]{:S(2)}, u32[]{:S(2)}) collective-permute-start(bf16[512,128]{1,0:T(8,128)(2,1)S(1)} %collective-permute-done.13.refs_0_), channel_id=1, source_target_pairs={{0,1},{1,0},{2,3},{3,2},{4,5},{5,4},{6,7},{7,6},{8,9},{9,8},{10,11... | collective-permute-start | bytes 393224 | tf_op jit(solution)/shard_map/ppermute | solution.py:32
  43.2 1.5 %collective-permute-start.16 = (bf16[512,128]{1,0:T(8,128)(2,1)S(1)}, bf16[512,128]{1,0:T(8,128)(2,1)S(1)}, u32[]{:S(2)}, u32[]{:S(2)}) collective-permute-start(bf16[512,128]{1,0:T(8,128)(2,1)S(1)} %collective-permute-done.15.refs_1_), channel_id=1, source_target_pairs={{0,1},{1,0},{2,3},{3,2},{4,5},{5,4},{6,7},{7,6},{8,9},{9,8},{10,11... | collective-permute-start | bytes 393224 | tf_op jit(solution)/shard_map/ppermute | solution.py:32

commit v7 on v6

--- a/solution.py
+++ b/solution.py
@@ -317,19 +317,19 @@
             rotated_re.append((real_part * c - imag_part * d).astype(bf16))
             rotated_im.append((real_part * d + imag_part * c).astype(bf16))
         total += lax.dot_general(
-            jnp.concatenate(rotated_re, axis=0), own[:, re_lanes], LANES, preferred_element_type=f32
+            own[:, re_lanes], jnp.concatenate(rotated_re, axis=0), LANES, preferred_element_type=f32
         )
         total += lax.dot_general(
-            jnp.concatenate(rotated_im, axis=0), own[:, im_lanes], LANES, preferred_element_type=f32
+            own[:, im_lanes], jnp.concatenate(rotated_im, axis=0), LANES, preferred_element_type=f32
         )
         turn(phases, now)
         return total
 
     columns = shift_count * references.shape[0]
     total = lax.fori_loop(
-        0, half_len // CHUNK, step, jnp.zeros((columns, group_rows), f32), unroll=True
-    )
-    scores = jnp.swapaxes(total, 0, 1) * (2.0 / math.sqrt(coef))
+        0, half_len // CHUNK, step, jnp.zeros((group_rows, columns), f32), unroll=True
+    )
+    scores = total * (2.0 / math.sqrt(coef))
     peak = jnp.max(scores, axis=1, keepdims=True)
     exponents = jnp.exp(scores - peak)
     total = jnp.sum(exponents, axis=1, keepdims=True)

time: 49.2 us -> 49.2 us (level)
  no operation moved by 1% of the time
where the time goes in v7:
time: 49.2 us; the launch traced here: 49 us
  starting transfers between devices  22.2 us (45%)
  Pallas kernels  15.5 us (32%)
  waiting for transfers between devices  9.59 us (19%)
  between operations  0.81 us (2%)
  local copies, waits for them, and re-layouts  0.8 us (2%)
    ppermute x18, starting transfers between devices, hop(): return lax.ppermute(value, axis, pairs)  17.3 us
    pallas_call x10, Pallas kernels, call(): pl.pallas_call(kernel, out_shape=[jax.ShapeDtypeStruct(shape, dtype) for...  15.5 us
    ppermute x18, waiting for transfers between devices, hop(): return lax.ppermute(value, axis, pairs)  8.81 us
    all_to_all x1, starting transfers between devices, whole_plane(): lax.all_to_all(message, ('img', 'ori'), split_axis=0, concat_axis=0, tile...  4.92 us
  transfers between devices with their start and end apart: 19, of which 10 were waited for; matrix products, arithmetic and copies ran while one was open for 2% of the time, Pallas kernels for 12%

profile of v7, /device:TPU:0, one launch (start us, length us, event | category | flops | bytes accessed | tf_op | source)
XLA Modules:
  0.0 49.0 jit_solution(16249136075797322707)
XLA Ops:
  0.6 4.0 %collective-permute-start = (bf16[256,128]{1,0:T(8,128)(2,1)}, bf16[256,128]{1,0:T(8,128)(2,1)S(1)}, u32[]{:S(2)}, u32[]{:S(2)}) collective-permute-start(bf16[256,128]{1,0:T(8,128)(2,1)} %bitcast.10), channel_id=1, source_target_pairs={{0,6},{1,7},{2,4},{3,5},{4,2},{5,3},{6,0},{7,1},{8,14},{9,15},{10,... | collective-permute-start | bytes 196616 | tf_op jit(solution)/shard_map/ppermute | solution.py:32
  4.6 0.5 %collective-permute-start.1 = (bf16[256,128]{1,0:T(8,128)(2,1)}, bf16[256,128]{1,0:T(8,128)(2,1)S(1)}, u32[]{:S(2)}, u32[]{:S(2)}) collective-permute-start(bf16[256,128]{1,0:T(8,128)(2,1)} %bitcast.11), channel_id=1, source_target_pairs={{0,4},{1,5},{2,6},{3,7},{4,0},{5,1},{6,2},{7,3},{8,12},{9,13},{10,... | collective-permute-start | bytes 196616 | tf_op jit(solution)/shard_map/ppermute | solution.py:32
  5.1 0.1 collective-permute-start.2
  5.2 0.8 %copy.12.shifts = f32[12,2]{1,0:T(8,128)S(1)} copy(f32[12,2]{0,1:T(2,128)} %param.11) | data formatting | bytes 192 | tf_op args[2]
  6.0 0.1 pad_add_fusion.place.refs_5_.refs_12_
  6.1 0.0 copy-start.5
  6.1 0.0 copy-start.6
  6.1 0.0 copy-start.7
  6.1 0.9 %shard_map.104 = (f32[2,2,16,256]{3,2,1,0:T(8,128)S(1)}, f32[2,16,1024]{2,1,0:T(8,128)S(1)}) custom-call(f32[12,2]{1,0:T(8,128)S(1)} %copy.12.shifts, s32[2]{0:T(128)S(1)} %pad_add_fusion.place.refs_5_.refs_12_), custom_call_target="tpu_custom_call" | custom-call | flops 13799999488 | tf_op jit(solution)/shard_map/pallas_call | solution.py:665
  7.1 0.0 collective-permute-done.refs_0_
  7.1 2.0 %collective-permute-done.1.refs_1_ = bf16[256,128]{1,0:T(8,128)(2,1)S(1)} collective-permute-done((bf16[256,128]{1,0:T(8,128)(2,1)}, bf16[256,128]{1,0:T(8,128)(2,1)S(1)}, u32[]{:S(2)}, u32[]{:S(2)}) %collective-permute-start.1) | collective-permute-done | bytes 65568 | tf_op jit(solution)/shard_map/ppermute | solution.py:32
  9.1 0.5 %collective-permute-done.2.refs_2_ = bf16[256,128]{1,0:T(8,128)(2,1)S(1)} collective-permute-done((bf16[256,128]{1,0:T(8,128)(2,1)}, bf16[256,128]{1,0:T(8,128)(2,1)S(1)}, u32[]{:S(2)}, u32[]{:S(2)}) %collective-permute-start.2) | collective-permute-done | bytes 65568 | tf_op jit(solution)/shard_map/ppermute | solution.py:32
  9.6 0.1 collective-permute-start.3
  9.7 1.5 %collective-permute-done.3.far = bf16[4,256,128]{2,1,0:T(8,128)(2,1)S(1)} collective-permute-done((bf16[4,256,128]{2,1,0:T(8,128)(2,1)S(1)}, bf16[4,256,128]{2,1,0:T(8,128)(2,1)S(1)}, u32[]{:S(2)}, u32[]{:S(2)}) %collective-permute-start.3) | collective-permute-done | bytes 262176 | tf_op jit(solution)/shard_map/ppermute | solution.py:32
  11.2 3.8 %shard_map.106 = (bf16[32,16,128]{2,1,0:T(8,128)(2,1)}, bf16[256,128]{1,0:T(8,128)(2,1)S(1)}) custom-call(bf16[4,256,128]{2,1,0:T(8,128)(2,1)S(1)} %shard_map.105.near, bf16[4,256,128]{2,1,0:T(8,128)(2,1)S(1)} %collective-permute-done.3.far, bf16[16,16384]{1,0:T(8,128)(2,1)S(1)} %copy-done, f32[2,2,16,256]{3,2,1,0:T(8,128)S(1)} %get-tuple-element.18.refs_4_.phases, ...), custom_call_target="tpu_custom_call" | custom-call | flops 1150000 | tf_op jit(solution)/shard_map/pallas_call | solution.py:665
  15.0 1.6 %collective-permute-start.4 = (bf16[256,128]{1,0:T(8,128)(2,1)S(1)}, bf16[256,128]{1,0:T(8,128)(2,1)S(1)}, u32[]{:S(2)}, u32[]{:S(2)}) collective-permute-start(bf16[256,128]{1,0:T(8,128)(2,1)S(1)} %get-tuple-element.20.refs_0_), channel_id=1, source_target_pairs={{0,8},{8,0},{16,24},{24,16},{1,9},{9,1},{17,25},{25,17},{2,10},{10... | collective-permute-start | bytes 196616 | tf_op jit(solution)/shard_map/ppermute | solution.py:32
  16.6 2.6 %collective-permute-start.5 = (bf16[256,128]{1,0:T(8,128)(2,1)S(1)}, bf16[256,128]{1,0:T(8,128)(2,1)S(1)}, u32[]{:S(2)}, u32[]{:S(2)}) collective-permute-start(bf16[256,128]{1,0:T(8,128)(2,1)S(1)} %get-tuple-element.20.refs_0_), channel_id=1, source_target_pairs={{0,16},{8,24},{16,0},{24,8},{1,17},{9,25},{17,1},{25,9},{2,18},{10... | collective-permute-start | bytes 196616 | tf_op jit(solution)/shard_map/ppermute | solution.py:32
  19.2 0.2 collective-permute-start.6
  19.4 4.9 %all-to-all-start = ((bf16[32,16,128]{2,1,0:T(8,128)(2,1)}), bf16[32,16,128]{2,1,0:T(8,128)(2,1)S(1)}, u32[]{:S(2)}, u32[]{:S(2)}) async-start(bf16[32,16,128]{2,1,0:T(8,128)(2,1)} %get-tuple-element.19), calls=%async_computation | async-start | bytes 262144 | tf_op jit(solution)/shard_map/all_to_all | solution.py:729
  24.3 0.0 collective-permute-done.4.refs_1_
  24.4 0.0 collective-permute-done.5.refs_2_
  24.4 1.0 %collective-permute-done.6.refs_3_ = bf16[256,128]{1,0:T(8,128)(2,1)S(1)} collective-permute-done((bf16[256,128]{1,0:T(8,128)(2,1)S(1)}, bf16[256,128]{1,0:T(8,128)(2,1)S(1)}, u32[]{:S(2)}, u32[]{:S(2)}) %collective-permute-start.6) | collective-permute-done | bytes 65568 | tf_op jit(solution)/shard_map/ppermute | solution.py:32
  25.4 1.8 %collective-permute-start.7 = (bf16[144,128]{1,0:T(8,128)(2,1)S(1)}, bf16[144,128]{1,0:T(8,128)(2,1)S(1)}, u32[]{:S(2)}, u32[]{:S(2)}) collective-permute-start(bf16[144,128]{1,0:T(8,128)(2,1)S(1)} %get-tuple-element.23.refs_3_), channel_id=1, source_target_pairs={{0,6},{1,7},{2,4},{3,5},{4,2},{5,3},{6,0},{7,1},{8,14},{9,15},{10,... | collective-permute-start | bytes 110600 | tf_op jit(solution)/shard_map/ppermute | solution.py:32
  27.2 0.6 %collective-permute-start.8 = (bf16[144,128]{1,0:T(8,128)(2,1)S(1)}, bf16[144,128]{1,0:T(8,128)(2,1)S(1)}, u32[]{:S(2)}, u32[]{:S(2)}) collective-permute-start(bf16[144,128]{1,0:T(8,128)(2,1)S(1)} %get-tuple-element.23.refs_3_), channel_id=1, source_target_pairs={{0,4},{1,5},{2,6},{3,7},{4,0},{5,1},{6,2},{7,3},{8,12},{9,13},{10,... | collective-permute-start | bytes 110600 | tf_op jit(solution)/shard_map/ppermute | solution.py:32
  27.7 1.2 %collective-permute-start.9 = (bf16[144,128]{1,0:T(8,128)(2,1)S(1)}, bf16[144,128]{1,0:T(8,128)(2,1)S(1)}, u32[]{:S(2)}, u32[]{:S(2)}) collective-permute-start(bf16[144,128]{1,0:T(8,128)(2,1)S(1)} %get-tuple-element.23.refs_3_), channel_id=1, source_target_pairs={{0,2},{1,3},{2,0},{3,1},{4,6},{5,7},{6,4},{7,5},{8,10},{9,11},{10,... | collective-permute-start | bytes 110600 | tf_op jit(solution)/shard_map/ppermute | solution.py:32
  29.0 1.6 %collective-permute-done.7.refs_0_ = bf16[144,128]{1,0:T(8,128)(2,1)S(1)} collective-permute-done((bf16[144,128]{1,0:T(8,128)(2,1)S(1)}, bf16[144,128]{1,0:T(8,128)(2,1)S(1)}, u32[]{:S(2)}, u32[]{:S(2)}) %collective-permute-start.7) | collective-permute-done | bytes 36896 | tf_op jit(solution)/shard_map/ppermute | solution.py:32
  30.5 0.7 %collective-permute-done.8.refs_1_ = bf16[144,128]{1,0:T(8,128)(2,1)S(1)} collective-permute-done((bf16[144,128]{1,0:T(8,128)(2,1)S(1)}, bf16[144,128]{1,0:T(8,128)(2,1)S(1)}, u32[]{:S(2)}, u32[]{:S(2)}) %collective-permute-start.8) | collective-permute-done | bytes 36896 | tf_op jit(solution)/shard_map/ppermute | solution.py:32
  31.3 0.5 %collective-permute-done.9.refs_2_ = bf16[144,128]{1,0:T(8,128)(2,1)S(1)} collective-permute-done((bf16[144,128]{1,0:T(8,128)(2,1)S(1)}, bf16[144,128]{1,0:T(8,128)(2,1)S(1)}, u32[]{:S(2)}, u32[]{:S(2)}) %collective-permute-start.9) | collective-permute-done | bytes 36896 | tf_op jit(solution)/shard_map/ppermute | solution.py:32
  31.8 0.8 %all-to-all-done.refs_0_.got = bf16[32,16,128]{2,1,0:T(8,128)(2,1)S(1)} async-done(((bf16[32,16,128]{2,1,0:T(8,128)(2,1)}), bf16[32,16,128]{2,1,0:T(8,128)(2,1)S(1)}, u32[]{:S(2)}, u32[]{:S(2)}) %all-to-all-start) | async-done | bytes 131104 | tf_op jit(solution)/shard_map/all_to_all | solution.py:729
  32.6 1.7 %shard_map.109 = (bf16[512,128]{1,0:T(8,128)(2,1)S(1)}, f32[32,128]{1,0:T(8,128)S(1)}) custom-call(bf16[32,16,128]{2,1,0:T(8,128)(2,1)S(1)} %all-to-all-done.refs_0_.got, bf16[1024,128]{1,0:T(8,128)(2,1)S(1)} %get-tuple-element.21.refs_1_, f32[2,16,1024]{2,1,0:T(8,128)S(1)} %get-tuple-element.22.refs_2_, bf16[384,512]{1,0:T(8,128)(2,1)S(1)} %copy-done.1, ...), custom_call_target="tpu_custom_call" | custom-call | flops 1150000 | tf_op jit(solution)/shard_map/pallas_call | solution.py:665
  34.3 1.4 %collective-permute-start.10 = (bf16[512,128]{1,0:T(8,128)(2,1)S(1)}, bf16[512,128]{1,0:T(8,128)(2,1)S(1)}, u32[]{:S(2)}, u32[]{:S(2)}) collective-permute-start(bf16[512,128]{1,0:T(8,128)(2,1)S(1)} %get-tuple-element.24.own), channel_id=1, source_target_pairs={{0,6},{1,7},{2,4},{3,5},{4,2},{5,3},{6,0},{7,1},{8,14},{9,15},{10,... | collective-permute-start | bytes 393224 | tf_op jit(solution)/shard_map/ppermute | solution.py:32
  35.7 0.6 %collective-permute-start.13 = (bf16[512,128]{1,0:T(8,128)(2,1)S(1)}, bf16[512,128]{1,0:T(8,128)(2,1)S(1)}, u32[]{:S(2)}, u32[]{:S(2)}) collective-permute-start(bf16[512,128]{1,0:T(8,128)(2,1)S(1)} %get-tuple-element.24.own), channel_id=1, source_target_pairs={{0,4},{1,5},{2,6},{3,7},{4,0},{5,1},{6,2},{7,3},{8,12},{9,13},{10,... | collective-permute-start | bytes 393224 | tf_op jit(solution)/shard_map/ppermute | solution.py:32
  36.2 1.6 %collective-permute-start.15 = (bf16[512,128]{1,0:T(8,128)(2,1)S(1)}, bf16[512,128]{1,0:T(8,128)(2,1)S(1)}, u32[]{:S(2)}, u32[]{:S(2)}) collective-permute-start(bf16[512,128]{1,0:T(8,128)(2,1)S(1)} %get-tuple-element.24.own), channel_id=1, source_target_pairs={{0,2},{1,3},{2,0},{3,1},{4,6},{5,7},{6,4},{7,5},{8,10},{9,11},{10,... | collective-permute-start | bytes 393224 | tf_op jit(solution)/shard_map/ppermute | solution.py:32
  37.8 0.0 collective-permute-start.17
  37.8 3.0 %shard_map.110 = (bf16[1024,4096]{1,0:T(8,128)(2,1)S(1)}, bf16[4096,128]{1,0:T(8,128)(2,1)S(1)}, bf16[256,256]{1,0:T(8,128)(2,1)S(1)}, bf16[512,256]{1,0:T(8,128)(2,1)S(1)}, bf16[512,128]{1,0:T(8,128)(2,1)S(1)}) custom-call(bf16[32,16,128]{2,1,0:T(8,128)(2,1)S(1)} %all-to-all-done.refs_0_.got, f32[32,128]{1,0:T(8,128)S(1)} %get-tuple-element.25.after.masses, ...), custom_call_target="tpu_custom_call" | custom-call | flops 1150000 | tf_op jit(solution)/shard_map/pallas_call | solution.py:665
  40.8 0.8 %collective-permute-done.10.other = bf16[512,128]{1,0:T(8,128)(2,1)S(1)} collective-permute-done((bf16[512,128]{1,0:T(8,128)(2,1)S(1)}, bf16[512,128]{1,0:T(8,128)(2,1)S(1)}, u32[]{:S(2)}, u32[]{:S(2)}) %collective-permute-start.10) | collective-permute-done | bytes 131104 | tf_op jit(solution)/shard_map/ppermute | solution.py:32
  41.6 0.9 %shard_map.111 = (f32[1024,256]{1,0:T(8,128)S(1)}, f32[256,8]{1,0:T(8,128)S(1)}, bf16[512,128]{1,0:T(8,128)(2,1)S(1)}) custom-call(bf16[512,128]{1,0:T(8,128)(2,1)S(1)} %get-tuple-element.24.own, bf16[512,128]{1,0:T(8,128)(2,1)S(1)} %collective-permute-done.10.other, bf16[1024,4096]{1,0:T(8,128)(2,1)S(1)} %get-tuple-element.26.chosen.refs_2_.refs_7_, ...), custom_call_target="tpu_custom_call" | custom-call | flops 1150000 | tf_op jit(solution)/shard_map/pallas_call | solution.py:665
  42.5 0.1 collective-permute-start.11
  42.6 0.5 %collective-permute-start.12 = (bf16[512,128]{1,0:T(8,128)(2,1)S(1)}, bf16[512,128]{1,0:T(8,128)(2,1)S(1)}, u32[]{:S(2)}, u32[]{:S(2)}) collective-permute-start(bf16[512,128]{1,0:T(8,128)(2,1)S(1)} %collective-permute-done.10.other), channel_id=1, source_target_pairs={{0,1},{1,0},{2,3},{3,2},{4,5},{5,4},{6,7},{7,6},{8,9},{9,8},{10,11... | collective-permute-start | bytes 393224 | tf_op jit(solution)/shard_map/ppermute | solution.py:32
  43.1 0.0 collective-permute-done.13.refs_0_
  43.1 0.1 collective-permute-start.14
  43.2 0.0 collective-permute-done.15.refs_1_
  43.2 0.4 collective-permute-start.16
  43.6 0.8 %shard_map.112.refs_6_ = f32[1024,256]{1,0:T(8,128)S(1)} custom-call(bf16[512,128]{1,0:T(8,128)(2,1)S(1)} %collective-permute-done.13.refs_0_, bf16[512,128]{1,0:T(8,128)(2,1)S(1)} %collective-permute-done.15.refs_1_, bf16[1024,4096]{1,0:T(8,128)(2,1)S(1)} %get-tuple-element.26.chosen.refs_2_.refs_7_, ...), custom_call_target="tpu_custom_call" | custom-call | flops 1150000 | tf_op jit(solution)/shard_map/pallas_call | solution.py:665
  44.5 0.0 collective-permute-done.17.refs_5_
  44.5 0.0 collective-permute-done.14.refs_2_
  44.5 0.2 collective-permute-done.16.refs_3_
  44.7 4.3 %shard_map.113 = (f32[256,128]{1,0:T(8,128)}, f32[4,16384]{1,0:T(4,128)}) custom-call(bf16[512,128]{1,0:T(8,128)(2,1)S(1)} %collective-permute-done.11.refs_0_, bf16[512,128]{1,0:T(8,128)(2,1)S(1)} %collective-permute-done.12.refs_1_, bf16[512,128]{1,0:T(8,128)(2,1)S(1)} %collective-permute-done.14.refs_2_, ...), custom_call_target="tpu_custom_call" | custom-call | flops 1150000 | tf_op jit(solution)/shard_map/pallas_call | solution.py:665
  (18 shorter events, 0.1 us)
Async XLA Ops:
  0.6 6.4 %collective-permute-start = (bf16[256,128]{1,0:T(8,128)(2,1)}, bf16[256,128]{1,0:T(8,128)(2,1)S(1)}, u32[]{:S(2)}, u32[]{:S(2)}) collective-permute-start(bf16[256,128]{1,0:T(8,128)(2,1)} %bitcast.10), channel_id=1, source_target_pairs={{0,6},{1,7},{2,4},{3,5},{4,2},{5,3},{6,0},{7,1},{8,14},{9,15},{10,... | collective-permute-start | bytes 196616 | tf_op jit(solution)/shard_map/ppermute | solution.py:32
  4.6 4.5 %collective-permute-start.1 = (bf16[256,128]{1,0:T(8,128)(2,1)}, bf16[256,128]{1,0:T(8,128)(2,1)S(1)}, u32[]{:S(2)}, u32[]{:S(2)}) collective-permute-start(bf16[256,128]{1,0:T(8,128)(2,1)} %bitcast.11), channel_id=1, source_target_pairs={{0,4},{1,5},{2,6},{3,7},{4,0},{5,1},{6,2},{7,3},{8,12},{9,13},{10,... | collective-permute-start | bytes 196616 | tf_op jit(solution)/shard_map/ppermute | solution.py:32
  5.1 4.5 %collective-permute-start.2 = (bf16[256,128]{1,0:T(8,128)(2,1)}, bf16[256,128]{1,0:T(8,128)(2,1)S(1)}, u32[]{:S(2)}, u32[]{:S(2)}) collective-permute-start(bf16[256,128]{1,0:T(8,128)(2,1)} %bitcast.12), channel_id=1, source_target_pairs={{0,2},{1,3},{2,0},{3,1},{4,6},{5,7},{6,4},{7,5},{8,10},{9,11},{10,... | collective-permute-start | bytes 196616 | tf_op jit(solution)/shard_map/ppermute | solution.py:32
  6.1 3.5 %copy-start.3 = (bf16[2,16384]{1,0:T(2,128)(2,1)S(1)}, bf16[2,16384]{1,0:T(2,128)(2,1)}, u32[]{:S(2)}) copy-start(bf16[2,16384]{1,0:T(2,128)(2,1)} %param.9) | copy-start | bytes 196612
  6.1 5.1 %copy-start = (bf16[16,16384]{1,0:T(8,128)(2,1)S(1)}, bf16[16,16384]{1,0:T(8,128)(2,1)}, u32[]{:S(2)}) copy-start(bf16[16,16384]{1,0:T(8,128)(2,1)} %references.1) | copy-start | bytes 1572868
  6.1 5.1 %copy-start.2 = (bf16[192,512]{1,0:T(8,128)(2,1)S(1)}, bf16[192,512]{1,0:T(8,128)(2,1)}, u32[]{:S(2)}) copy-start(bf16[192,512]{1,0:T(8,128)(2,1)} %constant.12.clone.pick) | copy-start | bytes 589828
  6.1 5.1 %copy-start.4 = (s32[512]{0:T(512)S(1)}, s32[512]{0:T(512)}, u32[]{:S(2)}) copy-start(s32[512]{0:T(512)} %param.13) | copy-start | bytes 6148
  6.1 5.1 %copy-start.5 = (s32[512,1]{0,1:T(1,128)S(1)}, s32[512,1]{0,1:T(1,128)}, u32[]{:S(2)}) copy-start(s32[512,1]{0,1:T(1,128)} %param.12) | copy-start | bytes 6148
  6.1 19.3 %copy-start.6 = (f32[128,128]{1,0:T(8,128)S(1)}, f32[128,128]{1,0:T(8,128)}, u32[]{:S(2)}) copy-start(f32[128,128]{1,0:T(8,128)} %refs_4_.1) | copy-start | bytes 196612
  6.1 19.3 %copy-start.7 = (f32[256]{0:T(256)S(1)}, f32[256]{0:T(256)}, u32[]{:S(2)}) copy-start(f32[256]{0:T(256)} %param.15) | copy-start | bytes 3076
  9.6 1.6 %collective-permute-start.3 = (bf16[4,256,128]{2,1,0:T(8,128)(2,1)S(1)}, bf16[4,256,128]{2,1,0:T(8,128)(2,1)S(1)}, u32[]{:S(2)}, u32[]{:S(2)}) collective-permute-start(bf16[4,256,128]{2,1,0:T(8,128)(2,1)S(1)} %shard_map.105.near), channel_id=1, source_target_pairs={{0,1},{1,0},{2,3},{3,2},{4,5},{5,4},{6,7},{7,6},{8,9},{9,8},{10,11... | collective-permute-start | bytes 786440 | tf_op jit(solution)/shard_map/ppermute | solution.py:32
  15.0 9.3 %collective-permute-start.4 = (bf16[256,128]{1,0:T(8,128)(2,1)S(1)}, bf16[256,128]{1,0:T(8,128)(2,1)S(1)}, u32[]{:S(2)}, u32[]{:S(2)}) collective-permute-start(bf16[256,128]{1,0:T(8,128)(2,1)S(1)} %get-tuple-element.20.refs_0_), channel_id=1, source_target_pairs={{0,8},{8,0},{16,24},{24,16},{1,9},{9,1},{17,25},{25,17},{2,10},{10... | collective-permute-start | bytes 196616 | tf_op jit(solution)/shard_map/ppermute | solution.py:32
  16.6 7.8 %collective-permute-start.5 = (bf16[256,128]{1,0:T(8,128)(2,1)S(1)}, bf16[256,128]{1,0:T(8,128)(2,1)S(1)}, u32[]{:S(2)}, u32[]{:S(2)}) collective-permute-start(bf16[256,128]{1,0:T(8,128)(2,1)S(1)} %get-tuple-element.20.refs_0_), channel_id=1, source_target_pairs={{0,16},{8,24},{16,0},{24,8},{1,17},{9,25},{17,1},{25,9},{2,18},{10... | collective-permute-start | bytes 196616 | tf_op jit(solution)/shard_map/ppermute | solution.py:32
  19.2 6.2 %collective-permute-start.6 = (bf16[256,128]{1,0:T(8,128)(2,1)S(1)}, bf16[256,128]{1,0:T(8,128)(2,1)S(1)}, u32[]{:S(2)}, u32[]{:S(2)}) collective-permute-start(bf16[256,128]{1,0:T(8,128)(2,1)S(1)} %get-tuple-element.20.refs_0_), channel_id=1, source_target_pairs={{0,24},{8,16},{16,8},{24,0},{1,25},{9,17},{17,9},{25,1},{2,26},{10... | collective-permute-start | bytes 196616 | tf_op jit(solution)/shard_map/ppermute | solution.py:32
  19.4 13.2 %all-to-all-start = ((bf16[32,16,128]{2,1,0:T(8,128)(2,1)}), bf16[32,16,128]{2,1,0:T(8,128)(2,1)S(1)}, u32[]{:S(2)}, u32[]{:S(2)}) async-start(bf16[32,16,128]{2,1,0:T(8,128)(2,1)} %get-tuple-element.19), calls=%async_computation | async-start | bytes 262144 | tf_op jit(solution)/shard_map/all_to_all | solution.py:729
  25.4 7.2 %copy-start.1 = (bf16[384,512]{1,0:T(8,128)(2,1)S(1)}, bf16[384,512]{1,0:T(8,128)(2,1)}, u32[]{:S(2)}) copy-start(bf16[384,512]{1,0:T(8,128)(2,1)} %constant.13.clone.refs_3_) | copy-start | bytes 1179652
  25.4 5.1 %collective-permute-start.7 = (bf16[144,128]{1,0:T(8,128)(2,1)S(1)}, bf16[144,128]{1,0:T(8,128)(2,1)S(1)}, u32[]{:S(2)}, u32[]{:S(2)}) collective-permute-start(bf16[144,128]{1,0:T(8,128)(2,1)S(1)} %get-tuple-element.23.refs_3_), channel_id=1, source_target_pairs={{0,6},{1,7},{2,4},{3,5},{4,2},{5,3},{6,0},{7,1},{8,14},{9,15},{10,... | collective-permute-start | bytes 110600 | tf_op jit(solution)/shard_map/ppermute | solution.py:32
  27.2 4.1 %collective-permute-start.8 = (bf16[144,128]{1,0:T(8,128)(2,1)S(1)}, bf16[144,128]{1,0:T(8,128)(2,1)S(1)}, u32[]{:S(2)}, u32[]{:S(2)}) collective-permute-start(bf16[144,128]{1,0:T(8,128)(2,1)S(1)} %get-tuple-element.23.refs_3_), channel_id=1, source_target_pairs={{0,4},{1,5},{2,6},{3,7},{4,0},{5,1},{6,2},{7,3},{8,12},{9,13},{10,... | collective-permute-start | bytes 110600 | tf_op jit(solution)/shard_map/ppermute | solution.py:32
  27.7 4.0 %collective-permute-start.9 = (bf16[144,128]{1,0:T(8,128)(2,1)S(1)}, bf16[144,128]{1,0:T(8,128)(2,1)S(1)}, u32[]{:S(2)}, u32[]{:S(2)}) collective-permute-start(bf16[144,128]{1,0:T(8,128)(2,1)S(1)} %get-tuple-element.23.refs_3_), channel_id=1, source_target_pairs={{0,2},{1,3},{2,0},{3,1},{4,6},{5,7},{6,4},{7,5},{8,10},{9,11},{10,... | collective-permute-start | bytes 110600 | tf_op jit(solution)/shard_map/ppermute | solution.py:32
  34.3 7.3 %collective-permute-start.10 = (bf16[512,128]{1,0:T(8,128)(2,1)S(1)}, bf16[512,128]{1,0:T(8,128)(2,1)S(1)}, u32[]{:S(2)}, u32[]{:S(2)}) collective-permute-start(bf16[512,128]{1,0:T(8,128)(2,1)S(1)} %get-tuple-element.24.own), channel_id=1, source_target_pairs={{0,6},{1,7},{2,4},{3,5},{4,2},{5,3},{6,0},{7,1},{8,14},{9,15},{10,... | collective-permute-start | bytes 393224 | tf_op jit(solution)/shard_map/ppermute | solution.py:32
  35.7 7.5 %collective-permute-start.13 = (bf16[512,128]{1,0:T(8,128)(2,1)S(1)}, bf16[512,128]{1,0:T(8,128)(2,1)S(1)}, u32[]{:S(2)}, u32[]{:S(2)}) collective-permute-start(bf16[512,128]{1,0:T(8,128)(2,1)S(1)} %get-tuple-element.24.own), channel_id=1, source_target_pairs={{0,4},{1,5},{2,6},{3,7},{4,0},{5,1},{6,2},{7,3},{8,12},{9,13},{10,... | collective-permute-start | bytes 393224 | tf_op jit(solution)/shard_map/ppermute | solution.py:32
  36.2 7.0 %collective-permute-start.15 = (bf16[512,128]{1,0:T(8,128)(2,1)S(1)}, bf16[512,128]{1,0:T(8,128)(2,1)S(1)}, u32[]{:S(2)}, u32[]{:S(2)}) collective-permute-start(bf16[512,128]{1,0:T(8,128)(2,1)S(1)} %get-tuple-element.24.own), channel_id=1, source_target_pairs={{0,2},{1,3},{2,0},{3,1},{4,6},{5,7},{6,4},{7,5},{8,10},{9,11},{10,... | collective-permute-start | bytes 393224 | tf_op jit(solution)/shard_map/ppermute | solution.py:32
  37.8 6.6 %collective-permute-start.17 = (bf16[4,144,128]{2,1,0:T(8,128)(2,1)S(1)}, bf16[4,144,128]{2,1,0:T(8,128)(2,1)S(1)}, u32[]{:S(2)}, u32[]{:S(2)}) collective-permute-start(bf16[4,144,128]{2,1,0:T(8,128)(2,1)S(1)} %shard_map.108.refs_4_), channel_id=1, source_target_pairs={{0,1},{1,0},{2,3},{3,2},{4,5},{5,4},{6,7},{7,6},{8,9},{9,8},{10,11... | collective-permute-start | bytes 442376 | tf_op jit(solution)/shard_map/ppermute | solution.py:32
  42.5 1.9 %collective-permute-start.11 = (bf16[512,128]{1,0:T(8,128)(2,1)S(1)}, bf16[512,128]{1,0:T(8,128)(2,1)S(1)}, u32[]{:S(2)}, u32[]{:S(2)}) collective-permute-start(bf16[512,128]{1,0:T(8,128)(2,1)S(1)} %get-tuple-element.29), channel_id=1, source_target_pairs={{0,1},{1,0},{2,3},{3,2},{4,5},{5,4},{6,7},{7,6},{8,9},{9,8},{10,11... | collective-permute-start | bytes 393224 | tf_op jit(solution)/shard_map/ppermute | solution.py:32
  42.6 1.9 %collective-permute-start.12 = (bf16[512,128]{1,0:T(8,128)(2,1)S(1)}, bf16[512,128]{1,0:T(8,128)(2,1)S(1)}, u32[]{:S(2)}, u32[]{:S(2)}) collective-permute-start(bf16[512,128]{1,0:T(8,128)(2,1)S(1)} %collective-permute-done.10.other), channel_id=1, source_target_pairs={{0,1},{1,0},{2,3},{3,2},{4,5},{5,4},{6,7},{7,6},{8,9},{9,8},{10,11... | collective-permute-start | bytes 393224 | tf_op jit(solution)/shard_map/ppermute | solution.py:32
  43.1 1.4 %collective-permute-start.14 = (bf16[512,128]{1,0:T(8,128)(2,1)S(1)}, bf16[512,128]{1,0:T(8,128)(2,1)S(1)}, u32[]{:S(2)}, u32[]{:S(2)}) collective-permute-start(bf16[512,128]{1,0:T(8,128)(2,1)S(1)} %collective-permute-done.13.refs_0_), channel_id=1, source_target_pairs={{0,1},{1,0},{2,3},{3,2},{4,5},{5,4},{6,7},{7,6},{8,9},{9,8},{10,11... | collective-permute-start | bytes 393224 | tf_op jit(solution)/shard_map/ppermute | solution.py:32
  43.2 1.5 %collective-permute-start.16 = (bf16[512,128]{1,0:T(8,128)(2,1)S(1)}, bf16[512,128]{1,0:T(8,128)(2,1)S(1)}, u32[]{:S(2)}, u32[]{:S(2)}) collective-permute-start(bf16[512,128]{1,0:T(8,128)(2,1)S(1)} %collective-permute-done.15.refs_1_), channel_id=1, source_target_pairs={{0,1},{1,0},{2,3},{3,2},{4,5},{5,4},{6,7},{7,6},{8,9},{9,8},{10,11... | collective-permute-start | bytes 393224 | tf_op jit(solution)/shard_map/ppermute | solution.py:32

commit v8 on v7

--- a/solution.py
+++ b/solution.py
@@ -647,8 +647,8 @@
     ]
     taken = jnp.dot(own_slots[...], jnp.concatenate(back, axis=1), preferred_element_type=f32)
     owner = own_owner_lanes[...].astype(f32)
-    total = jnp.zeros((sub_rows * tiles, SEGLEN), f32)
-    for w in range(shares):
+    total = taken[:, :SEGLEN]
+    for w in range(1, shares):
         total = jnp.where(owner == float(w), taken[:, w * SEGLEN : (w + 1) * SEGLEN], total)
     result[...] = total
     for j in range(tiles):

time: 49.2 us -> 49.2 us (level)
  no operation moved by 1% of the time
where the time goes in v8:
time: 49.2 us; the launch traced here: 49 us
  starting transfers between devices  22.2 us (45%)
  Pallas kernels  15.5 us (32%)
  waiting for transfers between devices  9.59 us (19%)
  between operations  0.81 us (2%)
  local copies, waits for them, and re-layouts  0.8 us (2%)
    ppermute x18, starting transfers between devices, hop(): return lax.ppermute(value, axis, pairs)  17.3 us
    pallas_call x10, Pallas kernels, call(): pl.pallas_call(kernel, out_shape=[jax.ShapeDtypeStruct(shape, dtype) for...  15.5 us
    ppermute x18, waiting for transfers between devices, hop(): return lax.ppermute(value, axis, pairs)  8.81 us
    all_to_all x1, starting transfers between devices, whole_plane(): lax.all_to_all(message, ('img', 'ori'), split_axis=0, concat_axis=0, tile...  4.92 us
  transfers between devices with their start and end apart: 19, of which 10 were waited for; matrix products, arithmetic and copies ran while one was open for 2% of the time, Pallas kernels for 12%

profile of v8, /device:TPU:0, one launch (start us, length us, event | category | flops | bytes accessed | tf_op | source)
XLA Modules:
  0.0 49.0 jit_solution(17155658514256930594)
XLA Ops:
  0.6 4.0 %collective-permute-start = (bf16[256,128]{1,0:T(8,128)(2,1)}, bf16[256,128]{1,0:T(8,128)(2,1)S(1)}, u32[]{:S(2)}, u32[]{:S(2)}) collective-permute-start(bf16[256,128]{1,0:T(8,128)(2,1)} %bitcast.10), channel_id=1, source_target_pairs={{0,6},{1,7},{2,4},{3,5},{4,2},{5,3},{6,0},{7,1},{8,14},{9,15},{10,... | collective-permute-start | bytes 196616 | tf_op jit(solution)/shard_map/ppermute | solution.py:32
  4.6 0.5 %collective-permute-start.1 = (bf16[256,128]{1,0:T(8,128)(2,1)}, bf16[256,128]{1,0:T(8,128)(2,1)S(1)}, u32[]{:S(2)}, u32[]{:S(2)}) collective-permute-start(bf16[256,128]{1,0:T(8,128)(2,1)} %bitcast.11), channel_id=1, source_target_pairs={{0,4},{1,5},{2,6},{3,7},{4,0},{5,1},{6,2},{7,3},{8,12},{9,13},{10,... | collective-permute-start | bytes 196616 | tf_op jit(solution)/shard_map/ppermute | solution.py:32
  5.1 0.1 collective-permute-start.2
  5.2 0.8 %copy.12.shifts = f32[12,2]{1,0:T(8,128)S(1)} copy(f32[12,2]{0,1:T(2,128)} %param.11) | data formatting | bytes 192 | tf_op args[2]
  6.0 0.1 pad_add_fusion.place.refs_5_.refs_12_
  6.1 0.0 copy-start.5
  6.1 0.0 copy-start.6
  6.1 0.0 copy-start.7
  6.1 0.9 %shard_map.104 = (f32[2,2,16,256]{3,2,1,0:T(8,128)S(1)}, f32[2,16,1024]{2,1,0:T(8,128)S(1)}) custom-call(f32[12,2]{1,0:T(8,128)S(1)} %copy.12.shifts, s32[2]{0:T(128)S(1)} %pad_add_fusion.place.refs_5_.refs_12_), custom_call_target="tpu_custom_call" | custom-call | flops 13799999488 | tf_op jit(solution)/shard_map/pallas_call | solution.py:665
  7.1 0.0 collective-permute-done.refs_0_
  7.1 2.0 %collective-permute-done.1.refs_1_ = bf16[256,128]{1,0:T(8,128)(2,1)S(1)} collective-permute-done((bf16[256,128]{1,0:T(8,128)(2,1)}, bf16[256,128]{1,0:T(8,128)(2,1)S(1)}, u32[]{:S(2)}, u32[]{:S(2)}) %collective-permute-start.1) | collective-permute-done | bytes 65568 | tf_op jit(solution)/shard_map/ppermute | solution.py:32
  9.1 0.5 %collective-permute-done.2.refs_2_ = bf16[256,128]{1,0:T(8,128)(2,1)S(1)} collective-permute-done((bf16[256,128]{1,0:T(8,128)(2,1)}, bf16[256,128]{1,0:T(8,128)(2,1)S(1)}, u32[]{:S(2)}, u32[]{:S(2)}) %collective-permute-start.2) | collective-permute-done | bytes 65568 | tf_op jit(solution)/shard_map/ppermute | solution.py:32
  9.6 0.1 collective-permute-start.3
  9.7 1.5 %collective-permute-done.3.far = bf16[4,256,128]{2,1,0:T(8,128)(2,1)S(1)} collective-permute-done((bf16[4,256,128]{2,1,0:T(8,128)(2,1)S(1)}, bf16[4,256,128]{2,1,0:T(8,128)(2,1)S(1)}, u32[]{:S(2)}, u32[]{:S(2)}) %collective-permute-start.3) | collective-permute-done | bytes 262176 | tf_op jit(solution)/shard_map/ppermute | solution.py:32
  11.2 3.8 %shard_map.106 = (bf16[32,16,128]{2,1,0:T(8,128)(2,1)}, bf16[256,128]{1,0:T(8,128)(2,1)S(1)}) custom-call(bf16[4,256,128]{2,1,0:T(8,128)(2,1)S(1)} %shard_map.105.near, bf16[4,256,128]{2,1,0:T(8,128)(2,1)S(1)} %collective-permute-done.3.far, bf16[16,16384]{1,0:T(8,128)(2,1)S(1)} %copy-done, f32[2,2,16,256]{3,2,1,0:T(8,128)S(1)} %get-tuple-element.18.refs_4_.phases, ...), custom_call_target="tpu_custom_call" | custom-call | flops 1150000 | tf_op jit(solution)/shard_map/pallas_call | solution.py:665
  15.0 1.6 %collective-permute-start.4 = (bf16[256,128]{1,0:T(8,128)(2,1)S(1)}, bf16[256,128]{1,0:T(8,128)(2,1)S(1)}, u32[]{:S(2)}, u32[]{:S(2)}) collective-permute-start(bf16[256,128]{1,0:T(8,128)(2,1)S(1)} %get-tuple-element.20.refs_0_), channel_id=1, source_target_pairs={{0,8},{8,0},{16,24},{24,16},{1,9},{9,1},{17,25},{25,17},{2,10},{10... | collective-permute-start | bytes 196616 | tf_op jit(solution)/shard_map/ppermute | solution.py:32
  16.6 2.6 %collective-permute-start.5 = (bf16[256,128]{1,0:T(8,128)(2,1)S(1)}, bf16[256,128]{1,0:T(8,128)(2,1)S(1)}, u32[]{:S(2)}, u32[]{:S(2)}) collective-permute-start(bf16[256,128]{1,0:T(8,128)(2,1)S(1)} %get-tuple-element.20.refs_0_), channel_id=1, source_target_pairs={{0,16},{8,24},{16,0},{24,8},{1,17},{9,25},{17,1},{25,9},{2,18},{10... | collective-permute-start | bytes 196616 | tf_op jit(solution)/shard_map/ppermute | solution.py:32
  19.2 0.2 collective-permute-start.6
  19.4 4.9 %all-to-all-start = ((bf16[32,16,128]{2,1,0:T(8,128)(2,1)}), bf16[32,16,128]{2,1,0:T(8,128)(2,1)S(1)}, u32[]{:S(2)}, u32[]{:S(2)}) async-start(bf16[32,16,128]{2,1,0:T(8,128)(2,1)} %get-tuple-element.19), calls=%async_computation | async-start | bytes 262144 | tf_op jit(solution)/shard_map/all_to_all | solution.py:729
  24.3 0.0 collective-permute-done.4.refs_1_
  24.4 0.0 collective-permute-done.5.refs_2_
  24.4 1.0 %collective-permute-done.6.refs_3_ = bf16[256,128]{1,0:T(8,128)(2,1)S(1)} collective-permute-done((bf16[256,128]{1,0:T(8,128)(2,1)S(1)}, bf16[256,128]{1,0:T(8,128)(2,1)S(1)}, u32[]{:S(2)}, u32[]{:S(2)}) %collective-permute-start.6) | collective-permute-done | bytes 65568 | tf_op jit(solution)/shard_map/ppermute | solution.py:32
  25.4 1.8 %collective-permute-start.7 = (bf16[144,128]{1,0:T(8,128)(2,1)S(1)}, bf16[144,128]{1,0:T(8,128)(2,1)S(1)}, u32[]{:S(2)}, u32[]{:S(2)}) collective-permute-start(bf16[144,128]{1,0:T(8,128)(2,1)S(1)} %get-tuple-element.23.refs_3_), channel_id=1, source_target_pairs={{0,6},{1,7},{2,4},{3,5},{4,2},{5,3},{6,0},{7,1},{8,14},{9,15},{10,... | collective-permute-start | bytes 110600 | tf_op jit(solution)/shard_map/ppermute | solution.py:32
  27.2 0.6 %collective-permute-start.8 = (bf16[144,128]{1,0:T(8,128)(2,1)S(1)}, bf16[144,128]{1,0:T(8,128)(2,1)S(1)}, u32[]{:S(2)}, u32[]{:S(2)}) collective-permute-start(bf16[144,128]{1,0:T(8,128)(2,1)S(1)} %get-tuple-element.23.refs_3_), channel_id=1, source_target_pairs={{0,4},{1,5},{2,6},{3,7},{4,0},{5,1},{6,2},{7,3},{8,12},{9,13},{10,... | collective-permute-start | bytes 110600 | tf_op jit(solution)/shard_map/ppermute | solution.py:32
  27.7 1.2 %collective-permute-start.9 = (bf16[144,128]{1,0:T(8,128)(2,1)S(1)}, bf16[144,128]{1,0:T(8,128)(2,1)S(1)}, u32[]{:S(2)}, u32[]{:S(2)}) collective-permute-start(bf16[144,128]{1,0:T(8,128)(2,1)S(1)} %get-tuple-element.23.refs_3_), channel_id=1, source_target_pairs={{0,2},{1,3},{2,0},{3,1},{4,6},{5,7},{6,4},{7,5},{8,10},{9,11},{10,... | collective-permute-start | bytes 110600 | tf_op jit(solution)/shard_map/ppermute | solution.py:32
  29.0 1.6 %collective-permute-done.7.refs_0_ = bf16[144,128]{1,0:T(8,128)(2,1)S(1)} collective-permute-done((bf16[144,128]{1,0:T(8,128)(2,1)S(1)}, bf16[144,128]{1,0:T(8,128)(2,1)S(1)}, u32[]{:S(2)}, u32[]{:S(2)}) %collective-permute-start.7) | collective-permute-done | bytes 36896 | tf_op jit(solution)/shard_map/ppermute | solution.py:32
  30.5 0.7 %collective-permute-done.8.refs_1_ = bf16[144,128]{1,0:T(8,128)(2,1)S(1)} collective-permute-done((bf16[144,128]{1,0:T(8,128)(2,1)S(1)}, bf16[144,128]{1,0:T(8,128)(2,1)S(1)}, u32[]{:S(2)}, u32[]{:S(2)}) %collective-permute-start.8) | collective-permute-done | bytes 36896 | tf_op jit(solution)/shard_map/ppermute | solution.py:32
  31.3 0.5 %collective-permute-done.9.refs_2_ = bf16[144,128]{1,0:T(8,128)(2,1)S(1)} collective-permute-done((bf16[144,128]{1,0:T(8,128)(2,1)S(1)}, bf16[144,128]{1,0:T(8,128)(2,1)S(1)}, u32[]{:S(2)}, u32[]{:S(2)}) %collective-permute-start.9) | collective-permute-done | bytes 36896 | tf_op jit(solution)/shard_map/ppermute | solution.py:32
  31.8 0.8 %all-to-all-done.refs_0_.got = bf16[32,16,128]{2,1,0:T(8,128)(2,1)S(1)} async-done(((bf16[32,16,128]{2,1,0:T(8,128)(2,1)}), bf16[32,16,128]{2,1,0:T(8,128)(2,1)S(1)}, u32[]{:S(2)}, u32[]{:S(2)}) %all-to-all-start) | async-done | bytes 131104 | tf_op jit(solution)/shard_map/all_to_all | solution.py:729
  32.6 1.7 %shard_map.109 = (bf16[512,128]{1,0:T(8,128)(2,1)S(1)}, f32[32,128]{1,0:T(8,128)S(1)}) custom-call(bf16[32,16,128]{2,1,0:T(8,128)(2,1)S(1)} %all-to-all-done.refs_0_.got, bf16[1024,128]{1,0:T(8,128)(2,1)S(1)} %get-tuple-element.21.refs_1_, f32[2,16,1024]{2,1,0:T(8,128)S(1)} %get-tuple-element.22.refs_2_, bf16[384,512]{1,0:T(8,128)(2,1)S(1)} %copy-done.1, ...), custom_call_target="tpu_custom_call" | custom-call | flops 1150000 | tf_op jit(solution)/shard_map/pallas_call | solution.py:665
  34.3 1.4 %collective-permute-start.10 = (bf16[512,128]{1,0:T(8,128)(2,1)S(1)}, bf16[512,128]{1,0:T(8,128)(2,1)S(1)}, u32[]{:S(2)}, u32[]{:S(2)}) collective-permute-start(bf16[512,128]{1,0:T(8,128)(2,1)S(1)} %get-tuple-element.24.own), channel_id=1, source_target_pairs={{0,6},{1,7},{2,4},{3,5},{4,2},{5,3},{6,0},{7,1},{8,14},{9,15},{10,... | collective-permute-start | bytes 393224 | tf_op jit(solution)/shard_map/ppermute | solution.py:32
  35.7 0.6 %collective-permute-start.13 = (bf16[512,128]{1,0:T(8,128)(2,1)S(1)}, bf16[512,128]{1,0:T(8,128)(2,1)S(1)}, u32[]{:S(2)}, u32[]{:S(2)}) collective-permute-start(bf16[512,128]{1,0:T(8,128)(2,1)S(1)} %get-tuple-element.24.own), channel_id=1, source_target_pairs={{0,4},{1,5},{2,6},{3,7},{4,0},{5,1},{6,2},{7,3},{8,12},{9,13},{10,... | collective-permute-start | bytes 393224 | tf_op jit(solution)/shard_map/ppermute | solution.py:32
  36.2 1.6 %collective-permute-start.15 = (bf16[512,128]{1,0:T(8,128)(2,1)S(1)}, bf16[512,128]{1,0:T(8,128)(2,1)S(1)}, u32[]{:S(2)}, u32[]{:S(2)}) collective-permute-start(bf16[512,128]{1,0:T(8,128)(2,1)S(1)} %get-tuple-element.24.own), channel_id=1, source_target_pairs={{0,2},{1,3},{2,0},{3,1},{4,6},{5,7},{6,4},{7,5},{8,10},{9,11},{10,... | collective-permute-start | bytes 393224 | tf_op jit(solution)/shard_map/ppermute | solution.py:32
  37.8 0.0 collective-permute-start.17
  37.8 3.0 %shard_map.110 = (bf16[1024,4096]{1,0:T(8,128)(2,1)S(1)}, bf16[4096,128]{1,0:T(8,128)(2,1)S(1)}, bf16[256,256]{1,0:T(8,128)(2,1)S(1)}, bf16[512,256]{1,0:T(8,128)(2,1)S(1)}, bf16[512,128]{1,0:T(8,128)(2,1)S(1)}) custom-call(bf16[32,16,128]{2,1,0:T(8,128)(2,1)S(1)} %all-to-all-done.refs_0_.got, f32[32,128]{1,0:T(8,128)S(1)} %get-tuple-element.25.after.masses, ...), custom_call_target="tpu_custom_call" | custom-call | flops 1150000 | tf_op jit(solution)/shard_map/pallas_call | solution.py:665
  40.8 0.8 %collective-permute-done.10.other = bf16[512,128]{1,0:T(8,128)(2,1)S(1)} collective-permute-done((bf16[512,128]{1,0:T(8,128)(2,1)S(1)}, bf16[512,128]{1,0:T(8,128)(2,1)S(1)}, u32[]{:S(2)}, u32[]{:S(2)}) %collective-permute-start.10) | collective-permute-done | bytes 131104 | tf_op jit(solution)/shard_map/ppermute | solution.py:32
  41.6 0.9 %shard_map.111 = (f32[1024,256]{1,0:T(8,128)S(1)}, f32[256,8]{1,0:T(8,128)S(1)}, bf16[512,128]{1,0:T(8,128)(2,1)S(1)}) custom-call(bf16[512,128]{1,0:T(8,128)(2,1)S(1)} %get-tuple-element.24.own, bf16[512,128]{1,0:T(8,128)(2,1)S(1)} %collective-permute-done.10.other, bf16[1024,4096]{1,0:T(8,128)(2,1)S(1)} %get-tuple-element.26.chosen.refs_2_.refs_7_, ...), custom_call_target="tpu_custom_call" | custom-call | flops 1150000 | tf_op jit(solution)/shard_map/pallas_call | solution.py:665
  42.5 0.1 collective-permute-start.11
  42.6 0.5 %collective-permute-start.12 = (bf16[512,128]{1,0:T(8,128)(2,1)S(1)}, bf16[512,128]{1,0:T(8,128)(2,1)S(1)}, u32[]{:S(2)}, u32[]{:S(2)}) collective-permute-start(bf16[512,128]{1,0:T(8,128)(2,1)S(1)} %collective-permute-done.10.other), channel_id=1, source_target_pairs={{0,1},{1,0},{2,3},{3,2},{4,5},{5,4},{6,7},{7,6},{8,9},{9,8},{10,11... | collective-permute-start | bytes 393224 | tf_op jit(solution)/shard_map/ppermute | solution.py:32
  43.1 0.0 collective-permute-done.13.refs_0_
  43.1 0.1 collective-permute-start.14
  43.2 0.0 collective-permute-done.15.refs_1_
  43.2 0.4 collective-permute-start.16
  43.6 0.8 %shard_map.112.refs_6_ = f32[1024,256]{1,0:T(8,128)S(1)} custom-call(bf16[512,128]{1,0:T(8,128)(2,1)S(1)} %collective-permute-done.13.refs_0_, bf16[512,128]{1,0:T(8,128)(2,1)S(1)} %collective-permute-done.15.refs_1_, bf16[1024,4096]{1,0:T(8,128)(2,1)S(1)} %get-tuple-element.26.chosen.refs_2_.refs_7_, ...), custom_call_target="tpu_custom_call" | custom-call | flops 1150000 | tf_op jit(solution)/shard_map/pallas_call | solution.py:665
  44.5 0.0 collective-permute-done.17.refs_5_
  44.5 0.0 collective-permute-done.14.refs_2_
  44.5 0.2 collective-permute-done.16.refs_3_
  44.7 4.3 %shard_map.113 = (f32[256,128]{1,0:T(8,128)}, f32[4,16384]{1,0:T(4,128)}) custom-call(bf16[512,128]{1,0:T(8,128)(2,1)S(1)} %collective-permute-done.11.refs_0_, bf16[512,128]{1,0:T(8,128)(2,1)S(1)} %collective-permute-done.12.refs_1_, bf16[512,128]{1,0:T(8,128)(2,1)S(1)} %collective-permute-done.14.refs_2_, ...), custom_call_target="tpu_custom_call" | custom-call | flops 1150000 | tf_op jit(solution)/shard_map/pallas_call | solution.py:665
  (18 shorter events, 0.1 us)
Async XLA Ops:
  0.6 6.4 %collective-permute-start = (bf16[256,128]{1,0:T(8,128)(2,1)}, bf16[256,128]{1,0:T(8,128)(2,1)S(1)}, u32[]{:S(2)}, u32[]{:S(2)}) collective-permute-start(bf16[256,128]{1,0:T(8,128)(2,1)} %bitcast.10), channel_id=1, source_target_pairs={{0,6},{1,7},{2,4},{3,5},{4,2},{5,3},{6,0},{7,1},{8,14},{9,15},{10,... | collective-permute-start | bytes 196616 | tf_op jit(solution)/shard_map/ppermute | solution.py:32
  4.6 4.5 %collective-permute-start.1 = (bf16[256,128]{1,0:T(8,128)(2,1)}, bf16[256,128]{1,0:T(8,128)(2,1)S(1)}, u32[]{:S(2)}, u32[]{:S(2)}) collective-permute-start(bf16[256,128]{1,0:T(8,128)(2,1)} %bitcast.11), channel_id=1, source_target_pairs={{0,4},{1,5},{2,6},{3,7},{4,0},{5,1},{6,2},{7,3},{8,12},{9,13},{10,... | collective-permute-start | bytes 196616 | tf_op jit(solution)/shard_map/ppermute | solution.py:32
  5.1 4.5 %collective-permute-start.2 = (bf16[256,128]{1,0:T(8,128)(2,1)}, bf16[256,128]{1,0:T(8,128)(2,1)S(1)}, u32[]{:S(2)}, u32[]{:S(2)}) collective-permute-start(bf16[256,128]{1,0:T(8,128)(2,1)} %bitcast.12), channel_id=1, source_target_pairs={{0,2},{1,3},{2,0},{3,1},{4,6},{5,7},{6,4},{7,5},{8,10},{9,11},{10,... | collective-permute-start | bytes 196616 | tf_op jit(solution)/shard_map/ppermute | solution.py:32
  6.1 3.5 %copy-start.3 = (bf16[2,16384]{1,0:T(2,128)(2,1)S(1)}, bf16[2,16384]{1,0:T(2,128)(2,1)}, u32[]{:S(2)}) copy-start(bf16[2,16384]{1,0:T(2,128)(2,1)} %param.9) | copy-start | bytes 196612
  6.1 5.1 %copy-start = (bf16[16,16384]{1,0:T(8,128)(2,1)S(1)}, bf16[16,16384]{1,0:T(8,128)(2,1)}, u32[]{:S(2)}) copy-start(bf16[16,16384]{1,0:T(8,128)(2,1)} %references.1) | copy-start | bytes 1572868
  6.1 5.1 %copy-start.2 = (bf16[192,512]{1,0:T(8,128)(2,1)S(1)}, bf16[192,512]{1,0:T(8,128)(2,1)}, u32[]{:S(2)}) copy-start(bf16[192,512]{1,0:T(8,128)(2,1)} %constant.12.clone.pick) | copy-start | bytes 589828
  6.1 5.1 %copy-start.4 = (s32[512]{0:T(512)S(1)}, s32[512]{0:T(512)}, u32[]{:S(2)}) copy-start(s32[512]{0:T(512)} %param.13) | copy-start | bytes 6148
  6.1 5.1 %copy-start.5 = (s32[512,1]{0,1:T(1,128)S(1)}, s32[512,1]{0,1:T(1,128)}, u32[]{:S(2)}) copy-start(s32[512,1]{0,1:T(1,128)} %param.12) | copy-start | bytes 6148
  6.1 19.3 %copy-start.6 = (f32[128,128]{1,0:T(8,128)S(1)}, f32[128,128]{1,0:T(8,128)}, u32[]{:S(2)}) copy-start(f32[128,128]{1,0:T(8,128)} %refs_4_.1) | copy-start | bytes 196612
  6.1 19.3 %copy-start.7 = (f32[256]{0:T(256)S(1)}, f32[256]{0:T(256)}, u32[]{:S(2)}) copy-start(f32[256]{0:T(256)} %param.15) | copy-start | bytes 3076
  9.6 1.6 %collective-permute-start.3 = (bf16[4,256,128]{2,1,0:T(8,128)(2,1)S(1)}, bf16[4,256,128]{2,1,0:T(8,128)(2,1)S(1)}, u32[]{:S(2)}, u32[]{:S(2)}) collective-permute-start(bf16[4,256,128]{2,1,0:T(8,128)(2,1)S(1)} %shard_map.105.near), channel_id=1, source_target_pairs={{0,1},{1,0},{2,3},{3,2},{4,5},{5,4},{6,7},{7,6},{8,9},{9,8},{10,11... | collective-permute-start | bytes 786440 | tf_op jit(solution)/shard_map/ppermute | solution.py:32
  15.0 9.3 %collective-permute-start.4 = (bf16[256,128]{1,0:T(8,128)(2,1)S(1)}, bf16[256,128]{1,0:T(8,128)(2,1)S(1)}, u32[]{:S(2)}, u32[]{:S(2)}) collective-permute-start(bf16[256,128]{1,0:T(8,128)(2,1)S(1)} %get-tuple-element.20.refs_0_), channel_id=1, source_target_pairs={{0,8},{8,0},{16,24},{24,16},{1,9},{9,1},{17,25},{25,17},{2,10},{10... | collective-permute-start | bytes 196616 | tf_op jit(solution)/shard_map/ppermute | solution.py:32
  16.6 7.8 %collective-permute-start.5 = (bf16[256,128]{1,0:T(8,128)(2,1)S(1)}, bf16[256,128]{1,0:T(8,128)(2,1)S(1)}, u32[]{:S(2)}, u32[]{:S(2)}) collective-permute-start(bf16[256,128]{1,0:T(8,128)(2,1)S(1)} %get-tuple-element.20.refs_0_), channel_id=1, source_target_pairs={{0,16},{8,24},{16,0},{24,8},{1,17},{9,25},{17,1},{25,9},{2,18},{10... | collective-permute-start | bytes 196616 | tf_op jit(solution)/shard_map/ppermute | solution.py:32
  19.2 6.2 %collective-permute-start.6 = (bf16[256,128]{1,0:T(8,128)(2,1)S(1)}, bf16[256,128]{1,0:T(8,128)(2,1)S(1)}, u32[]{:S(2)}, u32[]{:S(2)}) collective-permute-start(bf16[256,128]{1,0:T(8,128)(2,1)S(1)} %get-tuple-element.20.refs_0_), channel_id=1, source_target_pairs={{0,24},{8,16},{16,8},{24,0},{1,25},{9,17},{17,9},{25,1},{2,26},{10... | collective-permute-start | bytes 196616 | tf_op jit(solution)/shard_map/ppermute | solution.py:32
  19.4 13.2 %all-to-all-start = ((bf16[32,16,128]{2,1,0:T(8,128)(2,1)}), bf16[32,16,128]{2,1,0:T(8,128)(2,1)S(1)}, u32[]{:S(2)}, u32[]{:S(2)}) async-start(bf16[32,16,128]{2,1,0:T(8,128)(2,1)} %get-tuple-element.19), calls=%async_computation | async-start | bytes 262144 | tf_op jit(solution)/shard_map/all_to_all | solution.py:729
  25.4 7.2 %copy-start.1 = (bf16[384,512]{1,0:T(8,128)(2,1)S(1)}, bf16[384,512]{1,0:T(8,128)(2,1)}, u32[]{:S(2)}) copy-start(bf16[384,512]{1,0:T(8,128)(2,1)} %constant.13.clone.refs_3_) | copy-start | bytes 1179652
  25.4 5.1 %collective-permute-start.7 = (bf16[144,128]{1,0:T(8,128)(2,1)S(1)}, bf16[144,128]{1,0:T(8,128)(2,1)S(1)}, u32[]{:S(2)}, u32[]{:S(2)}) collective-permute-start(bf16[144,128]{1,0:T(8,128)(2,1)S(1)} %get-tuple-element.23.refs_3_), channel_id=1, source_target_pairs={{0,6},{1,7},{2,4},{3,5},{4,2},{5,3},{6,0},{7,1},{8,14},{9,15},{10,... | collective-permute-start | bytes 110600 | tf_op jit(solution)/shard_map/ppermute | solution.py:32
  27.2 4.1 %collective-permute-start.8 = (bf16[144,128]{1,0:T(8,128)(2,1)S(1)}, bf16[144,128]{1,0:T(8,128)(2,1)S(1)}, u32[]{:S(2)}, u32[]{:S(2)}) collective-permute-start(bf16[144,128]{1,0:T(8,128)(2,1)S(1)} %get-tuple-element.23.refs_3_), channel_id=1, source_target_pairs={{0,4},{1,5},{2,6},{3,7},{4,0},{5,1},{6,2},{7,3},{8,12},{9,13},{10,... | collective-permute-start | bytes 110600 | tf_op jit(solution)/shard_map/ppermute | solution.py:32
  27.7 4.0 %collective-permute-start.9 = (bf16[144,128]{1,0:T(8,128)(2,1)S(1)}, bf16[144,128]{1,0:T(8,128)(2,1)S(1)}, u32[]{:S(2)}, u32[]{:S(2)}) collective-permute-start(bf16[144,128]{1,0:T(8,128)(2,1)S(1)} %get-tuple-element.23.refs_3_), channel_id=1, source_target_pairs={{0,2},{1,3},{2,0},{3,1},{4,6},{5,7},{6,4},{7,5},{8,10},{9,11},{10,... | collective-permute-start | bytes 110600 | tf_op jit(solution)/shard_map/ppermute | solution.py:32
  34.3 7.3 %collective-permute-start.10 = (bf16[512,128]{1,0:T(8,128)(2,1)S(1)}, bf16[512,128]{1,0:T(8,128)(2,1)S(1)}, u32[]{:S(2)}, u32[]{:S(2)}) collective-permute-start(bf16[512,128]{1,0:T(8,128)(2,1)S(1)} %get-tuple-element.24.own), channel_id=1, source_target_pairs={{0,6},{1,7},{2,4},{3,5},{4,2},{5,3},{6,0},{7,1},{8,14},{9,15},{10,... | collective-permute-start | bytes 393224 | tf_op jit(solution)/shard_map/ppermute | solution.py:32
  35.7 7.5 %collective-permute-start.13 = (bf16[512,128]{1,0:T(8,128)(2,1)S(1)}, bf16[512,128]{1,0:T(8,128)(2,1)S(1)}, u32[]{:S(2)}, u32[]{:S(2)}) collective-permute-start(bf16[512,128]{1,0:T(8,128)(2,1)S(1)} %get-tuple-element.24.own), channel_id=1, source_target_pairs={{0,4},{1,5},{2,6},{3,7},{4,0},{5,1},{6,2},{7,3},{8,12},{9,13},{10,... | collective-permute-start | bytes 393224 | tf_op jit(solution)/shard_map/ppermute | solution.py:32
  36.2 7.0 %collective-permute-start.15 = (bf16[512,128]{1,0:T(8,128)(2,1)S(1)}, bf16[512,128]{1,0:T(8,128)(2,1)S(1)}, u32[]{:S(2)}, u32[]{:S(2)}) collective-permute-start(bf16[512,128]{1,0:T(8,128)(2,1)S(1)} %get-tuple-element.24.own), channel_id=1, source_target_pairs={{0,2},{1,3},{2,0},{3,1},{4,6},{5,7},{6,4},{7,5},{8,10},{9,11},{10,... | collective-permute-start | bytes 393224 | tf_op jit(solution)/shard_map/ppermute | solution.py:32
  37.8 6.6 %collective-permute-start.17 = (bf16[4,144,128]{2,1,0:T(8,128)(2,1)S(1)}, bf16[4,144,128]{2,1,0:T(8,128)(2,1)S(1)}, u32[]{:S(2)}, u32[]{:S(2)}) collective-permute-start(bf16[4,144,128]{2,1,0:T(8,128)(2,1)S(1)} %shard_map.108.refs_4_), channel_id=1, source_target_pairs={{0,1},{1,0},{2,3},{3,2},{4,5},{5,4},{6,7},{7,6},{8,9},{9,8},{10,11... | collective-permute-start | bytes 442376 | tf_op jit(solution)/shard_map/ppermute | solution.py:32
  42.5 1.9 %collective-permute-start.11 = (bf16[512,128]{1,0:T(8,128)(2,1)S(1)}, bf16[512,128]{1,0:T(8,128)(2,1)S(1)}, u32[]{:S(2)}, u32[]{:S(2)}) collective-permute-start(bf16[512,128]{1,0:T(8,128)(2,1)S(1)} %get-tuple-element.29), channel_id=1, source_target_pairs={{0,1},{1,0},{2,3},{3,2},{4,5},{5,4},{6,7},{7,6},{8,9},{9,8},{10,11... | collective-permute-start | bytes 393224 | tf_op jit(solution)/shard_map/ppermute | solution.py:32
  42.6 1.9 %collective-permute-start.12 = (bf16[512,128]{1,0:T(8,128)(2,1)S(1)}, bf16[512,128]{1,0:T(8,128)(2,1)S(1)}, u32[]{:S(2)}, u32[]{:S(2)}) collective-permute-start(bf16[512,128]{1,0:T(8,128)(2,1)S(1)} %collective-permute-done.10.other), channel_id=1, source_target_pairs={{0,1},{1,0},{2,3},{3,2},{4,5},{5,4},{6,7},{7,6},{8,9},{9,8},{10,11... | collective-permute-start | bytes 393224 | tf_op jit(solution)/shard_map/ppermute | solution.py:32
  43.1 1.4 %collective-permute-start.14 = (bf16[512,128]{1,0:T(8,128)(2,1)S(1)}, bf16[512,128]{1,0:T(8,128)(2,1)S(1)}, u32[]{:S(2)}, u32[]{:S(2)}) collective-permute-start(bf16[512,128]{1,0:T(8,128)(2,1)S(1)} %collective-permute-done.13.refs_0_), channel_id=1, source_target_pairs={{0,1},{1,0},{2,3},{3,2},{4,5},{5,4},{6,7},{7,6},{8,9},{9,8},{10,11... | collective-permute-start | bytes 393224 | tf_op jit(solution)/shard_map/ppermute | solution.py:32
  43.2 1.5 %collective-permute-start.16 = (bf16[512,128]{1,0:T(8,128)(2,1)S(1)}, bf16[512,128]{1,0:T(8,128)(2,1)S(1)}, u32[]{:S(2)}, u32[]{:S(2)}) collective-permute-start(bf16[512,128]{1,0:T(8,128)(2,1)S(1)} %collective-permute-done.15.refs_1_), channel_id=1, source_target_pairs={{0,1},{1,0},{2,3},{3,2},{4,5},{5,4},{6,7},{7,6},{8,9},{9,8},{10,11... | collective-permute-start | bytes 393224 | tf_op jit(solution)/shard_map/ppermute | solution.py:32
